TPU v7x, 32 devices: a whole 2x2x4 slice. The times are simulated.
32 devices in a mesh: dp: 32 (over z, y, x, core).
Axes of the slice: x: 2, y: 2, z: 4, core: 2. Of those that a mesh axis runs over, the one named last changes fastest.
Arguments:
- inputs: bfloat16 [64, 1024, 512], P('dp'), may hold values from -6 to 6
- valid_len: int32 [64], P('dp'), may hold values from 615 to 1024
- norm_first: bfloat16 [512], P('dp'), may hold values from 0.5 to 1.5
- w_qkv: bfloat16 [512, 1536], P('dp'), may hold values from -0.25 to 0.25
- w_out: bfloat16 [512, 512], P('dp'), may hold values from -1.5 to 1.5
- relative_bucket_table: bfloat16 [8, 16], replicated, may hold values from -4 to 4
- norm_second: bfloat16 [512], P('dp'), may hold values from 0.5 to 1.5
- w_up: bfloat16 [512, 2048], P('dp'), may hold values from -0.25 to 0.25
- w_down: bfloat16 [2048, 512], P('dp'), may hold values from -0.125 to 0.125
- output_gradient: bfloat16 [64, 1024, 512], P('dp'), may hold values from -6 to 6
Outputs:
- output: bfloat16 [64, 1024, 512], P('dp')
- grad_inputs: bfloat16 [64, 1024, 512], P('dp')
- grad_norm_first: float32 [512], P('dp')
- grad_w_qkv: float32 [512, 1536], P('dp')
- output_weight_gradient: float32 [512, 512], P('dp')
- grad_rel_table: float32 [8, 16], replicated
- grad_norm_second: float32 [512], P('dp')
- grad_w_up: float32 [512, 2048], P('dp')
- down_weight_gradient: float32 [2048, 512], P('dp')
All inputs are finite; a program needn't handle non-finite values.
Results may differ from a plain program's by a relative error of at most 0.013.
Values may be sent and summed in bfloat16 or wider, within the bound.
A program may use at most 256 MiB of HBM per device.

v0:
```python
import jax
import jax.numpy as jnp
import numpy as np
from jax import lax
from jax.sharding import PartitionSpec as P

epsilon = 1e-05
masked_score = -1e30
bucket_low = np.array([0, 1, 2, 3, 4, 5, 6, 7, 8, 12, 16, 32, 64, 128, 256, 512], np.int32)
bucket_high = np.array([1, 2, 3, 4, 5, 6, 7, 8, 12, 16, 32, 64, 128, 256, 512, 1 << 30], np.int32)


def layer_norm(values, scale_gain):
    centered = values - jnp.mean(values, axis=-1, keepdims=True)
    spread = jnp.mean(centered * centered, axis=-1, keepdims=True)
    return centered * lax.rsqrt(spread + epsilon) * scale_gain


def gelu_tanh(values):
    return jax.nn.gelu(values, approximate=True)


def bucket_mask(first_row, row_count, length):
    query_pos = first_row + jnp.arange(row_count, dtype=jnp.int32)
    key_pos = jnp.arange(length, dtype=jnp.int32)
    distance = query_pos[:, None] - key_pos[None, :]
    lower = jnp.asarray(bucket_low)[:, None, None]
    upper = jnp.asarray(bucket_high)[:, None, None]
    inner_activation = (distance[None] >= lower) & (distance[None] < upper)
    return (distance, key_pos, inner_activation)


def block_scores(block_queries, seq_keys, relative_position_bias, allowed, score_scale):
    raw_scores = (
        jnp.einsum("qhd,khd->hqk", block_queries, seq_keys, preferred_element_type=jnp.float32)
        * score_scale
    )
    return jnp.where(allowed[None], raw_scores + relative_position_bias, masked_score)


def attend_forward(query_rows, key_rows, value_rows, valid_len, relative_bucket_table):
    seq_count, length, head_count, head_dim = query_rows.shape
    row_count = min(512, length)
    score_scale = head_dim ** (-0.5)

    def one_block(state_carry, block_index):
        first_row = block_index * row_count
        distance, key_pos, inner_activation = bucket_mask(first_row, row_count, length)
        relative_position_bias = jnp.einsum(
            "jc,cma->jma",
            relative_bucket_table,
            inner_activation.astype(jnp.bfloat16),
            preferred_element_type=jnp.float32,
        )

        def one_sequence(carry_inner, seq_items):
            seq_queries, seq_keys, seq_values, valid_rows = seq_items
            block_queries = lax.dynamic_slice_in_dim(seq_queries, first_row, row_count, 0)
            allowed = (distance >= 0) & (key_pos < valid_rows)[None, :]
            scores = block_scores(
                block_queries, seq_keys, relative_position_bias, allowed, score_scale
            )
            row_max = jnp.max(scores, axis=-1, keepdims=True)
            weights = jnp.exp(scores - row_max)
            row_total = jnp.sum(weights, axis=-1, keepdims=True)
            probabilities = (weights / row_total).astype(jnp.bfloat16)
            attended = jnp.einsum(
                "hqk,khd->qhd", probabilities, seq_values, preferred_element_type=jnp.float32
            )
            return (carry_inner, (attended, (row_max + jnp.log(row_total))[..., 0]))

        unused, outputs = lax.scan(one_sequence, 0, (query_rows, key_rows, value_rows, valid_len))
        return (state_carry, outputs)

    unused, (attended, log_total) = lax.scan(
        one_block, 0, jnp.arange(length // row_count, dtype=jnp.int32)
    )
    attended = jnp.moveaxis(attended, 0, 1).reshape(seq_count, length, head_count * head_dim)
    log_total = jnp.moveaxis(log_total, 0, 2).reshape(seq_count, head_count, length)
    return (attended, log_total)


def attend_backward(
    query_rows, key_rows, value_rows, valid_len, relative_bucket_table, log_total, grad_rows
):
    seq_count, length, head_count, head_dim = query_rows.shape
    row_count = min(512, length)
    score_scale = head_dim ** (-0.5)

    def one_block(table_sum, block_index):
        first_row = block_index * row_count
        distance, key_pos, inner_activation = bucket_mask(first_row, row_count, length)
        bucket_index_rows = inner_activation.astype(jnp.bfloat16)
        relative_position_bias = jnp.einsum(
            "jc,cma->jma",
            relative_bucket_table,
            bucket_index_rows,
            preferred_element_type=jnp.float32,
        )

        def one_sequence(table_part, seq_items):
            seq_queries, seq_keys, seq_values, valid_rows, seq_total, seq_grads = seq_items
            block_queries = lax.dynamic_slice_in_dim(seq_queries, first_row, row_count, 0)
            block_grads = lax.dynamic_slice_in_dim(seq_grads, first_row, row_count, 0)
            block_total = lax.dynamic_slice_in_dim(seq_total, first_row, row_count, 1)
            allowed = (distance >= 0) & (key_pos < valid_rows)[None, :]
            scores = block_scores(
                block_queries, seq_keys, relative_position_bias, allowed, score_scale
            )
            probabilities = jnp.exp(scores - block_total[..., None])
            prob_grads = jnp.einsum(
                "qhd,khd->hqk", block_grads, seq_values, preferred_element_type=jnp.float32
            )
            row_dot = jnp.sum(probabilities * prob_grads, axis=-1, keepdims=True)
            score_gradients = (probabilities * (prob_grads - row_dot)).astype(jnp.bfloat16)
            query_grads = (
                jnp.einsum(
                    "hqk,khd->qhd", score_gradients, seq_keys, preferred_element_type=jnp.float32
                )
                * score_scale
            )
            key_grads = (
                jnp.einsum(
                    "hqk,qhd->khd",
                    score_gradients,
                    block_queries,
                    preferred_element_type=jnp.float32,
                )
                * score_scale
            )
            value_grads = jnp.einsum(
                "hqk,qhd->khd",
                probabilities.astype(jnp.bfloat16),
                block_grads,
                preferred_element_type=jnp.float32,
            )
            table_part = table_part + jnp.einsum(
                "pwg,cwg->pc",
                score_gradients,
                bucket_index_rows,
                preferred_element_type=jnp.float32,
            )
            return (table_part, (query_grads, key_grads, value_grads))

        table_sum, outputs = lax.scan(
            one_sequence,
            table_sum,
            (query_rows, key_rows, value_rows, valid_len, log_total, grad_rows),
        )
        return (table_sum, outputs)

    start_sum = jnp.zeros(relative_bucket_table.shape, jnp.float32)
    table_sum, (query_grads, key_grads, value_grads) = lax.scan(
        one_block, start_sum, jnp.arange(length // row_count, dtype=jnp.int32)
    )
    query_grads = jnp.moveaxis(query_grads, 0, 1).reshape(seq_count, length, head_count, head_dim)
    return (query_grads, jnp.sum(key_grads, axis=0), jnp.sum(value_grads, axis=0), table_sum)


def on_device(
    inputs,
    valid_len,
    norm_first,
    w_qkv,
    w_out,
    relative_bucket_table,
    norm_second,
    w_up,
    w_down,
    output_gradient,
):
    (
        gain_first,
        query_key_value_precise,
        output_weight_precise,
        gain_second,
        up_weight_precise,
        down_weight_precise,
    ) = (
        lax.all_gather(norm_first, "dp", axis=0, tiled=True),
        lax.all_gather(w_qkv, "dp", axis=0, tiled=True),
        lax.all_gather(w_out, "dp", axis=0, tiled=True),
        lax.all_gather(norm_second, "dp", axis=0, tiled=True),
        lax.all_gather(w_up, "dp", axis=0, tiled=True),
        lax.all_gather(w_down, "dp", axis=0, tiled=True),
    )
    seq_count, length, width = inputs.shape
    head_count = relative_bucket_table.shape[0]
    head_dim = width // head_count
    residual_stream = inputs.astype(jnp.float32)
    first_normalized, first_pull = jax.vjp(
        layer_norm, residual_stream, gain_first.astype(jnp.float32)
    )
    first_hidden_state = first_normalized.astype(jnp.bfloat16)
    projected_output = jnp.einsum(
        "apk,kq->apq",
        first_hidden_state,
        query_key_value_precise,
        preferred_element_type=jnp.float32,
    ).astype(jnp.bfloat16)
    projected_output = projected_output.reshape(seq_count, length, 3, head_count, head_dim)
    query_rows = projected_output[:, :, 0]
    key_rows = projected_output[:, :, 1]
    value_rows = projected_output[:, :, 2]
    attended, log_total = attend_forward(
        query_rows, key_rows, value_rows, valid_len, relative_bucket_table
    )
    attention_mixed = attended.astype(jnp.bfloat16)
    attention_result = residual_stream + jnp.einsum(
        "jmu,uf->jmf", attention_mixed, output_weight_precise, preferred_element_type=jnp.float32
    )
    second_normalized, second_pull = jax.vjp(
        layer_norm, attention_result, gain_second.astype(jnp.float32)
    )
    second_hidden_state = second_normalized.astype(jnp.bfloat16)
    preactivation_values = jnp.einsum(
        "qmj,ja->qma", second_hidden_state, up_weight_precise, preferred_element_type=jnp.float32
    )
    activated, act_pull = jax.vjp(gelu_tanh, preactivation_values)
    feedforward_hidden = activated.astype(jnp.bfloat16)
    result = attention_result + jnp.einsum(
        "hor,rt->hot", feedforward_hidden, down_weight_precise, preferred_element_type=jnp.float32
    )
    output = result.astype(jnp.bfloat16)
    query_key_value_backward, output_weight_backward, up_weight_backward, down_weight_backward = (
        lax.all_gather(w_qkv, "dp", axis=0, tiled=True),
        lax.all_gather(w_out, "dp", axis=0, tiled=True),
        lax.all_gather(w_up, "dp", axis=0, tiled=True),
        lax.all_gather(w_down, "dp", axis=0, tiled=True),
    )
    down_weight_gradient = jnp.einsum(
        "bvg,bvm->gm", feedforward_hidden, output_gradient, preferred_element_type=jnp.float32
    )
    hidden_gradient = jnp.einsum(
        "wtp,np->wtn", output_gradient, down_weight_backward, preferred_element_type=jnp.float32
    )
    preactivation_gradient = act_pull(hidden_gradient)[0].astype(jnp.bfloat16)
    grad_w_up = jnp.einsum(
        "viu,vih->uh",
        second_hidden_state,
        preactivation_gradient,
        preferred_element_type=jnp.float32,
    )
    grad_normed_second = jnp.einsum(
        "zgu,yu->zgy",
        preactivation_gradient,
        up_weight_backward,
        preferred_element_type=jnp.float32,
    )
    grad_after_part, grad_gain_second = second_pull(grad_normed_second)
    grad_after = output_gradient.astype(jnp.float32) + grad_after_part
    branch_gradient = grad_after.astype(jnp.bfloat16)
    output_weight_gradient = jnp.einsum(
        "avb,avi->bi", attention_mixed, branch_gradient, preferred_element_type=jnp.float32
    )
    grad_mixed = jnp.einsum(
        "qyg,zg->qyz", branch_gradient, output_weight_backward, preferred_element_type=jnp.float32
    ).astype(jnp.bfloat16)
    grad_mixed = grad_mixed.reshape(seq_count, length, head_count, head_dim)
    query_grads, key_grads, value_grads, table_sum = attend_backward(
        query_rows, key_rows, value_rows, valid_len, relative_bucket_table, log_total, grad_mixed
    )
    projected_gradient = (
        jnp.stack([query_grads, key_grads, value_grads], axis=2)
        .reshape(seq_count, length, 3 * width)
        .astype(jnp.bfloat16)
    )
    grad_w_qkv = jnp.einsum(
        "qwf,qwb->fb", first_hidden_state, projected_gradient, preferred_element_type=jnp.float32
    )
    grad_normed_first = jnp.einsum(
        "wmp,up->wmu",
        projected_gradient,
        query_key_value_backward,
        preferred_element_type=jnp.float32,
    )
    grad_input_part, grad_gain_first = first_pull(grad_normed_first)
    grad_inputs = (grad_after + grad_input_part).astype(jnp.bfloat16)
    owned = (
        lax.psum_scatter(grad_gain_first, "dp", scatter_dimension=0, tiled=True),
        lax.psum_scatter(grad_w_qkv, "dp", scatter_dimension=0, tiled=True),
        lax.psum_scatter(output_weight_gradient, "dp", scatter_dimension=0, tiled=True),
        lax.psum_scatter(grad_gain_second, "dp", scatter_dimension=0, tiled=True),
        lax.psum_scatter(grad_w_up, "dp", scatter_dimension=0, tiled=True),
        lax.psum_scatter(down_weight_gradient, "dp", scatter_dimension=0, tiled=True),
    )
    table_total = lax.psum(table_sum, "dp")
    return (
        output,
        grad_inputs,
        owned[0],
        owned[1],
        owned[2],
        table_total,
        owned[3],
        owned[4],
        owned[5],
    )


def solution(mesh):
    placed = (
        P("dp", None, None),
        P("dp"),
        P("dp"),
        P("dp", None),
        P("dp", None),
        P(),
        P("dp"),
        P("dp", None),
        P("dp", None),
        P("dp", None, None),
    )
    return jax.shard_map(
        on_device,
        mesh=mesh,
        in_specs=placed,
        out_specs=(
            P("dp", None, None),
            P("dp", None, None),
            P("dp"),
            P("dp", None),
            P("dp", None),
            P(),
            P("dp"),
            P("dp", None),
            P("dp", None),
        ),
        check_vma=False,
    )
```

profile of v0, /device:TPU:0, one launch (start us, length us, event | category | flops | bytes accessed | tf_op | source)
XLA Modules:
  0.0 1201.8 jit_solution(3419794259950692618)
XLA Ops:
  11.2 42.1 %all-reduce.5 = (bf16[512]{0:T(512)(128)(2,1)S(1)}, bf16[512]{0:T(512)(128)(2,1)S(1)}) all-reduce(bf16[512]{0:T(512)(128)(2,1)S(1)} %dynamic-update-slice, bf16[512]{0:T(512)(128)(2,1)S(1)} %dynamic-update-slice.1), channel_id=1, replica_groups=mesh['dp'=32] {'dp'}, use_global_device_ids=true, to_apply=%add | all-reduce | flops 1024 | bytes 4096
  53.9 44.8 %all_gather.24 = bf16[512,512]{1,0:T(8,128)(2,1)} all-gather(bf16[16,512]{1,0:T(8,128)(2,1)} %param.24), channel_id=1, replica_groups=mesh['dp'=32] {'dp'}, dimensions={0}, use_global_device_ids=true | all-gather | bytes 540672 | tf_op jit(solution)/shard_map/all_gather | solution.py:182
  131.0 173.5 %while.106 = (s32[]{:T(128)}, bf16[2,2,512,8,64]{2,4,3,1,0:T(8,128)(2,1)}, f32[2,2,8,512]{3,2,1,0:T(8,128)}, s32[2]{0:T(128)}, bf16[8,16]{1,0:T(8,128)(2,1)S(1)}...) while((s32[]{:T(128)}, ...), condition=%wide.region_7.8_spmd.clone, body=%wide.region_2.7_spmd.sunk.clone.sunk | while | flops 1272968704 | bytes 204680784 | solution.py:75
  141.8 18.8 %copy.97 = f32[8,512,1024]{2,1,0:T(8,128)} copy(f32[8,512,1024]{2,0,1:T(8,128)S(1)} %fusion.157) | data formatting | bytes 33554432 | tf_op jit(solution)/shard_map/while
  160.6 56.4 %while.109 = (s32[]{:T(128)}, bf16[2,512,8,64]{1,3,2,0:T(8,128)(2,1)S(1)}, f32[2,8,512]{2,1,0:T(8,128)S(1)}, bf16[2,1024,8,64]{1,3,2,0:T(8,128)(2,1)}, s32[2]{0:...) while((s32[]{:T(128)}, ...), condition=%wide.region_6.6_spmd.clone, body=%wide.region_3.5_spmd.clone.sunk | while | flops 1113060352 | bytes 147461872 | solution.py:72
  162.3 11.9 fusion.176
  190.6 11.9 fusion.176
  228.4 18.8 %copy.97 = f32[8,512,1024]{2,1,0:T(8,128)} copy(f32[8,512,1024]{2,0,1:T(8,128)S(1)} %fusion.157) | data formatting | bytes 33554432 | tf_op jit(solution)/shard_map/while
  247.2 56.1 %while.109 = (s32[]{:T(128)}, bf16[2,512,8,64]{1,3,2,0:T(8,128)(2,1)S(1)}, f32[2,8,512]{2,1,0:T(8,128)S(1)}, bf16[2,1024,8,64]{1,3,2,0:T(8,128)(2,1)}, s32[2]{0:...) while((s32[]{:T(128)}, ...), condition=%wide.region_6.6_spmd.clone, body=%wide.region_3.5_spmd.clone.sunk | while | flops 1113060352 | bytes 147461872 | solution.py:72
  248.9 11.8 fusion.176
  276.9 11.8 fusion.176
  321.2 13.3 %fusion.101 = f32[2,1024,2048]{2,1,0:T(8,128)} fusion(bf16[512,2048]{1,0:T(8,128)(2,1)} %all-gather.6.cloned.1.call-done, f32[2,1024,512]{1,2,0:T(8,128)} %copy-done.9, f32[512]{0:T(512)S(1)} %copy-done.39, f32[2,1024]{1,0:T(2,128)S(1)} %fusion.114, f32[2,1024]{1,0:T(2,128)S(1)} %broadcast_multiply_fusion), kind=kOutput, calls=%fused_computation.138 | convolution fusion | flops 4299161600 | bytes 23087104 | tf_op jit(solution)/shard_map/qmj,ja->qma/dot_general | solution.py:216
  334.5 20.7 %fusion.84 = bf16[2,1024,2048]{2,1,0:T(8,128)(2,1)} fusion(f32[2,1024,2048]{2,1,0:T(8,128)} %fusion.101, bf16[2,1024,512]{2,1,0:T(8,128)(2,1)} %param.29, bf16[2048,512]{1,0:T(8,128)(2,1)} %all-gather.8.cloned.1.call-done), kind=kOutput, calls=%fused_computation.100 | convolution fusion | flops 4378853376 | bytes 29360128 | tf_op jit(solution)/shard_map/wtp,np->wtn/dot_general | solution.py:234
  377.3 405.8 %while.108 = (s32[]{:T(128)}, f32[8,16]{1,0:T(8,128)}, bf16[2,2,512,8,64]{2,4,3,1,0:T(8,128)(2,1)}, f32[2,2,1024,8,64]{2,4,3,1,0:T(8,128)}, f32[2,2,1024,8,64]{2...) while((s32[]{:T(128)}, f32[8,16]{1,0:T(8,128)}, ...), condition=%wide.region_16.17_spmd.clone, body=%wide.region_12.16_spmd.sunk.clone.sunk | while | flops 3056334336 | bytes 384927232 | solution.py:153
  392.2 18.8 %copy.99 = f32[8,512,1024]{2,1,0:T(8,128)} copy(f32[8,512,1024]{2,0,1:T(8,128)S(1)} %fusion.160) | data formatting | bytes 33554432 | tf_op jit(solution)/shard_map/while
  411.0 158.8 %while.110 = (s32[]{:T(128)}, f32[8,16]{1,0:T(8,128)S(1)}, bf16[2,512,8,64]{1,3,2,0:T(8,128)(2,1)}, f32[2,1024,8,64]{1,3,2,0:T(8,128)}, f32[2,1024,8,64]{1,3,2,0...) while((s32[]{:T(128)}, f32[8,16]{1,0:T(8,128)S(1)}, ...), condition=%wide.region_15.15_spmd.clone, body=%wide.region_13.14_spmd.clone.sunk | while | flops 2896425984 | bytes 307323424 | solution.py:145
  422.6 18.3 %multiply_reduce_fusion.5 = (f32[8,512]{1,0:T(8,128)S(1)}, f32[8,512,1024]{2,1,0:T(8,128)}) fusion(f32[8,512,1024]{2,1,0:T(8,128)} %fusion.170, f32[8,512]{1,0:T(8,128)S(1)} %dynamic-slice_bitcast_fusion.2, f32[8,512,1024]{2,1,0:T(8,128)} %get-tuple-element.1658, bf16[2,1024,8,64]{1,3,2,0:T(8,128)(2,1)S(1)} %get-tuple-element.1657, s32[]{:T(128)S(6)} %copy.109, ...), kind=kOutput, calls=%fused_computation.41.clone.1 | convolution fusion | flops 562032640 | bytes 52462088 | tf_op jit(solution)/shard_map/while/body/eval_jaxpr/while/body/eval_jaxpr/qhd,khd->hqk/dot_general | solution.py:35
  440.9 11.6 multiply_convert_fusion.8
  469.3 12.7 %copy.100 = bf16[8,512,1024]{1,0,2:T(8,128)(2,1)} copy(bf16[8,512,1024]{2,1,0:T(8,128)(2,1)} %copy-done) | data formatting | bytes 16777216 | tf_op jit(solution)/shard_map/while/body/eval_jaxpr/while/body/eval_jaxpr/convert_element_type | solution.py:115
  502.0 18.2 %multiply_reduce_fusion.5 = (f32[8,512]{1,0:T(8,128)S(1)}, f32[8,512,1024]{2,1,0:T(8,128)}) fusion(f32[8,512,1024]{2,1,0:T(8,128)} %fusion.170, f32[8,512]{1,0:T(8,128)S(1)} %dynamic-slice_bitcast_fusion.2, f32[8,512,1024]{2,1,0:T(8,128)} %get-tuple-element.1658, bf16[2,1024,8,64]{1,3,2,0:T(8,128)(2,1)S(1)} %get-tuple-element.1657, s32[]{:T(128)S(6)} %copy.109, ...), kind=kOutput, calls=%fused_computation.41.clone.1 | convolution fusion | flops 562032640 | bytes 52462088 | tf_op jit(solution)/shard_map/while/body/eval_jaxpr/while/body/eval_jaxpr/qhd,khd->hqk/dot_general | solution.py:35
  548.6 12.7 %copy.100 = bf16[8,512,1024]{1,0,2:T(8,128)(2,1)} copy(bf16[8,512,1024]{2,1,0:T(8,128)(2,1)} %copy-done) | data formatting | bytes 16777216 | tf_op jit(solution)/shard_map/while/body/eval_jaxpr/while/body/eval_jaxpr/convert_element_type | solution.py:115
  595.2 18.8 %copy.99 = f32[8,512,1024]{2,1,0:T(8,128)} copy(f32[8,512,1024]{2,0,1:T(8,128)S(1)} %fusion.160) | data formatting | bytes 33554432 | tf_op jit(solution)/shard_map/while
  614.0 158.0 %while.110 = (s32[]{:T(128)}, f32[8,16]{1,0:T(8,128)S(1)}, bf16[2,512,8,64]{1,3,2,0:T(8,128)(2,1)}, f32[2,1024,8,64]{1,3,2,0:T(8,128)}, f32[2,1024,8,64]{1,3,2,0...) while((s32[]{:T(128)}, f32[8,16]{1,0:T(8,128)S(1)}, ...), condition=%wide.region_15.15_spmd.clone, body=%wide.region_13.14_spmd.clone.sunk | while | flops 2896425984 | bytes 307323424 | solution.py:145
  625.5 18.1 %multiply_reduce_fusion.5 = (f32[8,512]{1,0:T(8,128)S(1)}, f32[8,512,1024]{2,1,0:T(8,128)}) fusion(f32[8,512,1024]{2,1,0:T(8,128)} %fusion.170, f32[8,512]{1,0:T(8,128)S(1)} %dynamic-slice_bitcast_fusion.2, f32[8,512,1024]{2,1,0:T(8,128)} %get-tuple-element.1658, bf16[2,1024,8,64]{1,3,2,0:T(8,128)(2,1)S(1)} %get-tuple-element.1657, s32[]{:T(128)S(6)} %copy.109, ...), kind=kOutput, calls=%fused_computation.41.clone.1 | convolution fusion | flops 562032640 | bytes 52462088 | tf_op jit(solution)/shard_map/while/body/eval_jaxpr/while/body/eval_jaxpr/qhd,khd->hqk/dot_general | solution.py:35
  671.8 12.7 %copy.100 = bf16[8,512,1024]{1,0,2:T(8,128)(2,1)} copy(bf16[8,512,1024]{2,1,0:T(8,128)(2,1)} %copy-done) | data formatting | bytes 16777216 | tf_op jit(solution)/shard_map/while/body/eval_jaxpr/while/body/eval_jaxpr/convert_element_type | solution.py:115
  704.5 18.1 %multiply_reduce_fusion.5 = (f32[8,512]{1,0:T(8,128)S(1)}, f32[8,512,1024]{2,1,0:T(8,128)}) fusion(f32[8,512,1024]{2,1,0:T(8,128)} %fusion.170, f32[8,512]{1,0:T(8,128)S(1)} %dynamic-slice_bitcast_fusion.2, f32[8,512,1024]{2,1,0:T(8,128)} %get-tuple-element.1658, bf16[2,1024,8,64]{1,3,2,0:T(8,128)(2,1)S(1)} %get-tuple-element.1657, s32[]{:T(128)S(6)} %copy.109, ...), kind=kOutput, calls=%fused_computation.41.clone.1 | convolution fusion | flops 562032640 | bytes 52462088 | tf_op jit(solution)/shard_map/while/body/eval_jaxpr/while/body/eval_jaxpr/qhd,khd->hqk/dot_general | solution.py:35
  750.8 12.7 %copy.100 = bf16[8,512,1024]{1,0,2:T(8,128)(2,1)} copy(bf16[8,512,1024]{2,1,0:T(8,128)(2,1)} %copy-done) | data formatting | bytes 16777216 | tf_op jit(solution)/shard_map/while/body/eval_jaxpr/while/body/eval_jaxpr/convert_element_type | solution.py:115
  814.3 12.0 convolution_bitcast_fusion.1
  838.4 12.9 %add_convert_fusion.1 = bf16[2,1024,512]{1,2,0:T(8,128)(2,1)} fusion(f32[2,1024,512]{1,2,0:T(8,128)} %copy-done.9, bf16[2048,512]{1,0:T(8,128)(2,1)} %all-gather.8.cloned.1.call-done, f32[2,1024,2048]{2,1,0:T(8,128)} %fusion.101), kind=kOutput, calls=%fused_computation.123 | convolution fusion | flops 4334813184 | bytes 25165824 | tf_op jit(solution)/shard_map/hor,rt->hot/dot_general | solution.py:221
  865.0 37.1 %all-reduce.4 = (f32[512]{0:T(512)S(1)}, f32[8,16]{1,0:T(8,128)}, f32[512]{0:T(512)S(1)}) all-reduce(f32[512]{0:T(512)S(1)} %get-tuple-element.1110, f32[8,16]{1,0:T(8,128)S(1)} %copy-done.38, f32[512]{0:T(512)S(1)} %copy-done.41), channel_id=2, replica_groups=mesh['dp'=32] {'dp'}, use_global_device_ids=true, to_apply=%region_22.23.clone | all-reduce | flops 1152 | bytes 9216
  913.4 141.6 %reduce-scatter.11.cloned.1.call-done = f32[64,512]{1,0:T(8,128)} async-done(((f32[2048,512]{1,0:T(8,128)}), f32[64,512]{1,0:T(8,128)}) %reduce-scatter.11.cloned.1.call-update) | async-done | bytes 131088 | tf_op jit(solution)/shard_map/reduce_scatter | solution.py:285
  1055.0 139.7 %reduce-scatter.9.cloned.1.call-done = f32[16,2048]{1,0:T(8,128)} async-done(((f32[512,2048]{1,0:T(8,128)}), f32[16,2048]{1,0:T(8,128)}) %reduce-scatter.9.cloned.1.call-update) | async-done | bytes 131088 | tf_op jit(solution)/shard_map/reduce_scatter | solution.py:284
  (332 shorter events, 460.7 us)
Async XLA Ops:
  7.2 100.0 %all-gather.4.cloned.1.call-start = ((), (), s32[]{:S(2)}) async-start(), calls=%async_computation.4 | async-start | bytes 1622016 | tf_op jit(solution)/shard_map/all_gather | solution.py:181
  7.9 313.2 %all-gather.6.cloned.1.call-start = ((), (), s32[]{:S(2)}) async-start(), calls=%async_computation.5 | async-start | bytes 2162688 | tf_op jit(solution)/shard_map/all_gather | solution.py:184
  8.7 325.8 %all-gather.8.cloned.1.call-start = ((), (), s32[]{:S(2)}) async-start(), calls=%async_computation.6 | async-start | bytes 2162688 | tf_op jit(solution)/shard_map/all_gather | solution.py:185
  9.4 904.0 %reduce-scatter.7.cloned.1.call-start = ((), (), s32[]{:S(2)}) async-start(), calls=%async_computation.8 | async-start | bytes 1081344 | tf_op jit(solution)/shard_map/reduce_scatter | solution.py:282
  53.3 53.9 %copy-start.34 = (f32[512]{0:T(512)}, f32[512]{0:T(512)S(1)}, u32[]{:S(2)}) copy-start(f32[512]{0:T(512)S(1)} %convert_element_type.79) | copy-start | bytes 6148
  102.0 12.2 %copy-start.20 = (f32[2,1024]{1,0:T(2,128)}, f32[2,1024]{1,0:T(2,128)S(1)}, u32[]{:S(2)}) copy-start(f32[2,1024]{1,0:T(2,128)S(1)} %broadcast_multiply_fusion.1) | copy-start | bytes 24580
  160.5 56.4 %copy-start.30 = (f32[2,2,8,512]{3,2,1,0:T(8,128)S(1)}, f32[2,2,8,512]{3,2,1,0:T(8,128)}, u32[]{:S(2)}) copy-start(f32[2,2,8,512]{3,2,1,0:T(8,128)} %get-tuple-element.1724) | copy-start | bytes 196612 | tf_op jit(solution)/shard_map/while
  160.6 57.5 %copy-start.44 = (bf16[8,16]{1,0:T(8,128)(2,1)S(1)}, bf16[8,16]{1,0:T(8,128)(2,1)}, u32[]{:S(2)}) copy-start(bf16[8,16]{1,0:T(8,128)(2,1)} %get-tuple-element.1881) | copy-start | bytes 772 | tf_op jit(solution)/shard_map/while
  162.3 19.8 %copy-start.5 = (bf16[2,1024,8,64]{1,3,2,0:T(8,128)(2,1)S(1)}, bf16[2,1024,8,64]{1,3,2,0:T(8,128)(2,1)}, u32[]{:S(2)}) copy-start(bf16[2,1024,8,64]{1,3,2,0:T(8,128)(2,1)} %get-tuple-element.1695) | copy-start | bytes 6291460 | tf_op jit(solution)/shard_map/while/body/eval_jaxpr/while
  190.6 19.7 %copy-start.5 = (bf16[2,1024,8,64]{1,3,2,0:T(8,128)(2,1)S(1)}, bf16[2,1024,8,64]{1,3,2,0:T(8,128)(2,1)}, u32[]{:S(2)}) copy-start(bf16[2,1024,8,64]{1,3,2,0:T(8,128)(2,1)} %get-tuple-element.1695) | copy-start | bytes 6291460 | tf_op jit(solution)/shard_map/while/body/eval_jaxpr/while
  247.1 56.1 %copy-start.30 = (f32[2,2,8,512]{3,2,1,0:T(8,128)S(1)}, f32[2,2,8,512]{3,2,1,0:T(8,128)}, u32[]{:S(2)}) copy-start(f32[2,2,8,512]{3,2,1,0:T(8,128)} %get-tuple-element.1724) | copy-start | bytes 196612 | tf_op jit(solution)/shard_map/while
  247.1 57.2 %copy-start.44 = (bf16[8,16]{1,0:T(8,128)(2,1)S(1)}, bf16[8,16]{1,0:T(8,128)(2,1)}, u32[]{:S(2)}) copy-start(bf16[8,16]{1,0:T(8,128)(2,1)} %get-tuple-element.1881) | copy-start | bytes 772 | tf_op jit(solution)/shard_map/while
  248.9 19.7 %copy-start.5 = (bf16[2,1024,8,64]{1,3,2,0:T(8,128)(2,1)S(1)}, bf16[2,1024,8,64]{1,3,2,0:T(8,128)(2,1)}, u32[]{:S(2)}) copy-start(bf16[2,1024,8,64]{1,3,2,0:T(8,128)(2,1)} %get-tuple-element.1695) | copy-start | bytes 6291460 | tf_op jit(solution)/shard_map/while/body/eval_jaxpr/while
  276.9 19.7 %copy-start.5 = (bf16[2,1024,8,64]{1,3,2,0:T(8,128)(2,1)S(1)}, bf16[2,1024,8,64]{1,3,2,0:T(8,128)(2,1)}, u32[]{:S(2)}) copy-start(bf16[2,1024,8,64]{1,3,2,0:T(8,128)(2,1)} %get-tuple-element.1695) | copy-start | bytes 6291460 | tf_op jit(solution)/shard_map/while/body/eval_jaxpr/while
  318.6 44.8 %copy-start.28 = (f32[2,1024]{1,0:T(2,128)}, f32[2,1024]{1,0:T(2,128)S(1)}, u32[]{:S(2)}) copy-start(f32[2,1024]{1,0:T(2,128)S(1)} %broadcast_multiply_fusion) | copy-start | bytes 24580
  321.1 42.4 %copy-start.32 = (f32[2,1024]{1,0:T(2,128)}, f32[2,1024]{1,0:T(2,128)S(1)}, u32[]{:S(2)}) copy-start(f32[2,1024]{1,0:T(2,128)S(1)} %fusion.114) | copy-start | bytes 24580
  334.5 20.7 %copy-start.10 = (f32[2,1024,512]{1,2,0:T(8,128)S(1)}, f32[2,1024,512]{1,2,0:T(8,128)}, u32[]{:S(2)}) copy-start(f32[2,1024,512]{1,2,0:T(8,128)} %copy-done.9) | copy-start | bytes 12582916
  334.5 20.7 %copy-start.42 = (bf16[512,2048]{1,0:T(8,128)(2,1)S(1)}, bf16[512,2048]{1,0:T(8,128)(2,1)}, u32[]{:S(2)}) copy-start(bf16[512,2048]{1,0:T(8,128)(2,1)} %all-gather.6.cloned.1.call-done) | copy-start | bytes 6291460
  375.1 538.3 %reduce-scatter.5.cloned.1.call-start = ((), (), s32[]{:S(2)}) async-start(), calls=%async_computation.7 | async-start | bytes 3244032 | tf_op jit(solution)/shard_map/reduce_scatter | solution.py:281
  392.2 18.8 %copy-start.36 = (f32[8,16]{1,0:T(8,128)S(1)}, f32[8,16]{1,0:T(8,128)}, u32[]{:S(2)}) copy-start(f32[8,16]{1,0:T(8,128)} %get-tuple-element.1781) | copy-start | bytes 1540 | tf_op jit(solution)/shard_map/while
  411.0 11.6 copy-start.3
  440.8 15.5 %copy-start.1 = (f32[8,512,1024]{2,1,0:T(8,128)S(1)}, f32[8,512,1024]{2,1,0:T(8,128)}, u32[]{:S(2)}) copy-start(f32[8,512,1024]{2,1,0:T(8,128)} %get-tuple-element.1597) | copy-start | bytes 50331652 | tf_op jit(solution)/shard_map/while/body/eval_jaxpr/while
  490.4 11.6 copy-start.3
  520.2 15.4 %copy-start.1 = (f32[8,512,1024]{2,1,0:T(8,128)S(1)}, f32[8,512,1024]{2,1,0:T(8,128)}, u32[]{:S(2)}) copy-start(f32[8,512,1024]{2,1,0:T(8,128)} %get-tuple-element.1597) | copy-start | bytes 50331652 | tf_op jit(solution)/shard_map/while/body/eval_jaxpr/while
  595.2 18.8 %copy-start.36 = (f32[8,16]{1,0:T(8,128)S(1)}, f32[8,16]{1,0:T(8,128)}, u32[]{:S(2)}) copy-start(f32[8,16]{1,0:T(8,128)} %get-tuple-element.1781) | copy-start | bytes 1540 | tf_op jit(solution)/shard_map/while
  614.0 11.6 copy-start.3
  643.7 15.4 %copy-start.1 = (f32[8,512,1024]{2,1,0:T(8,128)S(1)}, f32[8,512,1024]{2,1,0:T(8,128)}, u32[]{:S(2)}) copy-start(f32[8,512,1024]{2,1,0:T(8,128)} %get-tuple-element.1597) | copy-start | bytes 50331652 | tf_op jit(solution)/shard_map/while/body/eval_jaxpr/while
  692.9 11.6 copy-start.3
  722.6 15.4 %copy-start.1 = (f32[8,512,1024]{2,1,0:T(8,128)S(1)}, f32[8,512,1024]{2,1,0:T(8,128)}, u32[]{:S(2)}) copy-start(f32[8,512,1024]{2,1,0:T(8,128)} %get-tuple-element.1597) | copy-start | bytes 50331652 | tf_op jit(solution)/shard_map/while/body/eval_jaxpr/while
  814.2 240.8 %reduce-scatter.11.cloned.1.call-start = ((), (), s32[]{:S(2)}) async-start(), calls=%async_computation.10 | async-start | bytes 4325376 | tf_op jit(solution)/shard_map/reduce_scatter | solution.py:285
  826.3 368.5 %reduce-scatter.9.cloned.1.call-start = ((), (), s32[]{:S(2)}) async-start(), calls=%async_computation.9 | async-start | bytes 4325376 | tf_op jit(solution)/shard_map/reduce_scatter | solution.py:284
  861.3 42.0 %copy-start.25 = (f32[2,1024]{1,0:T(2,128)S(1)}, f32[2,1024]{1,0:T(2,128)}, u32[]{:S(2)}) copy-start(f32[2,1024]{1,0:T(2,128)} %copy-done.24) | copy-start | bytes 24580
  (55 other events, 296.1 us)
Sparse Core Ops, SparseCore 0:
  10.9 58.0 all-gather.3
  71.9 55.3 all-gather.5
  130.1 55.2 all-gather.7
  375.2 130.9 reduce-scatter.6
  814.3 98.0 reduce-scatter.4
  915.2 139.7 reduce-scatter.10
  1057.9 136.7 reduce-scatter.8
where the time goes:
time: 1210 us; the launch traced here: 1200 us
  matrix products  400 us (33%)
  waiting for transfers between devices  284 us (23%)
  local copies, waits for them, and re-layouts  256 us (21%)
  blocking collectives  124 us (10%)
  other arithmetic  118 us (10%)
  between operations  14.8 us (1%)
    reduce_scatter x1, waiting for transfers between devices, on_device(): lax.psum_scatter(down_weight_gradient, 'dp', scatter_dimension=0, tiled=T...  142 us
    reduce_scatter x1, waiting for transfers between devices, on_device(): lax.psum_scatter(grad_w_up, 'dp', scatter_dimension=0, tiled=True)  140 us
    dot_general x8, matrix products, block_scores(): jnp.einsum('qhd,khd->hqk', block_queries, seq_keys, preferred_element_typ...  120 us
    while x96, local copies, waits for them, and re-layouts  102 us
    unnamed x2, blocking collectives  79.2 us
    convert_element_type x4, local copies, waits for them, and re-layouts, one_sequence(): (probabilities * (prob_grads - row_dot)).astype(jnp.bfloat16)  50.6 us
    convert_element_type x4, other arithmetic, one_sequence(): (probabilities * (prob_grads - row_dot)).astype(jnp.bfloat16)  46 us
    all_gather x1, blocking collectives, on_device(): lax.all_gather(w_out, 'dp', axis=0, tiled=True)  44.8 us
  transfers between devices with their start and end apart: 7, of which 2 were waited for; matrix products, arithmetic and copies ran while one was open for 58% of the time, Pallas kernels for 0%

commit v1 on v0

v1 whole, which is shorter than its diff:
```python
import functools

import jax
import jax.numpy as jnp
import numpy as np
from jax import lax
from jax.experimental import pallas as pl
from jax.experimental.pallas import tpu as pltpu
from jax.sharding import PartitionSpec as P

MESH = pl.DeviceIdType.MESH
F32 = jnp.float32
BF = jnp.bfloat16
EPS = 1e-05


AXES = ("z", "y", "x", "core")


def device_grid(devices):
    return (devices // 8, 2, 2, 2)


def grid_position(sizes):
    rest = lax.axis_index("dp")
    place = []
    for size in reversed(sizes):
        place.append(lax.rem(rest, size))
        rest = lax.div(rest, size)
    return tuple(reversed(place))


def device_at(place, sizes):
    index = place[0]
    for axis in range(1, 4):
        index = index * sizes[axis] + place[axis]
    return index


def moved(place, sizes, axis, step):
    other = list(place)
    other[axis] = lax.rem(place[axis] + step, sizes[axis])
    return tuple(other)


def greet(sizes):
    place = grid_position(sizes)
    barrier = pltpu.get_barrier_semaphore()
    count = 0
    for axis in range(4):
        for step in range(1, sizes[axis]):
            pl.semaphore_signal(
                barrier,
                inc=1,
                device_id=(device_at(moved(place, sizes, axis, step), sizes),),
                device_id_type=MESH,
            )
            count += 1
    pl.semaphore_wait(barrier, count)


class Gather:
    def __init__(self, sizes, order, own, whole, local_sem, send_sems, recv_sems):
        self.sizes, self.order = sizes, order
        self.own, self.whole = own, whole
        self.local_sem, self.send_sems, self.recv_sems = local_sem, send_sems, recv_sems

    def copies(self, phase):
        place = grid_position(self.sizes)
        done = self.order[:phase]
        index = tuple(slice(None) if a in done else place[a] for a in range(4))
        axis = self.order[phase]
        part = self.whole.at[index]
        return [
            pltpu.make_async_remote_copy(
                src_ref=self.own if phase == 0 else part,
                dst_ref=part,
                send_sem=self.send_sems.at[phase, step],
                recv_sem=self.recv_sems.at[phase, step],
                device_id=(device_at(moved(place, self.sizes, axis, step), self.sizes),),
                device_id_type=MESH,
            )
            for step in range(1, self.sizes[axis])
        ]

    def local(self):
        return pltpu.make_async_copy(
            self.own, self.whole.at[grid_position(self.sizes)], self.local_sem
        )

    def start(self, phase):
        if phase == 0:
            self.local().start()
        for copy in self.copies(phase):
            copy.start()

    def finish(self, phase):
        if phase == 0:
            self.local().wait()
        for copy in self.copies(phase):
            copy.wait()


class Scatter:
    def __init__(self, sizes, order, terms, sums, landing, result, send_sems, recv_sems):
        self.sizes, self.order = sizes, order
        self.held = [terms] + list(sums)
        self.landing, self.result = landing, result
        self.send_sems, self.recv_sems = send_sems, recv_sems

    @staticmethod
    def shapes(sizes, order, block):
        left, sums, landing = set(range(4)), [], []
        for phase, axis in enumerate(order):
            left.discard(axis)
            lead = tuple(sizes[a] for a in sorted(left))
            landing.append((sizes[axis] if sizes[axis] > 2 else 1,) + lead + block)
            if phase < 3:
                sums.append(lead + block)
        return sums, landing

    def pick(self, phase, coordinate):
        axis = self.order[phase]
        left = [a for a in range(4) if a not in self.order[:phase]]
        return tuple(coordinate if a == axis else slice(None) for a in left)

    def copies(self, phase):
        place = grid_position(self.sizes)
        axis = self.order[phase]
        out = []
        for step in range(1, self.sizes[axis]):
            other = moved(place, self.sizes, axis, step)
            out.append(
                pltpu.make_async_remote_copy(
                    src_ref=self.held[phase].at[self.pick(phase, other[axis])],
                    dst_ref=self.landing[phase].at[place[axis] if self.sizes[axis] > 2 else 0],
                    send_sem=self.send_sems.at[phase, step],
                    recv_sem=self.recv_sems.at[phase, step],
                    device_id=(device_at(other, self.sizes),),
                    device_id_type=MESH,
                )
            )
        return out

    def start(self, phase):
        for copy in self.copies(phase):
            copy.start()

    def finish(self, phase):
        for copy in self.copies(phase):
            copy.wait()
        place = grid_position(self.sizes)
        axis = self.order[phase]
        left = [a for a in range(4) if a not in self.order[: phase + 1]]
        held, landed = self.held[phase], self.landing[phase]
        lead = [self.sizes[a] for a in left]
        target = self.held[phase + 1] if phase < 3 else self.result

        def one(at):
            spot = tuple(at)
            full = list(spot)
            full.insert(sorted(left + [axis]).index(axis), place[axis])
            if self.sizes[axis] == 2:
                total = held[tuple(full)].astype(jnp.float32) + landed[(0,) + spot].astype(
                    jnp.float32
                )
            else:
                landed[(place[axis],) + spot] = held[tuple(full)]
                total = landed[(0,) + spot].astype(jnp.float32)
                for source in range(1, self.sizes[axis]):
                    total = total + landed[(source,) + spot].astype(jnp.float32)
            if phase < 3:
                target[spot] = total.astype(target.dtype)
            else:
                target[...] = total.astype(target.dtype)

        if not left:
            one(())
        else:
            def body(count, unused):
                at = []
                for size in reversed(lead):
                    at.append(lax.rem(count, size))
                    count = lax.div(count, size)
                one(reversed(at))
                return unused
            lax.fori_loop(0, int(np.prod(lead)), body, 0)


LOW=(0,1,2,3,4,5,6,7,8,12,16,32,64,128,256,512)
T=256
NEG=-1e30
def cp(**k): return pltpu.CompilerParams(vmem_limit_bytes=56*2**20, **k)
def dot_nt(a,b): return lax.dot_general(a,b,(((1,),(1,)),((),())),preferred_element_type=jnp.float32)
def dot_nn(a,b): return jnp.dot(a,b,preferred_element_type=jnp.float32)
def dot_tn(a,b): return lax.dot_general(a,b,(((0,),(0,)),((),())),preferred_element_type=jnp.float32)

def bias_of(dist, row):
    out=jnp.zeros(dist.shape,jnp.float32)+row[:,0:1]
    for b in range(1,16):
        out=jnp.where(dist>=LOW[b],row[:,b:b+1],out)
    return jnp.where(dist<0,NEG,out)

def build_bias(table_ref, hp, bias, transposed):
    lane=lax.broadcasted_iota(jnp.int32,(1,2*T),1)
    m=jnp.where(lane<T,lane,lane-2*T)
    for h in range(2):
        row=table_ref[0,h:h+1,:]
        for bd in range(3):
            w=bias_of(bd*T+(m if transposed else -m),row)
            tile=pltpu.roll(jnp.broadcast_to(w,(T,2*T)),0,1,stride=1,stride_axis=0)
            bias[h,bd]=tile[:,:T]
        bias[h,3]=jnp.broadcast_to(row[:,15:16],(T,T))

def split3(v):
    hi=v.astype(jnp.bfloat16); r=v-hi.astype(jnp.float32)
    mid=r.astype(jnp.bfloat16); lo=(r-mid.astype(jnp.float32)).astype(jnp.bfloat16)
    return hi,mid,lo

def halves(h, main, extra, rows):
    lane=lax.broadcasted_iota(jnp.int32,(rows,128),1)
    out=jnp.where((lane//64)==h,main,jnp.zeros((),main.dtype))
    base=64*(1-h)
    for n,e in enumerate(extra):
        if e is not None:
            out=jnp.where(lane==base+n,jnp.broadcast_to(e,(rows,128)).astype(jnp.bfloat16),out)
    return out

def fwd_kernel(vl_ref,table_ref,q_ref,k_ref,v_ref,mixed_ref,qa_ref,bias):
    hp=pl.program_id(0); s=pl.program_id(1)
    @pl.when(s==0)
    def _(): build_bias(table_ref,hp,bias,False)
    L=q_ref.shape[1]; nb=L//T
    one=jnp.ones((),jnp.bfloat16)
    key=lax.broadcasted_iota(jnp.int32,(L,1),0)
    mask=jnp.where(key<vl_ref[s],0.0,NEG)
    lane=lax.broadcasted_iota(jnp.int32,(T,128),1)
    ks=[halves(h,k_ref[0],[1.0,1.0,1.0,mask],L) for h in range(2)]
    for qb in range(nb):
        kk=(qb+1)*T
        qt=q_ref[0,qb*T:(qb+1)*T,:]*jnp.asarray(0.125,jnp.bfloat16)
        outs=[]
        for h in range(2):
            qh=halves(h,qt,[None,None,None,1.0],T)
            sc=dot_nt(qh,ks[h][:kk])
            sc=jnp.concatenate([sc[:,kb*T:(kb+1)*T]+bias[h,qb-kb] for kb in range(qb+1)],axis=1)
            mx=jnp.max(sc,axis=1,keepdims=True)
            p=jnp.exp(sc-mx)
            l=jnp.sum(p,axis=1,keepdims=True)
            o=dot_nn(p.astype(jnp.bfloat16),v_ref[0,:kk,:])
            outs.append(o*(1.0/l))
            hi,mid,lo=split3(-(mx+jnp.log(l)))
            qa_ref[0,0,h,qb*T:(qb+1)*T,:]=halves(h,qt,[hi,mid,lo,1.0],T)
        mixed_ref[0,qb*T:(qb+1)*T,:]=jnp.where(lane<64,outs[0],outs[1]).astype(jnp.bfloat16)

def attn_fwd(vl,table,qkv):
    S,L,W=qkv.shape; HP=W//3//128
    return pl.pallas_call(fwd_kernel,grid=(HP,S),
        in_specs=[pl.BlockSpec(memory_space=pltpu.SMEM),pl.BlockSpec((1,2,16),lambda h,s:(h,0,0)),
          pl.BlockSpec((1,L,128),lambda h,s:(s,0,h)),pl.BlockSpec((1,L,128),lambda h,s:(s,0,HP+h)),pl.BlockSpec((1,L,128),lambda h,s:(s,0,2*HP+h))],
        out_specs=[pl.BlockSpec((1,L,128),lambda h,s:(s,0,h)),pl.BlockSpec((1,1,2,L,128),lambda h,s:(s,h,0,0,0))],
        out_shape=[jax.ShapeDtypeStruct((S,L,HP*128),jnp.bfloat16),jax.ShapeDtypeStruct((S,HP,2,L,128),jnp.bfloat16)],
        scratch_shapes=[pltpu.VMEM((2,4,T,T),jnp.float32)],
        compiler_params=cp())(vl,table.astype(jnp.float32).reshape(HP,2,16),qkv,qkv,qkv)

def bwd_kernel(mode,vl_ref,table_ref,qa_ref,k_ref,v_ref,o_ref,g_ref,dq_ref,dk_ref,dv_ref,tab_ref,bias,gacc,far,dqt):
    hp=pl.program_id(0); s=pl.program_id(1)
    L=k_ref.shape[1]; nb=L//T
    @pl.when(s==0)
    def _():
        build_bias(table_ref,hp,bias,True)
        gacc[...]=jnp.zeros_like(gacc); far[...]=jnp.zeros_like(far)
    key=lax.broadcasted_iota(jnp.int32,(L,1),0)
    mask=jnp.where(key<vl_ref[s],0.0,NEG)
    lane=lax.broadcasted_iota(jnp.int32,(T,128),1)
    g=g_ref[0]
    prod=g.astype(jnp.float32)*o_ref[0].astype(jnp.float32)
    lane_l=lax.broadcasted_iota(jnp.int32,(L,128),1)
    ks=[halves(h,k_ref[0],[1.0,1.0,1.0,mask],L) for h in range(2)]
    vs=[halves(h,v_ref[0],[1.0,1.0,1.0],L) for h in range(2)]
    gs=[]
    for h in range(2):
        d=jnp.sum(jnp.where((lane_l//64)==h,prod,0.0),axis=1,keepdims=True)
        hi,mid,lo=split3(-d)
        gs.append(halves(h,g,[hi,mid,lo],L))
    if mode==0:
        kt=(k_ref[0]*jnp.asarray(0.125,jnp.bfloat16)).T
    dqs=[[None]*nb,[None]*nb]
    for kb in range(nb):
        dks=[];dvs=[]
        for h in range(2):
            qh=qa_ref[0,0,h]
            st=dot_nt(ks[h][kb*T:(kb+1)*T],qh[kb*T:])
            dp=dot_nt(vs[h][kb*T:(kb+1)*T],gs[h][kb*T:])
            st=jnp.concatenate([st[:,i*T:(i+1)*T]+bias[h,i] for i in range(nb-kb)],axis=1)
            p=jnp.exp(st)
            ds=p*dp
            pb=p.astype(jnp.bfloat16); dsb=ds.astype(jnp.bfloat16)
            dvs.append(dot_nn(pb,gs[h][kb*T:])); dks.append(dot_nn(dsb,qh[kb*T:]))
            for i in range(min(nb-kb,3)):
                gacc[h,i]+=ds[:,i*T:(i+1)*T]
            if nb-kb>3:
                far[h:h+1,:]+=jnp.sum(ds[:,3*T:],axis=0,keepdims=True)
            if mode==0:
                r=dot_nn(kt[h*64:(h+1)*64,kb*T:(kb+1)*T],dsb)
                if kb==0: dqt[h*64:(h+1)*64,:]=r
                else: dqt[h*64:(h+1)*64,kb*T:]+=r
            else:
                r=dot_tn(dsb,k_ref[0,kb*T:(kb+1)*T,:])
                if kb==0: dqt[h]=r
                else: dqt[h,kb*T:]+=r
        dk_ref[0,kb*T:(kb+1)*T,:]=jnp.where(lane<64,dks[0],dks[1]).astype(jnp.bfloat16)
        dv_ref[0,kb*T:(kb+1)*T,:]=jnp.where(lane<64,dvs[0],dvs[1]).astype(jnp.bfloat16)
    if mode==0:
        dq_ref[0]=dqt[...].T.astype(jnp.bfloat16)
    else:
        dq_ref[0]=(jnp.where(lane_l<64,dqt[0],dqt[1])*0.125).astype(jnp.bfloat16)
    @pl.when(s==pl.num_programs(1)-1)
    def _():
        lane2=lax.broadcasted_iota(jnp.int32,(1,2*T),1)
        m=jnp.where(lane2<T,lane2,lane2-2*T)
        bl=lax.broadcasted_iota(jnp.int32,(1,128),1)
        for h in range(2):
            row=jnp.where(bl==15,jnp.sum(far[h:h+1,:],axis=1,keepdims=True),0.0)
            for bd in range(3):
                w=jnp.concatenate([gacc[h,bd],jnp.zeros((T,T),jnp.float32)],axis=1)
                acc=w[:8]
                for a in range(1,T//8):
                    acc=acc+pltpu.roll(w[8*a:8*a+8],2*T-8*a,1)
                diag=acc[0:1]
                for a in range(1,8):
                    diag=diag+pltpu.roll(acc[a:a+1],2*T-a,1)
                dist=bd*T+m
                for b in range(16):
                    if LOW[b]>=(bd+1)*T or (b<15 and LOW[b+1]<=(bd-1)*T): continue
                    sel=dist>=LOW[b]
                    if b<15: sel=sel&(dist<LOW[b+1])
                    row=row+jnp.where(bl==b,jnp.sum(jnp.where(sel,diag,0.0),axis=1,keepdims=True),0.0)
            tab_ref[0,h:h+1,:]=row

def attn_bwd(vl,table,qa,qkv,mixed,gm,mode=0):
    S,L,W=qkv.shape; HP=W//3//128
    blk=lambda off:pl.BlockSpec((1,L,128),lambda h,s,off=off:(s,0,off+h))
    sh=jax.ShapeDtypeStruct((S,L,HP*128),jnp.bfloat16)
    return pl.pallas_call(functools.partial(bwd_kernel,mode),grid=(HP,S),
        in_specs=[pl.BlockSpec(memory_space=pltpu.SMEM),pl.BlockSpec((1,2,16),lambda h,s:(h,0,0)),
          pl.BlockSpec((1,1,2,L,128),lambda h,s:(s,h,0,0,0)),blk(HP),blk(2*HP),blk(0),blk(0)],
        out_specs=[blk(0),blk(0),blk(0),pl.BlockSpec((1,8,128),lambda h,s:(h,0,0))],
        out_shape=[sh,sh,sh,jax.ShapeDtypeStruct((HP,8,128),jnp.float32)],
        scratch_shapes=[pltpu.VMEM((2,4,T,T),jnp.float32),pltpu.VMEM((2,3,T,T),jnp.float32),pltpu.VMEM((8,T),jnp.float32),
           pltpu.VMEM((128,L) if mode==0 else (2,L,128),jnp.float32)],
        compiler_params=cp())(vl,table.astype(jnp.float32).reshape(HP,2,16),qa,qkv,qkv,mixed,gm)


def ln_parts(v):
    c=v-jnp.mean(v,axis=1,keepdims=True)
    r=lax.rsqrt(jnp.mean(c*c,axis=1,keepdims=True)+EPS)
    return c*r, r
def ln_back(e_in,gain,xhat,r):
    e=e_in*gain
    gv=r*(e-jnp.mean(e,axis=1,keepdims=True)-xhat*jnp.mean(e*xhat,axis=1,keepdims=True))
    return gv, jnp.sum(e_in*xhat,axis=0,keepdims=True)

def qkv_kernel(x_ref,g_ref,w_ref,n_ref,o_ref):
    xhat,_=ln_parts(x_ref[...].astype(F32))
    n=(xhat*g_ref[...].astype(F32)).astype(BF)
    n_ref[...]=n
    o_ref[...]=dot_nn(n,w_ref[...]).astype(BF)
def qkv_fwd(x,gain,w,B=512):
    R,D=x.shape; N=w.shape[1]
    return pl.pallas_call(qkv_kernel,grid=(R//B,),
      in_specs=[pl.BlockSpec((B,D),lambda i:(i,0)),pl.BlockSpec((1,D),lambda i:(0,0)),pl.BlockSpec((D,N),lambda i:(0,0))],
      out_specs=[pl.BlockSpec((B,D),lambda i:(i,0)),pl.BlockSpec((B,N),lambda i:(i,0))],
      out_shape=[jax.ShapeDtypeStruct((R,D),BF),jax.ShapeDtypeStruct((R,N),BF)],compiler_params=cp())(x,gain,w)

def ffn_kernel(x_ref,m_ref,og_ref,g_ref,wo_ref,wu_ref,wd_ref,out_ref,ga_ref,gm_ref,gwo_ref,gwu_ref,gwd_ref,gg_ref,ao,au,ad):
    i=pl.program_id(0)
    m=m_ref[...]; og=og_ref[...]
    after=x_ref[...].astype(F32)+dot_nn(m,wo_ref[...])
    xhat,r=ln_parts(after)
    gain=g_ref[...].astype(F32)
    n=(xhat*gain).astype(BF)
    pre=dot_nn(n,wu_ref[...])
    dh=dot_nt(og,wd_ref[...])
    c=0.7978845608028654
    sq=pre*pre
    t=jnp.tanh(pre*(c+c*0.044715*sq))
    half=0.5*(1.0+t)
    hid=(pre*half).astype(BF)
    dg=half+(0.5*pre)*(1.0-t*t)*(c+3*c*0.044715*sq)
    gp=(dh*dg).astype(BF)
    out_ref[...]=(after+dot_nn(hid,wd_ref[...])).astype(BF)
    pd=dot_tn(hid,og); pu=dot_tn(n,gp)
    dn=dot_nt(gp,wu_ref[...])
    gv,gg=ln_back(dn,gain,xhat,r)
    ga=og.astype(F32)+gv
    ga_ref[...]=ga
    gb=ga.astype(BF)
    po=dot_tn(m,gb)
    gm_ref[...]=dot_nt(gb,wo_ref[...]).astype(BF)
    @pl.when(i==0)
    def _():
        ad[...]=pd; au[...]=pu; ao[...]=po; gg_ref[...]=gg
    @pl.when(i>0)
    def _():
        ad[...]+=pd; au[...]+=pu; ao[...]+=po; gg_ref[...]+=gg
    @pl.when(i==pl.num_programs(0)-1)
    def _():
        gwo_ref[...]=ao[...].astype(BF); gwu_ref[...]=au[...].astype(BF); gwd_ref[...]=ad[...].astype(BF)
def ffn(x,m,og,gain,wo,wu,wd,B=512):
    R,D=x.shape; FF=wu.shape[1]
    row=pl.BlockSpec((B,D),lambda i:(i,0))
    full=lambda a,b:pl.BlockSpec((a,b),lambda i:(0,0))
    return pl.pallas_call(ffn_kernel,grid=(R//B,),
      in_specs=[row,row,row,full(1,D),full(D,D),full(D,FF),full(FF,D)],
      out_specs=[row,row,row,full(D,D),full(D,FF),full(FF,D),full(1,D)],
      out_shape=[jax.ShapeDtypeStruct((R,D),BF),jax.ShapeDtypeStruct((R,D),F32),jax.ShapeDtypeStruct((R,D),BF),
        jax.ShapeDtypeStruct((D,D),BF),jax.ShapeDtypeStruct((D,FF),BF),jax.ShapeDtypeStruct((FF,D),BF),jax.ShapeDtypeStruct((1,D),F32)],
      scratch_shapes=[pltpu.VMEM((D,D),F32),pltpu.VMEM((D,FF),F32),pltpu.VMEM((FF,D),F32)],
      compiler_params=cp())(x,m,og,gain,wo,wu,wd)

def qkvb_kernel(x_ref,n_ref,dq_ref,dk_ref,dv_ref,ga_ref,g_ref,w_ref,gi_ref,gw_ref,gg_ref,acc):
    i=pl.program_id(0)
    D=x_ref.shape[1]
    xhat,r=ln_parts(x_ref[...].astype(F32))
    n=n_ref[...]
    d=jnp.concatenate([dq_ref[...],dk_ref[...],dv_ref[...]],axis=1)
    pw=dot_tn(n,d)
    dn=dot_nt(d,w_ref[...])
    gv,gg=ln_back(dn,g_ref[...].astype(F32),xhat,r)
    gi_ref[...]=(ga_ref[...]+gv).astype(BF)
    @pl.when(i==0)
    def _():
        acc[...]=pw; gg_ref[...]=gg
    @pl.when(i>0)
    def _():
        acc[...]+=pw; gg_ref[...]+=gg
    @pl.when(i==pl.num_programs(0)-1)
    def _():
        gw_ref[...]=acc[...].astype(BF)
def qkv_bwd(x,n,dq,dk,dv,ga,gain,w,B=512):
    R,D=x.shape; N=w.shape[1]
    row=pl.BlockSpec((B,D),lambda i:(i,0))
    full=lambda a,b:pl.BlockSpec((a,b),lambda i:(0,0))
    return pl.pallas_call(qkvb_kernel,grid=(R//B,),
      in_specs=[row]*6+[full(1,D),full(D,N)],
      out_specs=[row,full(D,N),full(1,D)],
      out_shape=[jax.ShapeDtypeStruct((R,D),BF),jax.ShapeDtypeStruct((D,N),BF),jax.ShapeDtypeStruct((1,D),F32)],
      scratch_shapes=[pltpu.VMEM((D,N),F32)],
      compiler_params=cp())(x,n,dq,dk,dv,ga,gain,w)


def gather_kernel(sizes, orders, *refs):
    n = len(orders)
    own, whole, (local, send, recv) = refs[:n], refs[n:2 * n], refs[2 * n:]
    greet(sizes)
    parts = [Gather(sizes, orders[k], own[k], whole[k], local.at[k], send.at[k], recv.at[k]) for k in range(n)]
    for part in parts:
        part.start(0)
    for phase in range(4):
        for part in parts:
            part.finish(phase)
            if phase < 3:
                part.start(phase + 1)


def gather_all(sizes, arrays, orders):
    n = len(arrays)
    anyspace = pl.BlockSpec(memory_space=pl.ANY)
    return pl.pallas_call(
        functools.partial(gather_kernel, sizes, orders),
        in_specs=[anyspace] * n,
        out_specs=[anyspace] * n,
        out_shape=[jax.ShapeDtypeStruct(sizes + a.shape, a.dtype) for a in arrays],
        scratch_shapes=[pltpu.SemaphoreType.DMA((n,)), pltpu.SemaphoreType.DMA((n, 4, max(sizes))), pltpu.SemaphoreType.DMA((n, 4, max(sizes)))],
        compiler_params=pltpu.CompilerParams(collective_id=1, has_side_effects=True),
    )(*arrays)


def pack_small(sizes, small, gain_first, gain_second, table):
    for z in range(sizes[0]):
        block = [gain_first[:, z * 128:(z + 1) * 128], gain_second[:, z * 128:(z + 1) * 128], jnp.zeros((6, 128), F32)]
        block += [table[pair, 0:2, :] for pair in range(table.shape[0])]
        block = jnp.concatenate(block, axis=0)

        def body(count, unused):
            small[z, lax.div(count, 4), lax.rem(lax.div(count, 2), 2), lax.rem(count, 2)] = block
            return unused

        lax.fori_loop(0, 8, body, 0)


def scatter_kernel(sizes, orders, plan, *refs):
    n = len(orders)
    terms, (gain_first, gain_second, table), results = refs[:n - 1], refs[n - 1:n + 2], refs[n + 2:2 * n + 2]
    rest = list(refs[2 * n + 2:])
    small = rest.pop(0)
    send, recv = rest[-2:]
    pack_small(sizes, small, gain_first, gain_second, table)
    parts = []
    for k in range(n):
        sums, landing = plan[k]
        s = [rest.pop(0) for _ in sums]
        l = [rest.pop(0) for _ in landing]
        parts.append(Scatter(sizes, orders[k], small if k == n - 1 else terms[k], s, l, results[k], send.at[k], recv.at[k]))
    greet(sizes)
    for part in parts:
        part.start(0)
    for phase in range(4):
        for part in parts:
            part.finish(phase)
            if phase < 3:
                part.start(phase + 1)


def scatter_all(sizes, arrays, orders, gain_first, gain_second, table):
    arrays = [a.reshape(sizes + (a.shape[0] // int(np.prod(sizes)), a.shape[1])) for a in arrays]
    blocks = [a.shape[4:] for a in arrays] + [(16, 128)]
    types = [a.dtype for a in arrays] + [F32]
    n = len(blocks)
    plan = [Scatter.shapes(sizes, orders[k], blocks[k]) for k in range(n)]
    scratch = [pltpu.VMEM(sizes + (16, 128), F32)]
    for k in range(n):
        scratch += [pltpu.VMEM(s, types[k]) for s in plan[k][0] + plan[k][1]]
    scratch += [pltpu.SemaphoreType.DMA((n, 4, max(sizes)))] * 2
    vm = pl.BlockSpec(memory_space=pltpu.VMEM)
    return pl.pallas_call(
        functools.partial(scatter_kernel, sizes, orders, plan),
        in_specs=[vm] * (n + 2),
        out_specs=[vm] * n,
        out_shape=[jax.ShapeDtypeStruct(b, F32) for b in blocks],
        scratch_shapes=scratch,
        compiler_params=cp(collective_id=2, has_side_effects=True),
    )(*arrays, gain_first, gain_second, table)


def on_device(devices, inputs, valid_len, norm_first, w_qkv, w_out, relative_bucket_table, norm_second, w_up, w_down, output_gradient):
    S, L, D = inputs.shape
    R = S * L
    owned_rows = D // devices
    fast = devices == 32 and owned_rows == 16
    if fast:
        sizes = device_grid(devices)
        gains = jnp.zeros((16, 128), BF).at[0, :16].set(norm_first).at[1, :16].set(norm_second)
        got = gather_all(sizes, [w_qkv, gains, w_out, w_up, w_down], GATHER_ORDERS)
        wq, wo, wu, wd = [a.reshape(-1, a.shape[-1]) for a in (got[0], got[2], got[3], got[4])]
        both = got[1].reshape(devices, 16, 128)
        g1, g2 = both[:, 0, :16].reshape(1, D), both[:, 1, :16].reshape(1, D)
    else:
        g1, wq, wo, g2, wu, wd = [
            lax.all_gather(a, "dp", axis=0, tiled=True) for a in (norm_first, w_qkv, w_out, norm_second, w_up, w_down)
        ]
        g1, g2 = g1.reshape(1, D), g2.reshape(1, D)
    x = inputs.reshape(R, D)
    og = output_gradient.reshape(R, D)
    n1, qkv = qkv_fwd(x, g1, wq)
    qkv = qkv.reshape(S, L, 3 * D)
    mixed, qa = attn_fwd(valid_len, relative_bucket_table, qkv)
    out, ga, gm, gwo, gwu, gwd, gg2 = ffn(x, mixed.reshape(R, D), og, g2, wo, wu, wd)
    dq, dk, dv, tab = attn_bwd(valid_len, relative_bucket_table, qa, qkv, mixed, gm.reshape(S, L, D))
    gi, gwq, gg1 = qkv_bwd(x, n1, dq.reshape(R, D), dk.reshape(R, D), dv.reshape(R, D), ga, g1, wq)
    if fast:
        rq, ro, ru, rd, small = scatter_all(sizes, [gwq, gwo, gwu, gwd], SCATTER_ORDERS, gg1, gg2, tab)
        first = 16 * lax.rem(lax.axis_index("dp"), 8)
        r1 = lax.dynamic_slice(small[0], (first,), (16,))
        r2 = lax.dynamic_slice(small[1], (first,), (16,))
        rt = small[8:16, :16]
    else:
        rq, ro, ru, rd, r1, r2 = [
            lax.psum_scatter(a.astype(F32), "dp", scatter_dimension=0, tiled=True) for a in (gwq, gwo, gwu, gwd, gg1[0], gg2[0])
        ]
        rt = lax.psum(tab[:, :2, :16].reshape(relative_bucket_table.shape), "dp")
    return (out.reshape(S, L, D), gi.reshape(S, L, D), r1, rq, ro, rt, r2, ru, rd)


GATHER_ORDERS = ((0, 1, 2, 3), (0, 1, 2, 3), (0, 2, 1, 3), (0, 1, 2, 3), (0, 2, 1, 3))
SCATTER_ORDERS = ((3, 2, 1, 0), (3, 1, 2, 0), (3, 2, 1, 0), (3, 1, 2, 0), (3, 2, 1, 0))


def solution(mesh):
    placed = (
        P("dp", None, None), P("dp"), P("dp"), P("dp", None), P("dp", None), P(), P("dp"), P("dp", None), P("dp", None),
        P("dp", None, None),
    )
    return jax.shard_map(
        functools.partial(on_device, mesh.shape["dp"]),
        mesh=mesh,
        in_specs=placed,
        out_specs=(
            P("dp", None, None), P("dp", None, None), P("dp"), P("dp", None), P("dp", None), P(), P("dp"), P("dp", None),
            P("dp", None),
        ),
        check_vma=False,
    )
```

time: 1210 us -> 270 us (0.22)
  matrix products: 400 us -> 0 us
  waiting for transfers between devices: 284 us -> 0 us
  Pallas kernels: 0 us -> 255 us
  local copies, waits for them, and re-layouts: 256 us -> 13 us
  blocking collectives: 124 us -> 0 us
  other arithmetic: 118 us -> 1.28 us
  between operations: 14.8 us -> 0.69 us
    dot_general x48 -> x0, matrix products: 400 us -> none  [the longest x8 120 us: block_scores(): jnp.einsum('qhd,khd->hqk', block_queries, seq_keys, preferred_element_typ...]
    reduce_scatter x4 -> x0, waiting for transfers between devices: 281 us -> none  [the longest x1 142 us: on_device(): lax.psum_scatter(down_weight_gradient, 'dp', scatter_dimension=0, tiled=T...]
    pallas_call x0 -> x7, Pallas kernels: none -> 255 us  [the longest x1 55.2 us: gather_all(): pl.pallas_call(functools.partial(gather_kernel, sizes, orders), in_specs=...]
    while x96 -> x0, local copies, waits for them, and re-layouts: 102 us -> none
    unnamed x2 -> x0, blocking collectives: 79.2 us -> none
    convert_element_type x7 -> x0, local copies, waits for them, and re-layouts: 68.9 us -> none  [the longest x4 50.6 us: one_sequence(): (probabilities * (prob_grads - row_dot)).astype(jnp.bfloat16)]
    convert_element_type x8 -> x0, other arithmetic: 53.6 us -> none  [the longest x4 46 us: one_sequence(): (probabilities * (prob_grads - row_dot)).astype(jnp.bfloat16)]
    reduce_sum x11 -> x0, other arithmetic: 48.8 us -> none  [the longest x4 31.4 us: one_sequence(): row_total = jnp.sum(weights, axis=-1, keepdims=True)]
  transfers between devices with their start and end apart: 7 -> 0, of which waited for: 2 -> 0; matrix products, arithmetic and copies ran while one was open for 58% -> 0% of each run, Pallas kernels for 0% -> 0%
where the time goes in v1:
time: 270 us
  Pallas kernels  255 us (94%)
  local copies, waits for them, and re-layouts  13 us (5%)
    pallas_call x1, Pallas kernels, gather_all(): pl.pallas_call(functools.partial(gather_kernel, sizes, orders), in_specs=...  55.2 us
    pallas_call x1, Pallas kernels, scatter_all(): pl.pallas_call(functools.partial(scatter_kernel, sizes, orders, plan), in...  53 us
    pallas_call x1, Pallas kernels, ffn(): pl.pallas_call(ffn_kernel, grid=(R // B,), in_specs=[row, row, row, full(...  47.5 us
    pallas_call x1, Pallas kernels, attn_bwd(): pl.pallas_call(functools.partial(bwd_kernel, mode), grid=(HP, S), in_spec...  43 us
    pallas_call x1, Pallas kernels, attn_fwd(): pl.pallas_call(fwd_kernel, grid=(HP, S), in_specs=[pl.BlockSpec(memory_sp...  33.8 us
    pallas_call x1, Pallas kernels, qkv_bwd(): pl.pallas_call(qkvb_kernel, grid=(R // B,), in_specs=[row] * 6 + [full(1,...  14.4 us
    pallas_call x1, Pallas kernels, qkv_fwd(): pl.pallas_call(qkv_kernel, grid=(R // B,), in_specs=[pl.BlockSpec((B, D),...  8.08 us
    unnamed x6, local copies, waits for them, and re-layouts  6.63 us

profile of v1, /device:TPU:0, one launch (start us, length us, event | category | flops | bytes accessed | tf_op | source)
XLA Modules:
  0.0 269.9 jit_solution(14937093942184819368)
XLA Ops:
  0.6 1.3 convert.1.table_ref
  1.9 0.7 scatter.6
  2.6 0.8 scatter.9.refs_1_
  3.4 0.0 copy-start
  3.4 0.6 copy-done
  3.9 55.2 %shard_map.169 = (bf16[4,2,2,2,16,1536]{5,4,3,2,1,0:T(8,128)(2,1)}, bf16[4,2,2,2,16,128]{5,4,3,2,1,0:T(8,128)(2,1)}, bf16[4,2,2,2,16,512]{5,4,3,2,1,0:T(8,128)(2...) custom-call(bf16[16,1536]{1,0:T(8,128)(2,1)} %refs_0_.1, bf16[16,128]{1,0:T(8,128)(2,1)} %copy-done, ...), custom_call_target="tpu_custom_call" | custom-call | tf_op jit(solution)/shard_map/pallas_call | solution.py:470
  59.2 1.0 slice_reduce_fusion
  60.2 0.7 reshape_squeeze.6.g_ref
  60.8 8.1 %shard_map.170 = (bf16[2048,512]{1,0:T(8,128)(2,1)}, bf16[2048,1536]{1,0:T(8,128)(2,1)}) custom-call(bf16[2048,512]{1,0:T(8,128)(2,1)} %bitcast.32, bf16[1,512]{1,0:T(2,128)(2,1)} %reshape_squeeze.6.g_ref, bf16[512,1536]{1,0:T(8,128)(2,1)} %bitcast.36), custom_call_target="tpu_custom_call" | custom-call | tf_op jit(solution)/shard_map/pallas_call | solution.py:371
  68.9 33.8 %shard_map.171 = (bf16[2,1024,512]{2,1,0:T(8,128)(2,1)}, bf16[2,4,2,1024,128]{4,3,2,1,0:T(8,128)(2,1)}) custom-call(s32[2]{0:T(128)} %vl_ref.3, f32[4,2,16]{2,1,0:T(2,128)} %convert.1.table_ref, bf16[2,1024,1536]{2,1,0:T(8,128)(2,1)} %bitcast.27, bf16[2,1024,1536]{2,1,0:T(8,128)(2,1)} %bitcast.28, bf16[2,1024,1536]{2,1,0:T(8,128)(2,1)} %bitcast.29), custom_call_target="tpu_custom_call" | custom-call | tf_op jit(solution)/shard_map/pallas_call | solution.py:258
  102.7 0.7 reshape_squeeze.7.g_ref
  103.4 47.5 %shard_map.172 = (bf16[2048,512]{1,0:T(8,128)(2,1)}, f32[2048,512]{1,0:T(8,128)}, bf16[2048,512]{1,0:T(8,128)(2,1)}, bf16[512,512]{1,0:T(8,128)(2,1)}, bf16[512,...) custom-call(bf16[2048,512]{1,0:T(8,128)(2,1)} %bitcast.33, bf16[2048,512]{1,0:T(8,128)(2,1)} %bitcast.35, ...), custom_call_target="tpu_custom_call" | custom-call | tf_op jit(solution)/shard_map/pallas_call | solution.py:414
  150.8 43.0 %shard_map.173 = (bf16[2,1024,512]{2,1,0:T(8,128)(2,1)}, bf16[2,1024,512]{2,1,0:T(8,128)(2,1)}, bf16[2,1024,512]{2,1,0:T(8,128)(2,1)}, f32[4,8,128]{2,1,0:T(8,128)}) custom-call(s32[2]{0:T(128)} %vl_ref.3, f32[4,2,16]{2,1,0:T(2,128)} %convert.1.table_ref, bf16[2,4,2,1024,128]{4,3,2,1,0:T(8,128)(2,1)} %get-tuple-element.70.qa_ref, ...), custom_call_target="tpu_custom_call" | custom-call | tf_op jit(solution)/shard_map/pallas_call | solution.py:345
  193.8 14.4 %shard_map.174 = (bf16[2048,512]{1,0:T(8,128)(2,1)}, bf16[512,1536]{1,0:T(8,128)(2,1)}, f32[1,512]{1,0:T(1,128)}) custom-call(bf16[2048,512]{1,0:T(8,128)(2,1)} %bitcast.34, bf16[2048,512]{1,0:T(8,128)(2,1)} %get-tuple-element.69.n_ref, bf16[2048,512]{1,0:T(8,128)(2,1)} %bitcast.39, bf16[2048,512]{1,0:T(8,128)(2,1)} %bitcast.40, bf16[2048,512]{1,0:T(8,128)(2,1)} %bitcast.41, ...), custom_call_target="tpu_custom_call" | custom-call | tf_op jit(solution)/shard_map/pallas_call | solution.py:445
  208.2 53.0 %shard_map.175 = (f32[16,1536]{1,0:T(8,128)}, f32[16,512]{1,0:T(8,128)}, f32[16,2048]{1,0:T(8,128)}, f32[64,512]{1,0:T(8,128)}, f32[16,128]{1,0:T(8,128)}) custom-call(bf16[4,2,2,2,16,1536]{5,4,3,2,1,0:T(8,128)(2,1)} %bitcast.47, bf16[4,2,2,2,16,512]{5,4,3,2,1,0:T(8,128)(2,1)} %bitcast.49, bf16[4,2,2,2,16,2048]{5,4,3,2,1,0:T(8,128)(2,1)} %bitcast.43, ...), custom_call_target="tpu_custom_call" | custom-call | tf_op jit(solution)/shard_map/pallas_call | solution.py:527
  261.2 0.8 fusion
  262.0 0.6 dynamic-slice_bitcast_fusion
  262.6 1.3 slice.53
  263.8 1.5 copy.30
  265.4 1.4 copy.31
  266.8 1.6 copy.32
  268.3 1.6 copy.33
Async XLA Ops:
  3.4 0.6 copy-start

commit v2 on v1

v2 whole, which is shorter than its diff:
```python
import functools
import itertools

import jax
import jax.numpy as jnp
import numpy as np
from jax import lax
from jax.experimental import pallas as pl
from jax.experimental.pallas import tpu as pltpu
from jax.sharding import PartitionSpec as P

MESH = pl.DeviceIdType.MESH
F32 = jnp.float32
BF = jnp.bfloat16
EPS = 1e-05


def device_grid(devices):
    return (devices // 8, 2, 2, 2)


def grid_position(sizes):
    rest = lax.axis_index("dp")
    place = []
    for size in reversed(sizes):
        place.append(lax.rem(rest, size))
        rest = lax.div(rest, size)
    return tuple(reversed(place))


def flat(place, sizes):
    index = place[0]
    for one, size in zip(place[1:], sizes[1:]):
        index = index * size + one
    return index


def moves(sizes, group):
    return [m for m in itertools.product(*[range(sizes[a]) for a in group]) if any(m)]


def moved(place, sizes, group, move):
    other = list(place)
    for axis, step in zip(group, move):
        if step:
            other[axis] = lax.rem(place[axis] + step, sizes[axis])
    return tuple(other)


def greet(sizes, groups):
    place = grid_position(sizes)
    barrier = pltpu.get_barrier_semaphore()
    count = 0
    for group in groups:
        for move in moves(sizes, group):
            pl.semaphore_signal(
                barrier,
                inc=1,
                device_id=(flat(moved(place, sizes, group, move), sizes),),
                device_id_type=MESH,
            )
            count += 1
    pl.semaphore_wait(barrier, count)


class Gather:
    def __init__(self, sizes, order, own, whole, local_sem, send_sems, recv_sems):
        self.sizes, self.order = sizes, order
        self.own, self.whole = own, whole
        self.local_sem, self.send_sems, self.recv_sems = local_sem, send_sems, recv_sems

    def copies(self, phase):
        place = grid_position(self.sizes)
        done = [a for group in self.order[:phase] for a in group]
        group = self.order[phase]
        part = self.whole.at[tuple(slice(None) if a in done else place[a] for a in range(4))]
        return [
            pltpu.make_async_remote_copy(
                src_ref=self.own if phase == 0 else part,
                dst_ref=part,
                send_sem=self.send_sems.at[phase, k],
                recv_sem=self.recv_sems.at[phase, k],
                device_id=(flat(moved(place, self.sizes, group, move), self.sizes),),
                device_id_type=MESH,
            )
            for k, move in enumerate(moves(self.sizes, group))
        ]

    def local(self):
        return pltpu.make_async_copy(self.own, self.whole.at[grid_position(self.sizes)], self.local_sem)

    def start(self, phase):
        if phase == 0:
            self.local().start()
        for copy in self.copies(phase):
            copy.start()

    def finish(self, phase):
        if phase == 0:
            self.local().wait()
        for copy in self.copies(phase):
            copy.wait()


class Scatter:
    def __init__(self, sizes, order, terms, sums, landing, result, send_sems, recv_sems):
        self.sizes, self.order = sizes, order
        self.held = [terms] + list(sums)
        self.landing, self.result = landing, result
        self.send_sems, self.recv_sems = send_sems, recv_sems

    @staticmethod
    def shapes(sizes, order, block):
        left, sums, landing = set(range(4)), [], []
        for phase, group in enumerate(order):
            left -= set(group)
            lead = tuple(sizes[a] for a in sorted(left))
            slots = int(np.prod([sizes[a] for a in group]))
            landing.append((slots if slots > 2 else 1,) + lead + block)
            if phase < len(order) - 1:
                sums.append(lead + block)
        return sums, landing

    def before(self, phase):
        done = [a for group in self.order[:phase] for a in group]
        return [a for a in range(4) if a not in done]

    def slot(self, phase, place):
        group = self.order[phase]
        if self.landing[phase].shape[0] == 1:
            return 0
        return flat([place[a] for a in group], [self.sizes[a] for a in group])

    def copies(self, phase):
        place = grid_position(self.sizes)
        group = self.order[phase]
        out = []
        for k, move in enumerate(moves(self.sizes, group)):
            other = moved(place, self.sizes, group, move)
            part = tuple(other[a] if a in group else slice(None) for a in self.before(phase))
            out.append(
                pltpu.make_async_remote_copy(
                    src_ref=self.held[phase].at[part],
                    dst_ref=self.landing[phase].at[self.slot(phase, place)],
                    send_sem=self.send_sems.at[phase, k],
                    recv_sem=self.recv_sems.at[phase, k],
                    device_id=(flat(other, self.sizes),),
                    device_id_type=MESH,
                )
            )
        return out

    def start(self, phase):
        for copy in self.copies(phase):
            copy.start()

    def finish(self, phase):
        for copy in self.copies(phase):
            copy.wait()
        place = grid_position(self.sizes)
        group = self.order[phase]
        held, landed = self.held[phase], self.landing[phase]
        before = self.before(phase)
        left = [a for a in before if a not in group]
        last = phase == len(self.order) - 1
        target = self.result if last else self.held[phase + 1]

        def one(at):
            spot = dict(zip(left, at))
            mine = held[tuple(place[a] if a in group else spot[a] for a in before)]
            at = tuple(at)
            if landed.shape[0] == 1:
                total = mine.astype(F32) + landed[(0,) + at].astype(F32)
            else:
                landed[(self.slot(phase, place),) + at] = mine
                total = landed[(0,) + at].astype(F32)
                for source in range(1, landed.shape[0]):
                    total = total + landed[(source,) + at].astype(F32)
            if at:
                target[at] = total.astype(target.dtype)
            else:
                target[...] = total.astype(target.dtype)

        if not left:
            one(())
        else:
            lead = [self.sizes[a] for a in left]

            def body(count, unused):
                at = []
                for size in reversed(lead):
                    at.append(lax.rem(count, size))
                    count = lax.div(count, size)
                one(at[::-1])
                return unused

            lax.fori_loop(0, int(np.prod(lead)), body, 0)


def semaphores(items):
    return [pltpu.SemaphoreType.DMA((items, 4, 16)), pltpu.SemaphoreType.DMA((items, 4, 16))]


def run_schedule(step, schedule, parts):
    for at, actions in sorted(schedule.items()):

        @pl.when(step == at)
        def _(actions=actions):
            for action, item, phase in actions:
                getattr(parts[item], action)(phase)


LOW=(0,1,2,3,4,5,6,7,8,12,16,32,64,128,256,512)
T=256
NEG=-1e30
def cp(**k): return pltpu.CompilerParams(vmem_limit_bytes=56*2**20, **k)
def dot_nt(a,b): return lax.dot_general(a,b,(((1,),(1,)),((),())),preferred_element_type=jnp.float32)
def dot_nn(a,b): return jnp.dot(a,b,preferred_element_type=jnp.float32)
def dot_tn(a,b): return lax.dot_general(a,b,(((0,),(0,)),((),())),preferred_element_type=jnp.float32)

def bias_of(dist, row):
    out=jnp.zeros(dist.shape,jnp.float32)+row[:,0:1]
    for b in range(1,16):
        out=jnp.where(dist>=LOW[b],row[:,b:b+1],out)
    return jnp.where(dist<0,NEG,out)

def table_row(table_ref,head):
    whole=table_ref[...].astype(jnp.float32)
    at=lax.broadcasted_iota(jnp.int32,whole.shape,0)
    return jnp.sum(jnp.where(at==head,whole,0.0),axis=0,keepdims=True)

def build_bias(table_ref, hp, bias, transposed):
    lane=lax.broadcasted_iota(jnp.int32,(1,2*T),1)
    m=jnp.where(lane<T,lane,lane-2*T)
    for h in range(2):
        row=table_row(table_ref,2*hp+h)
        for bd in range(3):
            w=bias_of(bd*T+(m if transposed else -m),row)
            tile=pltpu.roll(jnp.broadcast_to(w,(T,2*T)),0,1,stride=1,stride_axis=0)
            bias[h,bd]=tile[:,:T]
        bias[h,3]=jnp.broadcast_to(row[:,15:16],(T,T))

def split3(v):
    hi=v.astype(jnp.bfloat16); r=v-hi.astype(jnp.float32)
    mid=r.astype(jnp.bfloat16); lo=(r-mid.astype(jnp.float32)).astype(jnp.bfloat16)
    return hi,mid,lo

def halves(h, main, extra, rows):
    lane=lax.broadcasted_iota(jnp.int32,(rows,128),1)
    out=jnp.where((lane//64)==h,main,jnp.zeros((),main.dtype))
    base=64*(1-h)
    for n,e in enumerate(extra):
        if e is not None:
            out=jnp.where(lane==base+n,jnp.broadcast_to(e,(rows,128)).astype(jnp.bfloat16),out)
    return out

def ln_parts(v):
    c=v-jnp.mean(v,axis=1,keepdims=True)
    r=lax.rsqrt(jnp.mean(c*c,axis=1,keepdims=True)+EPS)
    return c*r, r
def ln_back(e_in,gain,xhat,r):
    e=e_in*gain
    gv=r*(e-jnp.mean(e,axis=1,keepdims=True)-xhat*jnp.mean(e*xhat,axis=1,keepdims=True))
    return (gv,)

def ffn_kernel(x_ref,m_ref,og_ref,g_ref,wo_ref,wu_ref,wd_ref,out_ref,ga_ref,gm_ref,gwo_ref,gwu_ref,gwd_ref,ao,au,ad):
    i=pl.program_id(0)
    m=m_ref[...]; og=og_ref[...]
    after=x_ref[...].astype(F32)+dot_nn(m,wo_ref[...])
    xhat,r=ln_parts(after)
    gain=g_ref[...].astype(F32)
    n=(xhat*gain).astype(BF)
    pre=dot_nn(n,wu_ref[...])
    dh=dot_nt(og,wd_ref[...])
    c=0.7978845608028654
    sq=pre*pre
    t=jnp.tanh(pre*(c+c*0.044715*sq))
    half=0.5*(1.0+t)
    hid=(pre*half).astype(BF)
    dg=half+(0.5*pre)*(1.0-t*t)*(c+3*c*0.044715*sq)
    gp=(dh*dg).astype(BF)
    out_ref[...]=(after+dot_nn(hid,wd_ref[...])).astype(BF)
    pd=dot_tn(hid,og); pu=dot_tn(n,gp)
    dn=dot_nt(gp,wu_ref[...])
    (gv,)=ln_back(dn,gain,xhat,r)
    ga=og.astype(F32)+gv
    ga_ref[...]=ga
    gb=ga.astype(BF)
    po=dot_tn(m,gb)
    gm_ref[...]=dot_nt(gb,wo_ref[...]).astype(BF)
    @pl.when(i==0)
    def _():
        ad[...]=pd; au[...]=pu; ao[...]=po
    @pl.when(i>0)
    def _():
        ad[...]+=pd; au[...]+=pu; ao[...]+=po
    @pl.when(i==pl.num_programs(0)-1)
    def _():
        gwo_ref[...]=ao[...].astype(BF); gwu_ref[...]=au[...].astype(BF); gwd_ref[...]=ad[...].astype(BF)
def ffn(x,m,og,gain,wo,wu,wd,B=512):
    R,D=x.shape; FF=wu.shape[1]
    row=pl.BlockSpec((B,D),lambda i:(i,0))
    full=lambda a,b:pl.BlockSpec((a,b),lambda i:(0,0))
    return pl.pallas_call(ffn_kernel,grid=(R//B,),
      in_specs=[row,row,row,full(1,D),full(D,D),full(D,FF),full(FF,D)],
      out_specs=[row,row,row,full(D,D),full(D,FF),full(FF,D)],
      out_shape=[jax.ShapeDtypeStruct((R,D),BF),jax.ShapeDtypeStruct((R,D),F32),jax.ShapeDtypeStruct((R,D),BF),
        jax.ShapeDtypeStruct((D,D),BF),jax.ShapeDtypeStruct((D,FF),BF),jax.ShapeDtypeStruct((FF,D),BF)],
      scratch_shapes=[pltpu.VMEM((D,D),F32),pltpu.VMEM((D,FF),F32),pltpu.VMEM((FF,D),F32)],
      compiler_params=cp())(x,m,og,gain,wo,wu,wd)


SPREAD = ((0, 1, 2), (3,))
GATHER_ORDERS = {
    "gains": SPREAD, "q0": SPREAD, "q1": SPREAD,
    "q2": ((0,), (1,), (2,), (3,)), "q3": ((0,), (2,), (1,), (3,)),
    "out": ((0,), (1,), (2,), (3,)), "up": ((0,), (1,), (2,), (3,)), "down": ((0,), (2,), (1,), (3,)),
}
GATHER_SCHEDULE = {
    1: [("finish", "q1", 0), ("start", "q1", 1), ("finish", "q2", 0), ("start", "q2", 1), ("finish", "up", 0), ("start", "up", 1), ("start", "out", 0)],
    2: [("finish", "q1", 1), ("finish", "q2", 1), ("start", "q2", 2), ("finish", "down", 0), ("start", "down", 1), ("start", "q3", 0), ("finish", "up", 1), ("start", "up", 2)],
    3: [("finish", "q2", 2), ("start", "q2", 3), ("finish", "out", 0), ("start", "out", 1), ("finish", "q3", 0), ("start", "q3", 1), ("finish", "down", 1), ("start", "down", 2)],
    4: [("finish", "q2", 3), ("finish", "q3", 1), ("start", "q3", 2), ("finish", "out", 1), ("start", "out", 2)],
    5: [("finish", "q3", 2), ("start", "q3", 3), ("finish", "up", 2), ("start", "up", 3), ("finish", "out", 2), ("start", "out", 3)],
    6: [("finish", "q3", 3), ("finish", "down", 2), ("start", "down", 3)],
    7: [("finish", "up", 3), ("finish", "out", 3)],
}


def first_kernel(sizes, *refs):
    remote = sizes is not None
    refs = list(refs)
    take = lambda count: [refs.pop(0) for _ in range(count)]
    vl_ref, table_ref, x_ref = take(3)
    if remote:
        gains_own, wq_own, wo_own, wu_own, wd_own = take(5)
    else:
        g_ref, w_ref = take(2)
    mixed_ref, qa_ref, qkv_ref, n_ref = take(4)
    if remote:
        g1_ref, g2_ref, wq_out, wo_ref, wu_ref, wd_ref = take(6)
    bias, xhat = take(2)
    hp = pl.program_id(0)
    s = pl.program_id(1)
    pairs = pl.num_programs(0)
    S, L = qkv_ref.shape[1:3]
    step = hp * S + s
    R, D = x_ref.shape
    B = 512
    if remote:
        q_own, wq, gains, local, send, recv, out_sem = take(7)
        names = list(GATHER_ORDERS)
        own = dict(gains=gains_own, out=wo_own, up=wu_own, down=wd_own)
        whole = dict(gains=gains, out=wo_ref, up=wu_ref, down=wd_ref)
        for pair in range(4):
            own["q%d" % pair], whole["q%d" % pair] = q_own.at[pair], wq.at[pair]
        parts = {
            name: Gather(sizes, GATHER_ORDERS[name], own[name], whole[name], local.at[k], send.at[k], recv.at[k])
            for k, name in enumerate(names)
        }
        out_copy = lambda pair: pltpu.make_async_copy(wq.at[pair], wq_out.at[pair], out_sem.at[pair])

    @pl.when(step == 0)
    def _():
        if remote:
            for pair in range(4):
                for part in range(3):
                    q_own[pair, :, part * 128:(part + 1) * 128] = wq_own[:, (part * 4 + pair) * 128:(part * 4 + pair + 1) * 128]
            greet(sizes, SPREAD)
            parts["q0"].start(0)
            parts["gains"].start(0)

        def norm(block, unused):
            at = pl.ds(pl.multiple_of(block * B, B), B)
            xhat[at, :] = ln_parts(x_ref[at, :].astype(F32))[0]
            return unused

        lax.fori_loop(0, R // B, norm, 0)
        if remote:
            parts["gains"].finish(0)
            parts["q0"].finish(0)
            parts["gains"].start(1)
            parts["q0"].start(1)
            parts["q1"].start(0)
            parts["q2"].start(0)
            parts["up"].start(0)
            parts["down"].start(0)
            parts["gains"].finish(1)
            tiles = []
            for z in range(sizes[0]):
                tile = jnp.zeros((16, 128), F32)
                for y, a, c in itertools.product(*[range(size) for size in sizes[1:]]):
                    tile = tile + gains[z, y, a, c].astype(F32)
                tiles.append(tile)
            tile = jnp.concatenate(tiles, axis=1)
            g1_ref[...] = tile[0:1, :]
            g2_ref[...] = tile[1:2, :]
            gain = tile[0:1, :]
        else:
            gain = g_ref[...]

        def scale(block, unused):
            at = pl.ds(pl.multiple_of(block * B, B), B)
            n_ref[at, :] = (xhat[at, :] * gain).astype(BF)
            return unused

        lax.fori_loop(0, R // B, scale, 0)
        if remote:
            parts["q0"].finish(1)

    if remote:
        run_schedule(step, GATHER_SCHEDULE, parts)

    @pl.when(s == 0)
    def _():
        build_bias(table_ref, hp, bias, False)
        weights = wq[hp].reshape(D, 384) if remote else w_ref[0]
        if remote:
            out_copy(hp).start()
        for seq in range(S):
            for half in range(L // B):
                row = seq * L + half * B
                qkv_ref[0, seq, half * B:(half + 1) * B, :] = dot_nn(n_ref[row:row + B, :], weights).astype(BF)

    attend(vl_ref[s], qkv_ref.at[0, s], mixed_ref.at[0], qa_ref.at[0, 0], bias)

    if remote:

        @pl.when(step == pairs * S - 1)
        def _():
            parts["down"].finish(3)
            for pair in range(4):
                out_copy(pair).wait()


def attend(valid, qkv_ref, mixed_ref, qa_ref, bias):
    L = qkv_ref.shape[0]
    nb = L // T
    key = lax.broadcasted_iota(jnp.int32, (L, 1), 0)
    mask = jnp.where(key < valid, 0.0, NEG)
    lane = lax.broadcasted_iota(jnp.int32, (T, 128), 1)
    ks = [halves(h, qkv_ref[:, 128:256], [1.0, 1.0, 1.0, mask], L) for h in range(2)]
    v = qkv_ref[:, 256:384]
    for qb in range(nb):
        kk = (qb + 1) * T
        qt = qkv_ref[qb * T:(qb + 1) * T, 0:128] * jnp.asarray(0.125, BF)
        outs = []
        for h in range(2):
            qh = halves(h, qt, [None, None, None, 1.0], T)
            sc = dot_nt(qh, ks[h][:kk])
            sc = jnp.concatenate([sc[:, kb * T:(kb + 1) * T] + bias[h, qb - kb] for kb in range(qb + 1)], axis=1)
            mx = jnp.max(sc, axis=1, keepdims=True)
            p = jnp.exp(sc - mx)
            l = jnp.sum(p, axis=1, keepdims=True)
            o = dot_nn(p.astype(BF), v[:kk])
            outs.append(o * (1.0 / l))
            hi, mid, lo = split3(-(mx + jnp.log(l)))
            qa_ref[h, qb * T:(qb + 1) * T, :] = halves(h, qt, [hi, mid, lo, 1.0], T)
        mixed_ref[qb * T:(qb + 1) * T, :] = jnp.where(lane < 64, outs[0], outs[1]).astype(BF)


def whole_block(shape):
    return pl.BlockSpec(shape, lambda *unused: (0,) * len(shape))


def first_half(sizes, vl, table, x, S, weights):
    R, D = x.shape
    L = R // S
    HP = D // 128
    remote = sizes is not None
    anyspace = pl.BlockSpec(memory_space=pl.ANY)
    in_specs = [pl.BlockSpec(memory_space=pltpu.SMEM), whole_block(table.shape), whole_block((R, D))]
    out_specs = [
        pl.BlockSpec((1, L, 128), lambda h, s: (s, 0, h)),
        pl.BlockSpec((1, 1, 2, L, 128), lambda h, s: (s, h, 0, 0, 0)),
        pl.BlockSpec((1, S, L, 384), lambda h, s: (h, 0, 0, 0)),
        whole_block((R, D)),
    ]
    out_shape = [
        jax.ShapeDtypeStruct((S, L, D), BF),
        jax.ShapeDtypeStruct((S, HP, 2, L, 128), BF),
        jax.ShapeDtypeStruct((HP, S, L, 384), BF),
        jax.ShapeDtypeStruct((R, D), BF),
    ]
    scratch = [pltpu.VMEM((2, 4, T, T), F32), pltpu.VMEM((R, D), F32)]
    if remote:
        gains, wq, wo, wu, wd = weights
        in_specs += [whole_block(gains.shape), whole_block(wq.shape), anyspace, anyspace, anyspace]
        out_specs += [whole_block((1, D)), whole_block((1, D))] + [anyspace] * 4
        out_shape += [jax.ShapeDtypeStruct((1, D), F32)] * 2
        out_shape += [jax.ShapeDtypeStruct((HP,) + sizes + (16, 384), BF)]
        out_shape += [jax.ShapeDtypeStruct(sizes + w.shape, BF) for w in (wo, wu, wd)]
        scratch += [
            pltpu.VMEM((HP, 16, 384), BF),
            pltpu.VMEM((HP,) + sizes + (16, 384), BF),
            pltpu.VMEM(sizes + (16, 128), BF),
            pltpu.SemaphoreType.DMA((len(GATHER_ORDERS),)),
        ] + semaphores(len(GATHER_ORDERS)) + [pltpu.SemaphoreType.DMA((HP,))]
        params = cp(collective_id=1, has_side_effects=True)
    else:
        gain, wq = weights
        in_specs += [whole_block((1, D)), pl.BlockSpec((1, D, 384), lambda h, s: (h, 0, 0))]
        params = cp()
    return pl.pallas_call(
        functools.partial(first_kernel, sizes), grid=(HP, S), in_specs=in_specs, out_specs=out_specs, out_shape=out_shape,
        scratch_shapes=scratch, compiler_params=params,
    )(vl, table, x, *weights)


SCATTER_ORDERS = {
    "out": ((3,), (2,), (1,), (0,)), "up": ((3,), (2,), (1,), (0,)), "down": ((3,), (1,), (2,), (0,)),
    "q0": ((3,), (1,), (2,), (0,)), "q1": ((3,), (2,), (1,), (0,)), "q2": ((3,), (1,), (2,), (0,)), "q3": ((3,), (0, 1, 2)),
}
SCATTER_SCHEDULE = {
    0: [("start", "up", 0), ("start", "down", 0), ("start", "out", 0)],
    1: [("finish", "up", 0), ("start", "up", 1), ("finish", "down", 0), ("start", "down", 1), ("finish", "out", 0), ("start", "out", 1)],
    2: [("start", "q0", 0)],
    3: [("finish", "q0", 0), ("start", "q0", 1), ("finish", "out", 1), ("start", "out", 2)],
    4: [("finish", "up", 1), ("start", "up", 2), ("finish", "down", 1), ("start", "down", 2), ("start", "q1", 0), ("finish", "out", 2), ("start", "out", 3)],
    5: [("finish", "q1", 0), ("start", "q1", 1), ("finish", "q0", 1), ("start", "q0", 2)],
    6: [("finish", "up", 2), ("start", "up", 3), ("finish", "down", 2), ("start", "down", 3), ("start", "q2", 0), ("finish", "out", 3)],
    7: [("finish", "q1", 1), ("start", "q1", 2), ("finish", "q2", 0), ("start", "q2", 1), ("finish", "q0", 2), ("start", "q0", 3)],
    8: [("start", "q3", 0), ("start", "table", 0), ("finish", "q2", 1), ("start", "q2", 2), ("finish", "q1", 2), ("start", "q1", 3)],
    9: [("finish", "q3", 0), ("start", "q3", 1), ("finish", "table", 0), ("start", "table", 1), ("finish", "up", 3), ("finish", "q0", 3)],
    10: [("finish", "q2", 2), ("start", "q2", 3), ("finish", "down", 3), ("finish", "table", 1)],
    11: [("finish", "q1", 3)],
}
SCATTER_TAIL = [("finish", "q2", 3), ("finish", "q3", 1)]


def last_kernel(sizes, plan, *refs):
    remote = sizes is not None
    refs = list(refs)
    take = lambda count: [refs.pop(0) for _ in range(count)]
    vl_ref, table_ref, qa_ref, qkv_ref, o_ref, g_ref, n_ref, w_ref, gain_ref, x_ref, ga_ref = take(11)
    if remote:
        wo_terms, wu_terms, wd_terms = take(3)
    gi_ref, tab_ref = take(2)
    if remote:
        results = dict(zip(SCATTER_ORDERS, take(7)))
    else:
        (gw_ref,) = take(1)
    bias, gacc, far, dqt, grads = take(5)
    t = pl.program_id(0)
    pairs = grads.shape[0]
    S = grads.shape[1] // qkv_ref.shape[2]
    steps = pairs * S
    hp = lax.div(t, S)
    s = lax.rem(t, S)
    L = qkv_ref.shape[2]
    R = S * L
    D = x_ref.shape[1]
    if remote:
        wq_terms, tab_own, tab_all, local = take(4)
        terms = dict(out=wo_terms, up=wu_terms, down=wd_terms)
        for pair in range(4):
            terms["q%d" % pair] = wq_terms.at[pair]
        send, recv = refs[-2:]
        parts = {}
        for k, name in enumerate(SCATTER_ORDERS):
            sums, landing = plan[name]
            parts[name] = Scatter(
                sizes, SCATTER_ORDERS[name], terms[name], take(len(sums)), take(len(landing)), results[name], send.at[k], recv.at[k]
            )
        parts["table"] = Gather(sizes, SPREAD, tab_own, tab_all, local, send.at[len(plan)], recv.at[len(plan)])

        @pl.when(t == 0)
        def _():
            greet(sizes, SPREAD)

        run_schedule(t, SCATTER_SCHEDULE, parts)

    @pl.when(t < steps)
    def _():
        @pl.when(s == 0)
        def _():
            build_bias(table_ref, hp, bias, True)
            gacc[...] = jnp.zeros_like(gacc)
            far[...] = jnp.zeros_like(far)

        at = pl.multiple_of(s * L, L)
        attend_back(vl_ref[s], qa_ref.at[0, 0], qkv_ref.at[0, 0], o_ref[0], g_ref[0], grads, hp, at, bias, gacc, far, dqt)

        @pl.when(s == S - 1)
        def _():
            rows = table_terms(gacc, far)
            place = pl.ds(pl.multiple_of(hp * 8, 8), 8)
            (tab_own if remote else tab_ref)[place, :] = rows
            for part in range(3):
                gw = dot_tn(n_ref[...], grads[hp, :, part * 128:(part + 1) * 128]).astype(BF)
                if remote:
                    wq_terms[hp, :, :, :, :, :, part * 128:(part + 1) * 128] = gw.reshape(sizes + (16, 128))
                else:
                    gw_ref[hp, :, part * 128:(part + 1) * 128] = gw

    @pl.when(t >= steps)
    def _():
        B = x_ref.shape[0]
        at = pl.ds(pl.multiple_of((t - steps) * B, B), B)
        xhat, r = ln_parts(x_ref[...].astype(F32))
        dn = None
        for pair in range(pairs):
            weights = w_ref[pair]
            term = dot_nt(grads[pair, at, :], weights)
            dn = term if dn is None else dn + term
        gi_ref[...] = (ga_ref[...] + ln_back(dn, gain_ref[...], xhat, r)[0]).astype(BF)

    if remote:

        @pl.when(t == pl.num_programs(0) - 1)
        def _():
            for action, item, phase in SCATTER_TAIL:
                getattr(parts[item], action)(phase)
            total = None
            for at in itertools.product(*[range(size) for size in sizes]):
                block = tab_all[at]
                total = block if total is None else total + block
            tab_ref[...] = total


def table_terms(gacc, far):
    lane2 = lax.broadcasted_iota(jnp.int32, (1, 2 * T), 1)
    m = jnp.where(lane2 < T, lane2, lane2 - 2 * T)
    bl = lax.broadcasted_iota(jnp.int32, (1, 128), 1)
    rows = []
    for h in range(2):
        row = jnp.where(bl == 15, jnp.sum(far[h:h + 1, :], axis=1, keepdims=True), 0.0)
        for bd in range(3):
            w = jnp.concatenate([gacc[h, bd], jnp.zeros((T, T), F32)], axis=1)
            acc = w[:8]
            for a in range(1, T // 8):
                acc = acc + pltpu.roll(w[8 * a:8 * a + 8], 2 * T - 8 * a, 1)
            diag = acc[0:1]
            for a in range(1, 8):
                diag = diag + pltpu.roll(acc[a:a + 1], 2 * T - a, 1)
            dist = bd * T + m
            for b in range(16):
                if LOW[b] >= (bd + 1) * T or (b < 15 and LOW[b + 1] <= (bd - 1) * T):
                    continue
                sel = dist >= LOW[b]
                if b < 15:
                    sel = sel & (dist < LOW[b + 1])
                row = row + jnp.where(bl == b, jnp.sum(jnp.where(sel, diag, 0.0), axis=1, keepdims=True), 0.0)
        rows.append(row)
    return jnp.concatenate(rows + [jnp.zeros((6, 128), F32)], axis=0)


def attend_back(valid, qa_ref, qkv_ref, o, g, grads, hp, first, bias, gacc, far, dqt):
    L = qkv_ref.shape[0]
    nb = L // T
    key = lax.broadcasted_iota(jnp.int32, (L, 1), 0)
    mask = jnp.where(key < valid, 0.0, NEG)
    lane = lax.broadcasted_iota(jnp.int32, (T, 128), 1)
    prod = g.astype(F32) * o.astype(F32)
    lane_l = lax.broadcasted_iota(jnp.int32, (L, 128), 1)
    k = qkv_ref[:, 128:256]
    ks = [halves(h, k, [1.0, 1.0, 1.0, mask], L) for h in range(2)]
    vs = [halves(h, qkv_ref[:, 256:384], [1.0, 1.0, 1.0], L) for h in range(2)]
    gs = []
    for h in range(2):
        d = jnp.sum(jnp.where((lane_l // 64) == h, prod, 0.0), axis=1, keepdims=True)
        hi, mid, lo = split3(-d)
        gs.append(halves(h, g, [hi, mid, lo], L))
    kt = (k * jnp.asarray(0.125, BF)).T
    for kb in range(nb):
        dks, dvs = [], []
        for h in range(2):
            qh = qa_ref[h]
            st = dot_nt(ks[h][kb * T:(kb + 1) * T], qh[kb * T:])
            dp = dot_nt(vs[h][kb * T:(kb + 1) * T], gs[h][kb * T:])
            st = jnp.concatenate([st[:, i * T:(i + 1) * T] + bias[h, i] for i in range(nb - kb)], axis=1)
            p = jnp.exp(st)
            ds = p * dp
            pb = p.astype(BF)
            dsb = ds.astype(BF)
            dvs.append(dot_nn(pb, gs[h][kb * T:]))
            dks.append(dot_nn(dsb, qh[kb * T:]))
            for i in range(min(nb - kb, 3)):
                gacc[h, i] += ds[:, i * T:(i + 1) * T]
            if nb - kb > 3:
                far[h:h + 1, :] += jnp.sum(ds[:, 3 * T:], axis=0, keepdims=True)
            r = dot_nn(kt[h * 64:(h + 1) * 64, kb * T:(kb + 1) * T], dsb)
            if kb == 0:
                dqt[h * 64:(h + 1) * 64, :] = r
            else:
                dqt[h * 64:(h + 1) * 64, kb * T:] += r
        at = pl.ds(first + kb * T, T)
        grads[hp, at, 128:256] = jnp.where(lane < 64, dks[0], dks[1]).astype(BF)
        grads[hp, at, 256:384] = jnp.where(lane < 64, dvs[0], dvs[1]).astype(BF)
    grads[hp, pl.ds(first, L), 0:128] = dqt[...].T.astype(BF)


def last_half(sizes, vl, table, qa, qkv, mixed, gm, n1, wq, gain, x, ga, ffn_grads):
    HP, S, L, W = qkv.shape
    R, D = x.shape
    B = 512
    steps = HP * S
    remote = sizes is not None
    pair = lambda t: jnp.minimum(t, steps - 1) // S
    seq = lambda t: jnp.minimum(t, steps - 1) % S
    late = pl.BlockSpec((B, D), lambda t: (jnp.maximum(t - steps, 0), 0))
    in_specs = [
        pl.BlockSpec(memory_space=pltpu.SMEM),
        whole_block(table.shape),
        pl.BlockSpec((1, 1, 2, L, 128), lambda t: (seq(t), pair(t), 0, 0, 0)),
        pl.BlockSpec((1, 1, L, W), lambda t: (pair(t), seq(t), 0, 0)),
        pl.BlockSpec((1, L, 128), lambda t: (seq(t), 0, pair(t))),
        pl.BlockSpec((1, L, 128), lambda t: (seq(t), 0, pair(t))),
        whole_block((R, D)),
        whole_block((HP, D, W)),
        whole_block((1, D)),
        late,
        late,
    ]
    out_specs = [late, whole_block((8 * HP, 128))]
    out_shape = [jax.ShapeDtypeStruct((R, D), BF), jax.ShapeDtypeStruct((8 * HP, 128), F32)]
    scratch = [
        pltpu.VMEM((2, 4, T, T), F32), pltpu.VMEM((2, 3, T, T), F32), pltpu.VMEM((8, T), F32), pltpu.VMEM((128, L), F32),
        pltpu.VMEM((HP, R, W), BF),
    ]
    args = [vl, table, qa, qkv, mixed, gm, n1, wq, gain, x, ga]
    plan = None
    if remote:
        count = int(np.prod(sizes))
        terms = [a.reshape(sizes + (a.shape[0] // count, a.shape[1])) for a in ffn_grads]
        args += terms
        in_specs += [whole_block(a.shape) for a in terms]
        blocks = dict(zip(("out", "up", "down"), [a.shape[4:] for a in terms]))
        for k in range(HP):
            blocks["q%d" % k] = (16, W)
        plan = {name: Scatter.shapes(sizes, SCATTER_ORDERS[name], blocks[name]) for name in SCATTER_ORDERS}
        out_specs += [whole_block(blocks[name]) for name in SCATTER_ORDERS]
        out_shape += [jax.ShapeDtypeStruct(blocks[name], F32) for name in SCATTER_ORDERS]
        scratch += [
            pltpu.VMEM((HP,) + sizes + (16, W), BF), pltpu.VMEM((8 * HP, 128), F32), pltpu.VMEM(sizes + (8 * HP, 128), F32),
            pltpu.SemaphoreType.DMA,
        ]
        for name in SCATTER_ORDERS:
            scratch += [pltpu.VMEM(shape, BF) for shape in plan[name][0] + plan[name][1]]
        scratch += semaphores(len(SCATTER_ORDERS) + 1)
        params = cp(collective_id=2, has_side_effects=True)
    else:
        out_specs += [whole_block((HP, D, W))]
        out_shape += [jax.ShapeDtypeStruct((HP, D, W), BF)]
        params = cp()
    return pl.pallas_call(
        functools.partial(last_kernel, sizes, plan), grid=(steps + R // B,), in_specs=in_specs, out_specs=out_specs,
        out_shape=out_shape, scratch_shapes=scratch, compiler_params=params,
    )(*args)


def finish_kernel(*refs):
    refs = list(refs)
    take = lambda count: [refs.pop(0) for _ in range(count)]
    tab_ref, ro_ref, ru_ref, rd_ref = take(4)
    pieces = take(4)
    gains_ref, wq_ref, wu_ref = take(3)
    tab_out, wq_out, wo_out, wu_out, wd_out, g1_out, g2_out = refs
    table = jnp.concatenate([tab_ref[8 * pair:8 * pair + 2, :] for pair in range(4)], axis=0)
    tab_out[...] = table[:, :16]
    wo_out[...] = ro_ref[...]
    wu_out[...] = ru_ref[...]
    wd_out[...] = rd_ref[...]
    for pair in range(4):
        for part in range(3):
            wq_out[:, (part * 4 + pair) * 128:(part * 4 + pair + 1) * 128] = pieces[pair][:, part * 128:(part + 1) * 128]
    lane = lax.broadcasted_iota(jnp.int32, (16, 128), 1)
    row = lax.broadcasted_iota(jnp.int32, (16, 128), 0)
    own = lane == row + 16 * lax.rem(lax.axis_index("dp"), 8)
    square = lax.broadcasted_iota(jnp.int32, (16, 16), 0) == lax.broadcasted_iota(jnp.int32, (16, 16), 1)
    gains = gains_ref[...].astype(F32)
    for k, (w, grad, out) in enumerate(((wq_ref, wq_out, g1_out), (wu_ref, wu_out, g2_out))):
        gain = jnp.sum(jnp.where(own, gains[k:k + 1, :], 0.0), axis=1, keepdims=True)
        dots = jnp.sum(w[...].astype(F32) * grad[...], axis=1, keepdims=True)
        out[...] = jnp.sum(jnp.where(square, dots / gain, 0.0), axis=0, keepdims=True)


def finish(tab, results, gains, wq, wu):
    ro, ru, rd = results[:3]
    out_shape = [
        jax.ShapeDtypeStruct((8, 16), F32), jax.ShapeDtypeStruct(wq.shape, F32), jax.ShapeDtypeStruct(ro.shape, F32),
        jax.ShapeDtypeStruct(ru.shape, F32), jax.ShapeDtypeStruct(rd.shape, F32), jax.ShapeDtypeStruct((1, 16), F32),
        jax.ShapeDtypeStruct((1, 16), F32),
    ]
    return pl.pallas_call(finish_kernel, out_shape=out_shape, compiler_params=cp())(tab, *results, gains, wq, wu)


def on_device(devices, inputs, valid_len, norm_first, w_qkv, w_out, relative_bucket_table, norm_second, w_up, w_down, output_gradient):
    S, L, D = inputs.shape
    R = S * L
    HP = D // 128
    FFW = w_up.shape[1]
    fast = devices == 32 and D == 512 and S == 2
    table = relative_bucket_table
    x = inputs.reshape(R, D)
    og = output_gradient.reshape(R, D)
    by_pair = lambda w: w.reshape(D, 3, HP, 128).transpose(2, 0, 1, 3).reshape(HP, D, 384)
    if fast:
        sizes = device_grid(devices)
        mine = jnp.arange(128) // 16 == lax.rem(lax.axis_index("dp"), 8)
        place = lambda g: jnp.where(mine, jnp.tile(g, 8), jnp.zeros((), BF))
        row = jnp.arange(16)[:, None]
        gains = jnp.where(row == 0, place(norm_first), jnp.where(row == 1, place(norm_second), jnp.zeros((), BF)))
        mixed, qa, qkv, n1, g1, g2, wq, wo, wu, wd = first_half(
            sizes, valid_len, table, x, S, [gains, w_qkv, w_out, w_up, w_down]
        )
        wq, wo, wu, wd = wq.reshape(HP, D, 384), wo.reshape(D, D), wu.reshape(D, FFW), wd.reshape(FFW, D)
    else:
        sizes = None
        g1, wq, wo, g2, wu, wd = [
            lax.all_gather(a, "dp", axis=0, tiled=True) for a in (norm_first, w_qkv, w_out, norm_second, w_up, w_down)
        ]
        g1, g2 = g1.reshape(1, D).astype(F32), g2.reshape(1, D).astype(F32)
        wq = by_pair(wq)
        mixed, qa, qkv, n1 = first_half(None, valid_len, table, x, S, [g1, wq])
    out, ga, gm, gwo, gwu, gwd = ffn(x, mixed.reshape(R, D), og, g2, wo, wu, wd)
    got = last_half(
        sizes, valid_len, table, qa, qkv, mixed, gm.reshape(S, L, D), n1, wq, g1, x, ga, [gwo, gwu, gwd]
    )
    gi, tab = got[:2]
    if fast:
        rt, rq, ro, ru, rd, r1, r2 = finish(tab, got[2:], gains, w_qkv, w_up)
        r1, r2 = r1.reshape(-1), r2.reshape(-1)
    else:
        gwq = got[2].reshape(HP, D, 3, 128).transpose(1, 2, 0, 3).reshape(D, 3 * D)
        rq, ro, ru, rd = [
            lax.psum_scatter(a.astype(F32), "dp", scatter_dimension=0, tiled=True) for a in (gwq, gwo, gwu, gwd)
        ]
        r1 = jnp.sum(w_qkv.astype(F32) * rq, axis=1) / norm_first.astype(F32)
        r2 = jnp.sum(w_up.astype(F32) * ru, axis=1) / norm_second.astype(F32)
        rt = lax.psum(tab.reshape(HP, 8, 128)[:, :2, :16].reshape(table.shape), "dp")
    return (out.reshape(S, L, D), gi.reshape(S, L, D), r1, rq, ro, rt, r2, ru, rd)


def solution(mesh):
    placed = (
        P("dp", None, None), P("dp"), P("dp"), P("dp", None), P("dp", None), P(), P("dp"), P("dp", None), P("dp", None),
        P("dp", None, None),
    )
    return jax.shard_map(
        functools.partial(on_device, mesh.shape["dp"]),
        mesh=mesh,
        in_specs=placed,
        out_specs=(
            P("dp", None, None), P("dp", None, None), P("dp"), P("dp", None), P("dp", None), P(), P("dp"), P("dp", None),
            P("dp", None),
        ),
        check_vma=False,
    )
```

time: 270 us -> 229 us (0.85)
  Pallas kernels: 255 us -> 223 us
  local copies, waits for them, and re-layouts: 13 us -> 4.54 us
    pallas_call x6 -> x3, Pallas kernels: 207 us -> 175 us  [the longest x1 92.1 us: last_half(): pl.pallas_call(functools.partial(last_kernel, sizes, plan), grid=(steps +...]
    unnamed x6 -> x1, local copies, waits for them, and re-layouts: 6.63 us -> 3.04 us
    slice x3 -> x0, local copies, waits for them, and re-layouts: 3.05 us -> none  [the longest x1 1.27 us: on_device(): rt = small[8:16, :16]]
where the time goes in v2:
time: 229 us
  Pallas kernels  223 us (97%)
  local copies, waits for them, and re-layouts  4.54 us (2%)
    pallas_call x1, Pallas kernels, last_half(): pl.pallas_call(functools.partial(last_kernel, sizes, plan), grid=(steps +...  92.1 us
    pallas_call x1, Pallas kernels, first_half(): pl.pallas_call(functools.partial(first_kernel, sizes), grid=(HP, S), in_s...  81.2 us
    pallas_call x1, Pallas kernels, ffn(): pl.pallas_call(ffn_kernel, grid=(R // B,), in_specs=[row, row, row, full(...  47.6 us

profile of v2, /device:TPU:0, one launch (start us, length us, event | category | flops | bytes accessed | tf_op | source)
XLA Modules:
  0.0 228.6 jit_solution(3707710840490004598)
XLA Ops:
  0.7 0.7 tile.8
  1.3 0.1 tile.9
  1.4 0.7 tile.20
  2.1 0.1 tile.21
  2.2 0.7 select_select_fusion.refs_3_.refs_8_
  2.8 81.2 %shard_map.169 = (bf16[2,1024,512]{2,1,0:T(8,128)(2,1)}, bf16[2,4,2,1024,128]{4,3,2,1,0:T(8,128)(2,1)}, bf16[4,2,1024,384]{3,2,1,0:T(8,128)(2,1)}, bf16[2048,512...) custom-call(s32[2]{0:T(128)} %refs_0_.3, ...), custom_call_target="tpu_custom_call" | custom-call | tf_op jit(solution)/shard_map/pallas_call | solution.py:504
  84.0 47.6 %shard_map.170 = (bf16[2048,512]{1,0:T(8,128)(2,1)}, f32[2048,512]{1,0:T(8,128)}, bf16[2048,512]{1,0:T(8,128)(2,1)}, bf16[512,512]{1,0:T(8,128)(2,1)}, bf16[512,...) custom-call(bf16[2048,512]{1,0:T(8,128)(2,1)} %bitcast.16, bf16[2048,512]{1,0:T(8,128)(2,1)} %bitcast.18, ...), custom_call_target="tpu_custom_call" | custom-call | tf_op jit(solution)/shard_map/pallas_call | solution.py:304
  131.6 92.1 %shard_map.171 = (bf16[2048,512]{1,0:T(8,128)(2,1)}, f32[32,128]{1,0:T(8,128)}, f32[16,512]{1,0:T(8,128)}, f32[16,2048]{1,0:T(8,128)}, f32[64,512]{1,0:T(8,128)}...) custom-call(s32[2]{0:T(128)} %refs_0_.3, bf16[8,16]{1,0:T(8,128)(2,1)} %refs_1_.3, ...), custom_call_target="tpu_custom_call" | custom-call | tf_op jit(solution)/shard_map/pallas_call | solution.py:746
  223.7 1.9 shard_map.172
  225.6 3.0 %copy.20 = bf16[2,1024,512]{2,1,0:T(8,128)(2,1)} copy(bf16[2,1024,512]{2,1,0:T(8,128)(2,1)} %bitcast.19) | data formatting | bytes 4194304
  (2 shorter events, 0.0 us)

commit v3 on v2

--- a/solution.py
+++ b/solution.py
@@ -50,7 +50,6 @@
 def greet(sizes, groups):
     place = grid_position(sizes)
     barrier = pltpu.get_barrier_semaphore()
-    count = 0
     for group in groups:
         for move in moves(sizes, group):
             pl.semaphore_signal(
@@ -59,13 +58,15 @@
                 device_id=(flat(moved(place, sizes, group, move), sizes),),
                 device_id_type=MESH,
             )
-            count += 1
-    pl.semaphore_wait(barrier, count)
+
+
+def await_greetings(sizes, groups):
+    pl.semaphore_wait(pltpu.get_barrier_semaphore(), sum(len(moves(sizes, group)) for group in groups))
 
 
 class Gather:
-    def __init__(self, sizes, order, own, whole, local_sem, send_sems, recv_sems):
-        self.sizes, self.order = sizes, order
+    def __init__(self, sizes, order, own, whole, local_sem, send_sems, recv_sems, first):
+        self.sizes, self.order, self.first = sizes, order, first
         self.own, self.whole = own, whole
         self.local_sem, self.send_sems, self.recv_sems = local_sem, send_sems, recv_sems
 
@@ -78,8 +79,8 @@
             pltpu.make_async_remote_copy(
                 src_ref=self.own if phase == 0 else part,
                 dst_ref=part,
-                send_sem=self.send_sems.at[phase, k],
-                recv_sem=self.recv_sems.at[phase, k],
+                send_sem=self.send_sems.at[self.first + sum(len(moves(self.sizes, g)) for g in self.order[:phase]) + k],
+                recv_sem=self.recv_sems.at[self.first + sum(len(moves(self.sizes, g)) for g in self.order[:phase]) + k],
                 device_id=(flat(moved(place, self.sizes, group, move), self.sizes),),
                 device_id_type=MESH,
             )
@@ -103,8 +104,8 @@
 
 
 class Scatter:
-    def __init__(self, sizes, order, terms, sums, landing, result, send_sems, recv_sems):
-        self.sizes, self.order = sizes, order
+    def __init__(self, sizes, order, terms, sums, landing, result, send_sems, recv_sems, first):
+        self.sizes, self.order, self.first = sizes, order, first
         self.held = [terms] + list(sums)
         self.landing, self.result = landing, result
         self.send_sems, self.recv_sems = send_sems, recv_sems
@@ -142,8 +143,8 @@
                 pltpu.make_async_remote_copy(
                     src_ref=self.held[phase].at[part],
                     dst_ref=self.landing[phase].at[self.slot(phase, place)],
-                    send_sem=self.send_sems.at[phase, k],
-                    recv_sem=self.recv_sems.at[phase, k],
+                    send_sem=self.send_sems.at[self.first + sum(len(moves(self.sizes, g)) for g in self.order[:phase]) + k],
+                    recv_sem=self.recv_sems.at[self.first + sum(len(moves(self.sizes, g)) for g in self.order[:phase]) + k],
                     device_id=(flat(other, self.sizes),),
                     device_id_type=MESH,
                 )
@@ -197,17 +198,26 @@
             lax.fori_loop(0, int(np.prod(lead)), body, 0)
 
 
-def semaphores(items):
-    return [pltpu.SemaphoreType.DMA((items, 4, 16)), pltpu.SemaphoreType.DMA((items, 4, 16))]
-
-
-def run_schedule(step, schedule, parts):
+def firsts(sizes, orders):
+    counts = [sum(len(moves(sizes, group)) for group in order) for order in orders]
+    return [sum(counts[:k]) for k in range(len(counts))], sum(counts)
+
+
+def semaphores(sizes, orders):
+    return [pltpu.SemaphoreType.DMA((firsts(sizes, orders)[1],))] * 2
+
+
+def run_actions(actions, parts):
+    for action, item, phase in actions:
+        getattr(parts[item], action)(phase)
+
+
+def run_schedule(tick, schedule, parts):
     for at, actions in sorted(schedule.items()):
 
-        @pl.when(step == at)
+        @pl.when(tick == at)
         def _(actions=actions):
-            for action, item, phase in actions:
-                getattr(parts[item], action)(phase)
+            run_actions(actions, parts)
 
 
 LOW=(0,1,2,3,4,5,6,7,8,12,16,32,64,128,256,512)
@@ -229,16 +239,26 @@
     at=lax.broadcasted_iota(jnp.int32,whole.shape,0)
     return jnp.sum(jnp.where(at==head,whole,0.0),axis=0,keepdims=True)
 
-def build_bias(table_ref, hp, bias, transposed):
-    lane=lax.broadcasted_iota(jnp.int32,(1,2*T),1)
-    m=jnp.where(lane<T,lane,lane-2*T)
-    for h in range(2):
-        row=table_row(table_ref,2*hp+h)
-        for bd in range(3):
-            w=bias_of(bd*T+(m if transposed else -m),row)
-            tile=pltpu.roll(jnp.broadcast_to(w,(T,2*T)),0,1,stride=1,stride_axis=0)
-            bias[h,bd]=tile[:,:T]
-        bias[h,3]=jnp.broadcast_to(row[:,15:16],(T,T))
+H = 128
+VARIED = (0, 1, 2, 4)
+
+
+def build_bias(row, store):
+    lane = lax.broadcasted_iota(jnp.int32, (1, 2 * H), 1)
+    m = jnp.where(lane < H, lane, lane - 2 * H)
+    for n, delta in enumerate(VARIED):
+        for transposed in (False, True):
+            w = bias_of(delta * H + (m if transposed else -m), row)
+            tile = pltpu.roll(jnp.broadcast_to(w, (H, 2 * H)), 0, 1, stride=1, stride_axis=0)
+            store(n, transposed, tile[:, :H])
+
+
+def biased(tile, delta, bias, row):
+    if delta < 0:
+        return jnp.full((H, H), NEG, F32)
+    if delta in VARIED:
+        return tile + bias[VARIED.index(delta)]
+    return tile + row[:, 14:15] if delta == 3 else tile + row[:, 15:16]
 
 def split3(v):
     hi=v.astype(jnp.bfloat16); r=v-hi.astype(jnp.float32)
@@ -311,20 +331,42 @@
 
 
 SPREAD = ((0, 1, 2), (3,))
+ZXY, YZX, XZY, XYZ = (((a,), (b,), (c,), (3,)) for a, b, c in ((0, 2, 1), (1, 0, 2), (2, 0, 1), (2, 1, 0)))
 GATHER_ORDERS = {
-    "gains": SPREAD, "q0": SPREAD, "q1": SPREAD,
-    "q2": ((0,), (1,), (2,), (3,)), "q3": ((0,), (2,), (1,), (3,)),
-    "out": ((0,), (1,), (2,), (3,)), "up": ((0,), (1,), (2,), (3,)), "down": ((0,), (2,), (1,), (3,)),
+    "q0": SPREAD, "gains": SPREAD, "q2": XZY, "q1": ZXY, "down1": XZY, "q3": ZXY, "down0": ZXY, "up0": YZX, "out": XYZ, "up1": YZX,
 }
-GATHER_SCHEDULE = {
-    1: [("finish", "q1", 0), ("start", "q1", 1), ("finish", "q2", 0), ("start", "q2", 1), ("finish", "up", 0), ("start", "up", 1), ("start", "out", 0)],
-    2: [("finish", "q1", 1), ("finish", "q2", 1), ("start", "q2", 2), ("finish", "down", 0), ("start", "down", 1), ("start", "q3", 0), ("finish", "up", 1), ("start", "up", 2)],
-    3: [("finish", "q2", 2), ("start", "q2", 3), ("finish", "out", 0), ("start", "out", 1), ("finish", "q3", 0), ("start", "q3", 1), ("finish", "down", 1), ("start", "down", 2)],
-    4: [("finish", "q2", 3), ("finish", "q3", 1), ("start", "q3", 2), ("finish", "out", 1), ("start", "out", 2)],
-    5: [("finish", "q3", 2), ("start", "q3", 3), ("finish", "up", 2), ("start", "up", 3), ("finish", "out", 2), ("start", "out", 3)],
-    6: [("finish", "q3", 3), ("finish", "down", 2), ("start", "down", 3)],
-    7: [("finish", "up", 3), ("finish", "out", 3)],
-}
+
+
+def timetable(starts):
+    table = {}
+    for item, ticks in starts.items():
+        for phase, tick in enumerate(ticks):
+            if phase:
+                table.setdefault(tick, []).append(("finish", item, phase - 1))
+            if phase < len(ticks) - 1:
+                table.setdefault(tick, []).append(("start", item, phase))
+    return table
+
+
+GATHER_SCHEDULE = timetable(
+    {
+        "q2": (-1, 0, 2, 4, 5), "q1": (0, 2, 3, 3, 3), "down1": (-1, 0, 3, 6, 8), "q3": (0, 3, 4, 6, 7),
+        "down0": (0, 3, 5, 7, 8), "up0": (-1, 0, 4, 7, 8), "out": (-1, 0, 2, 7, 9), "up1": (-1, 0, 6, 8, 9),
+    }
+)
+
+
+def own_lanes():
+    row = lax.broadcasted_iota(jnp.int32, (16, 128), 0)
+    lane = lax.broadcasted_iota(jnp.int32, (16, 128), 1)
+    return lane == row + 16 * lax.rem(lax.axis_index("dp"), 8)
+
+
+def placed_gains(first_ref, second_ref):
+    row = lax.broadcasted_iota(jnp.int32, (16, 16), 0)
+    both = jnp.where(row == 0, first_ref[...].reshape(1, 16).astype(F32), 0.0)
+    both = jnp.where(row == 1, second_ref[...].reshape(1, 16).astype(F32), both)
+    return dot_nn(both.astype(BF), jnp.where(own_lanes(), 1.0, 0.0).astype(BF)).astype(BF)
 
 
 def first_kernel(sizes, *refs):
@@ -333,13 +375,14 @@
     take = lambda count: [refs.pop(0) for _ in range(count)]
     vl_ref, table_ref, x_ref = take(3)
     if remote:
-        gains_own, wq_own, wo_own, wu_own, wd_own = take(5)
+        first_ref, second_ref, wq_own, wo_own, wu_own, wd_own = take(6)
     else:
         g_ref, w_ref = take(2)
-    mixed_ref, qa_ref, qkv_ref, n_ref = take(4)
+    mixed_ref, qa_ref, qkv_ref, nt_ref, bt_ref = take(5)
     if remote:
         g1_ref, g2_ref, wq_out, wo_ref, wu_ref, wd_ref = take(6)
-    bias, xhat = take(2)
+    bias, bias_t, xhat, xhat_t, n_s, nt_s, held_sem = take(7)
+    keep = [pltpu.make_async_copy(nt_s, nt_ref, held_sem.at[0]), pltpu.make_async_copy(bias_t, bt_ref, held_sem.at[1])]
     hp = pl.program_id(0)
     s = pl.program_id(1)
     pairs = pl.num_programs(0)
@@ -348,14 +391,20 @@
     R, D = x_ref.shape
     B = 512
     if remote:
-        q_own, wq, gains, local, send, recv, out_sem = take(7)
+        q_own, wq, gains_own, gains, local, send, recv, out_sem = take(8)
         names = list(GATHER_ORDERS)
-        own = dict(gains=gains_own, out=wo_own, up=wu_own, down=wd_own)
-        whole = dict(gains=gains, out=wo_ref, up=wu_ref, down=wd_ref)
+        own = dict(gains=gains_own, out=wo_own)
+        whole = dict(gains=gains, out=wo_ref)
+        for half in range(2):
+            cols = slice(half * wu_own.shape[1] // 2, (half + 1) * wu_own.shape[1] // 2)
+            rows = slice(half * wd_own.shape[0] // 2, (half + 1) * wd_own.shape[0] // 2)
+            own["up%d" % half], whole["up%d" % half] = wu_own.at[:, cols], wu_ref.at[:, :, :, :, :, cols]
+            own["down%d" % half], whole["down%d" % half] = wd_own.at[rows], wd_ref.at[:, :, :, :, rows]
         for pair in range(4):
             own["q%d" % pair], whole["q%d" % pair] = q_own.at[pair], wq.at[pair]
+        place = firsts(sizes, GATHER_ORDERS.values())[0]
         parts = {
-            name: Gather(sizes, GATHER_ORDERS[name], own[name], whole[name], local.at[k], send.at[k], recv.at[k])
+            name: Gather(sizes, GATHER_ORDERS[name], own[name], whole[name], local.at[k], send, recv, place[k])
             for k, name in enumerate(names)
         }
         out_copy = lambda pair: pltpu.make_async_copy(wq.at[pair], wq_out.at[pair], out_sem.at[pair])
@@ -363,28 +412,46 @@
     @pl.when(step == 0)
     def _():
         if remote:
+            greet(sizes, SPREAD)
+            gains_own[...] = placed_gains(first_ref, second_ref)
             for pair in range(4):
                 for part in range(3):
                     q_own[pair, :, part * 128:(part + 1) * 128] = wq_own[:, (part * 4 + pair) * 128:(part * 4 + pair + 1) * 128]
-            greet(sizes, SPREAD)
+
+        def all_biases(head, unused):
+            def store(n, transposed, tile):
+                (bias_t if transposed else bias)[head, n] = tile
+
+            build_bias(table_row(table_ref, head), store)
+            return unused
+
+        lax.fori_loop(0, 2 * pairs, all_biases, 0)
+
+        def norm(block, unused):
+            at = pl.ds(pl.multiple_of(block * B, B), B)
+            xh = ln_parts(x_ref[at, :].astype(F32))[0]
+            xhat[at, :] = xh
+            return unused
+
+        lax.fori_loop(0, R // B, norm, 0)
+        if remote:
+            await_greetings(sizes, SPREAD)
             parts["q0"].start(0)
             parts["gains"].start(0)
-
-        def norm(block, unused):
+            run_actions(GATHER_SCHEDULE[-1], parts)
+
+        def turn(block, unused):
             at = pl.ds(pl.multiple_of(block * B, B), B)
-            xhat[at, :] = ln_parts(x_ref[at, :].astype(F32))[0]
+            xhat_t[:, at] = xhat[at, :].T
             return unused
 
-        lax.fori_loop(0, R // B, norm, 0)
+        lax.fori_loop(0, R // B, turn, 0)
         if remote:
             parts["gains"].finish(0)
             parts["q0"].finish(0)
             parts["gains"].start(1)
             parts["q0"].start(1)
-            parts["q1"].start(0)
-            parts["q2"].start(0)
-            parts["up"].start(0)
-            parts["down"].start(0)
+            run_actions(GATHER_SCHEDULE[0], parts)
             parts["gains"].finish(1)
             tiles = []
             for z in range(sizes[0]):
@@ -398,42 +465,46 @@
             gain = tile[0:1, :]
         else:
             gain = g_ref[...]
+        gain_t = jnp.broadcast_to(gain, (8, D)).T[:, 0:1]
 
         def scale(block, unused):
             at = pl.ds(pl.multiple_of(block * B, B), B)
-            n_ref[at, :] = (xhat[at, :] * gain).astype(BF)
+            n_s[at, :] = (xhat[at, :] * gain).astype(BF)
+            nt_s[:, at] = (xhat_t[:, at] * gain_t).astype(BF)
             return unused
 
         lax.fori_loop(0, R // B, scale, 0)
+        for copy in keep:
+            copy.start()
         if remote:
             parts["q0"].finish(1)
 
     if remote:
-        run_schedule(step, GATHER_SCHEDULE, parts)
+        run_schedule(step + 1, {tick: GATHER_SCHEDULE[tick] for tick in GATHER_SCHEDULE if 0 < tick < 9}, parts)
 
     @pl.when(s == 0)
     def _():
-        build_bias(table_ref, hp, bias, False)
         weights = wq[hp].reshape(D, 384) if remote else w_ref[0]
         if remote:
             out_copy(hp).start()
         for seq in range(S):
             for half in range(L // B):
                 row = seq * L + half * B
-                qkv_ref[0, seq, half * B:(half + 1) * B, :] = dot_nn(n_ref[row:row + B, :], weights).astype(BF)
-
-    attend(vl_ref[s], qkv_ref.at[0, s], mixed_ref.at[0], qa_ref.at[0, 0], bias)
-
-    if remote:
-
-        @pl.when(step == pairs * S - 1)
-        def _():
-            parts["down"].finish(3)
+                qkv_ref[0, seq, half * B:(half + 1) * B, :] = dot_nn(n_s[row:row + B, :], weights).astype(BF)
+
+    attend(vl_ref[s], qkv_ref.at[0, s], mixed_ref.at[0], qa_ref.at[0, 0], bias, table_ref, hp)
+
+    @pl.when(step == pairs * S - 1)
+    def _():
+        for copy in keep:
+            copy.wait()
+        if remote:
+            run_actions(GATHER_SCHEDULE[9], parts)
             for pair in range(4):
                 out_copy(pair).wait()
 
 
-def attend(valid, qkv_ref, mixed_ref, qa_ref, bias):
+def attend(valid, qkv_ref, mixed_ref, qa_ref, bias, table_ref, hp):
     L = qkv_ref.shape[0]
     nb = L // T
     key = lax.broadcasted_iota(jnp.int32, (L, 1), 0)
@@ -441,6 +512,7 @@
     lane = lax.broadcasted_iota(jnp.int32, (T, 128), 1)
     ks = [halves(h, qkv_ref[:, 128:256], [1.0, 1.0, 1.0, mask], L) for h in range(2)]
     v = qkv_ref[:, 256:384]
+    rows = [table_row(table_ref, 2 * hp + h) for h in range(2)]
     for qb in range(nb):
         kk = (qb + 1) * T
         qt = qkv_ref[qb * T:(qb + 1) * T, 0:128] * jnp.asarray(0.125, BF)
@@ -448,7 +520,19 @@
         for h in range(2):
             qh = halves(h, qt, [None, None, None, 1.0], T)
             sc = dot_nt(qh, ks[h][:kk])
-            sc = jnp.concatenate([sc[:, kb * T:(kb + 1) * T] + bias[h, qb - kb] for kb in range(qb + 1)], axis=1)
+            sc = jnp.concatenate(
+                [
+                    jnp.concatenate(
+                        [
+                            biased(sc[i * H:(i + 1) * H, j * H:(j + 1) * H], 2 * qb + i - j, bias.at[2 * hp + h], rows[h])
+                            for j in range(kk // H)
+                        ],
+                        axis=1,
+                    )
+                    for i in range(2)
+                ],
+                axis=0,
+            )
             mx = jnp.max(sc, axis=1, keepdims=True)
             p = jnp.exp(sc - mx)
             l = jnp.sum(p, axis=1, keepdims=True)
@@ -474,18 +558,23 @@
         pl.BlockSpec((1, L, 128), lambda h, s: (s, 0, h)),
         pl.BlockSpec((1, 1, 2, L, 128), lambda h, s: (s, h, 0, 0, 0)),
         pl.BlockSpec((1, S, L, 384), lambda h, s: (h, 0, 0, 0)),
-        whole_block((R, D)),
+        anyspace,
+        anyspace,
     ]
     out_shape = [
         jax.ShapeDtypeStruct((S, L, D), BF),
         jax.ShapeDtypeStruct((S, HP, 2, L, 128), BF),
         jax.ShapeDtypeStruct((HP, S, L, 384), BF),
-        jax.ShapeDtypeStruct((R, D), BF),
+        jax.ShapeDtypeStruct((D, R), BF),
+        jax.ShapeDtypeStruct((2 * HP, len(VARIED), H, H), F32),
     ]
-    scratch = [pltpu.VMEM((2, 4, T, T), F32), pltpu.VMEM((R, D), F32)]
+    scratch = [
+        pltpu.VMEM((2 * HP, len(VARIED), H, H), F32), pltpu.VMEM((2 * HP, len(VARIED), H, H), F32), pltpu.VMEM((R, D), F32),
+        pltpu.VMEM((D, R), F32), pltpu.VMEM((R, D), BF), pltpu.VMEM((D, R), BF), pltpu.SemaphoreType.DMA((2,)),
+    ]
     if remote:
-        gains, wq, wo, wu, wd = weights
-        in_specs += [whole_block(gains.shape), whole_block(wq.shape), anyspace, anyspace, anyspace]
+        first, second, wq, wo, wu, wd = weights
+        in_specs += [whole_block(first.shape), whole_block(second.shape), whole_block(wq.shape), anyspace, anyspace, anyspace]
         out_specs += [whole_block((1, D)), whole_block((1, D))] + [anyspace] * 4
         out_shape += [jax.ShapeDtypeStruct((1, D), F32)] * 2
         out_shape += [jax.ShapeDtypeStruct((HP,) + sizes + (16, 384), BF)]
@@ -493,9 +582,10 @@
         scratch += [
             pltpu.VMEM((HP, 16, 384), BF),
             pltpu.VMEM((HP,) + sizes + (16, 384), BF),
+            pltpu.VMEM((16, 128), BF),
             pltpu.VMEM(sizes + (16, 128), BF),
             pltpu.SemaphoreType.DMA((len(GATHER_ORDERS),)),
-        ] + semaphores(len(GATHER_ORDERS)) + [pltpu.SemaphoreType.DMA((HP,))]
+        ] + semaphores(sizes, GATHER_ORDERS.values()) + [pltpu.SemaphoreType.DMA((HP,))]
         params = cp(collective_id=1, has_side_effects=True)
     else:
         gain, wq = weights
@@ -507,40 +597,32 @@
     )(vl, table, x, *weights)
 
 
+CXYZ, CYXZ, CXZY, CYZX = (((3,), (a,), (b,), (c,)) for a, b, c in ((2, 1, 0), (1, 2, 0), (2, 0, 1), (1, 0, 2)))
+DIRECT = ((3,), (0, 1, 2))
 SCATTER_ORDERS = {
-    "out": ((3,), (2,), (1,), (0,)), "up": ((3,), (2,), (1,), (0,)), "down": ((3,), (1,), (2,), (0,)),
-    "q0": ((3,), (1,), (2,), (0,)), "q1": ((3,), (2,), (1,), (0,)), "q2": ((3,), (1,), (2,), (0,)), "q3": ((3,), (0, 1, 2)),
+    "up0": CYXZ, "down0": CXYZ, "out": CYZX, "up1": CXZY, "down1": CYXZ, "q0": CYZX, "q1": CXZY, "q2": DIRECT, "q3": DIRECT,
 }
-SCATTER_SCHEDULE = {
-    0: [("start", "up", 0), ("start", "down", 0), ("start", "out", 0)],
-    1: [("finish", "up", 0), ("start", "up", 1), ("finish", "down", 0), ("start", "down", 1), ("finish", "out", 0), ("start", "out", 1)],
-    2: [("start", "q0", 0)],
-    3: [("finish", "q0", 0), ("start", "q0", 1), ("finish", "out", 1), ("start", "out", 2)],
-    4: [("finish", "up", 1), ("start", "up", 2), ("finish", "down", 1), ("start", "down", 2), ("start", "q1", 0), ("finish", "out", 2), ("start", "out", 3)],
-    5: [("finish", "q1", 0), ("start", "q1", 1), ("finish", "q0", 1), ("start", "q0", 2)],
-    6: [("finish", "up", 2), ("start", "up", 3), ("finish", "down", 2), ("start", "down", 3), ("start", "q2", 0), ("finish", "out", 3)],
-    7: [("finish", "q1", 1), ("start", "q1", 2), ("finish", "q2", 0), ("start", "q2", 1), ("finish", "q0", 2), ("start", "q0", 3)],
-    8: [("start", "q3", 0), ("start", "table", 0), ("finish", "q2", 1), ("start", "q2", 2), ("finish", "q1", 2), ("start", "q1", 3)],
-    9: [("finish", "q3", 0), ("start", "q3", 1), ("finish", "table", 0), ("start", "table", 1), ("finish", "up", 3), ("finish", "q0", 3)],
-    10: [("finish", "q2", 2), ("start", "q2", 3), ("finish", "down", 3), ("finish", "table", 1)],
-    11: [("finish", "q1", 3)],
-}
-SCATTER_TAIL = [("finish", "q2", 3), ("finish", "q3", 1)]
+SCATTER_SCHEDULE = timetable(
+    {
+        "q3": (8, 9, 12), "out": (1, 2, 3, 5, 6), "up0": (1, 2, 4, 5, 7), "up1": (1, 2, 4, 6, 7), "q1": (4, 5, 6, 7, 8),
+        "q0": (2, 3, 5, 7, 8), "down0": (1, 3, 5, 6, 8), "down1": (1, 3, 6, 7, 9), "q2": (6, 7, 11), "table": (8, 9, 11),
+    }
+)
 
 
 def last_kernel(sizes, plan, *refs):
     remote = sizes is not None
     refs = list(refs)
     take = lambda count: [refs.pop(0) for _ in range(count)]
-    vl_ref, table_ref, qa_ref, qkv_ref, o_ref, g_ref, n_ref, w_ref, gain_ref, x_ref, ga_ref = take(11)
+    vl_ref, table_ref, bias, qa_ref, qkv_ref, o_ref, g_ref, nt_ref, w_ref, gain_ref, x_ref, ga_ref = take(12)
     if remote:
         wo_terms, wu_terms, wd_terms = take(3)
     gi_ref, tab_ref = take(2)
     if remote:
-        results = dict(zip(SCATTER_ORDERS, take(7)))
+        results = dict(zip(SCATTER_ORDERS, take(9)))
     else:
         (gw_ref,) = take(1)
-    bias, gacc, far, dqt, grads = take(5)
+    gacc, far, dqt, grads = take(4)
     t = pl.program_id(0)
     pairs = grads.shape[0]
     S = grads.shape[1] // qkv_ref.shape[2]
@@ -552,65 +634,71 @@
     D = x_ref.shape[1]
     if remote:
         wq_terms, tab_own, tab_all, local = take(4)
-        terms = dict(out=wo_terms, up=wu_terms, down=wd_terms)
+        terms = dict(out=wo_terms)
+        for half in range(2):
+            cols = slice(half * wu_terms.shape[5] // 2, (half + 1) * wu_terms.shape[5] // 2)
+            rows = slice(half * wd_terms.shape[4] // 2, (half + 1) * wd_terms.shape[4] // 2)
+            terms["up%d" % half] = wu_terms.at[:, :, :, :, :, cols]
+            terms["down%d" % half] = wd_terms.at[:, :, :, :, rows]
         for pair in range(4):
             terms["q%d" % pair] = wq_terms.at[pair]
         send, recv = refs[-2:]
+        place = firsts(sizes, [*SCATTER_ORDERS.values(), SPREAD])[0]
         parts = {}
         for k, name in enumerate(SCATTER_ORDERS):
             sums, landing = plan[name]
             parts[name] = Scatter(
-                sizes, SCATTER_ORDERS[name], terms[name], take(len(sums)), take(len(landing)), results[name], send.at[k], recv.at[k]
+                sizes, SCATTER_ORDERS[name], terms[name], take(len(sums)), take(len(landing)), results[name], send, recv, place[k]
             )
-        parts["table"] = Gather(sizes, SPREAD, tab_own, tab_all, local, send.at[len(plan)], recv.at[len(plan)])
+        parts["table"] = Gather(sizes, SPREAD, tab_own, tab_all, local, send, recv, place[-1])
 
         @pl.when(t == 0)
         def _():
             greet(sizes, SPREAD)
 
-        run_schedule(t, SCATTER_SCHEDULE, parts)
+        @pl.when(t == 1)
+        def _():
+            await_greetings(sizes, SPREAD)
+
+        run_schedule(t, {at: SCATTER_SCHEDULE[at] for at in SCATTER_SCHEDULE if at < 12}, parts)
 
     @pl.when(t < steps)
     def _():
         @pl.when(s == 0)
         def _():
-            build_bias(table_ref, hp, bias, True)
             gacc[...] = jnp.zeros_like(gacc)
             far[...] = jnp.zeros_like(far)
 
         at = pl.multiple_of(s * L, L)
-        attend_back(vl_ref[s], qa_ref.at[0, 0], qkv_ref.at[0, 0], o_ref[0], g_ref[0], grads, hp, at, bias, gacc, far, dqt)
+        attend_back(vl_ref[s], qa_ref.at[0, 0], qkv_ref.at[0, 0], o_ref[0], g_ref[0], grads, hp, at, bias, table_ref, gacc, far, dqt)
 
         @pl.when(s == S - 1)
         def _():
             rows = table_terms(gacc, far)
             place = pl.ds(pl.multiple_of(hp * 8, 8), 8)
             (tab_own if remote else tab_ref)[place, :] = rows
-            for part in range(3):
-                gw = dot_tn(n_ref[...], grads[hp, :, part * 128:(part + 1) * 128]).astype(BF)
-                if remote:
-                    wq_terms[hp, :, :, :, :, :, part * 128:(part + 1) * 128] = gw.reshape(sizes + (16, 128))
-                else:
-                    gw_ref[hp, :, part * 128:(part + 1) * 128] = gw
+            gw = dot_nn(nt_ref[...], grads[hp]).astype(BF)
+            if remote:
+                wq_terms[hp] = gw.reshape(sizes + (16, 384))
+            else:
+                gw_ref[hp] = gw
 
     @pl.when(t >= steps)
     def _():
         B = x_ref.shape[0]
         at = pl.ds(pl.multiple_of((t - steps) * B, B), B)
         xhat, r = ln_parts(x_ref[...].astype(F32))
-        dn = None
-        for pair in range(pairs):
-            weights = w_ref[pair]
-            term = dot_nt(grads[pair, at, :], weights)
-            dn = term if dn is None else dn + term
+        dn = dot_nt(
+            jnp.concatenate([grads[pair, at, :] for pair in range(pairs)], axis=1),
+            jnp.concatenate([w_ref[pair] for pair in range(pairs)], axis=1),
+        )
         gi_ref[...] = (ga_ref[...] + ln_back(dn, gain_ref[...], xhat, r)[0]).astype(BF)
 
     if remote:
 
         @pl.when(t == pl.num_programs(0) - 1)
         def _():
-            for action, item, phase in SCATTER_TAIL:
-                getattr(parts[item], action)(phase)
+            run_actions(SCATTER_SCHEDULE[12], parts)
             total = None
             for at in itertools.product(*[range(size) for size in sizes]):
                 block = tab_all[at]
@@ -619,23 +707,25 @@
 
 
 def table_terms(gacc, far):
-    lane2 = lax.broadcasted_iota(jnp.int32, (1, 2 * T), 1)
-    m = jnp.where(lane2 < T, lane2, lane2 - 2 * T)
+    lane = lax.broadcasted_iota(jnp.int32, (1, 2 * H), 1)
+    m = jnp.where(lane < H, lane, lane - 2 * H)
     bl = lax.broadcasted_iota(jnp.int32, (1, 128), 1)
     rows = []
     for h in range(2):
-        row = jnp.where(bl == 15, jnp.sum(far[h:h + 1, :], axis=1, keepdims=True), 0.0)
-        for bd in range(3):
-            w = jnp.concatenate([gacc[h, bd], jnp.zeros((T, T), F32)], axis=1)
+        row = jnp.zeros((1, 128), F32)
+        for b in (14, 15):
+            row = row + jnp.where(bl == b, jnp.sum(jnp.sum(far[h, b - 14], axis=0, keepdims=True), axis=1, keepdims=True), 0.0)
+        for n, delta in enumerate(VARIED):
+            w = jnp.concatenate([gacc[h, n], jnp.zeros((H, H), F32)], axis=1)
             acc = w[:8]
-            for a in range(1, T // 8):
-                acc = acc + pltpu.roll(w[8 * a:8 * a + 8], 2 * T - 8 * a, 1)
+            for a in range(1, H // 8):
+                acc = acc + pltpu.roll(w[8 * a:8 * a + 8], 2 * H - 8 * a, 1)
             diag = acc[0:1]
             for a in range(1, 8):
-                diag = diag + pltpu.roll(acc[a:a + 1], 2 * T - a, 1)
-            dist = bd * T + m
+                diag = diag + pltpu.roll(acc[a:a + 1], 2 * H - a, 1)
+            dist = delta * H + m
             for b in range(16):
-                if LOW[b] >= (bd + 1) * T or (b < 15 and LOW[b + 1] <= (bd - 1) * T):
+                if LOW[b] >= (delta + 1) * H or (b < 15 and LOW[b + 1] <= (delta - 1) * H):
                     continue
                 sel = dist >= LOW[b]
                 if b < 15:
@@ -645,8 +735,9 @@
     return jnp.concatenate(rows + [jnp.zeros((6, 128), F32)], axis=0)
 
 
-def attend_back(valid, qa_ref, qkv_ref, o, g, grads, hp, first, bias, gacc, far, dqt):
+def attend_back(valid, qa_ref, qkv_ref, o, g, grads, hp, first, bias, table_ref, gacc, far, dqt):
     L = qkv_ref.shape[0]
+    rows = [table_row(table_ref, 2 * hp + h) for h in range(2)]
     nb = L // T
     key = lax.broadcasted_iota(jnp.int32, (L, 1), 0)
     mask = jnp.where(key < valid, 0.0, NEG)
@@ -668,17 +759,29 @@
             qh = qa_ref[h]
             st = dot_nt(ks[h][kb * T:(kb + 1) * T], qh[kb * T:])
             dp = dot_nt(vs[h][kb * T:(kb + 1) * T], gs[h][kb * T:])
-            st = jnp.concatenate([st[:, i * T:(i + 1) * T] + bias[h, i] for i in range(nb - kb)], axis=1)
+            st = jnp.concatenate(
+                [
+                    jnp.concatenate(
+                        [biased(st[j * H:(j + 1) * H, i * H:(i + 1) * H], i - j, bias.at[0, h], rows[h]) for i in range(2 * (nb - kb))],
+                        axis=1,
+                    )
+                    for j in range(2)
+                ],
+                axis=0,
+            )
             p = jnp.exp(st)
             ds = p * dp
             pb = p.astype(BF)
             dsb = ds.astype(BF)
             dvs.append(dot_nn(pb, gs[h][kb * T:]))
             dks.append(dot_nn(dsb, qh[kb * T:]))
-            for i in range(min(nb - kb, 3)):
-                gacc[h, i] += ds[:, i * T:(i + 1) * T]
-            if nb - kb > 3:
-                far[h:h + 1, :] += jnp.sum(ds[:, 3 * T:], axis=0, keepdims=True)
+            for delta in range(2 * (nb - kb)):
+                both = [ds[j * H:(j + 1) * H, i * H:(i + 1) * H] for j in range(2) for i in range(2 * (nb - kb)) if i - j == delta]
+                both = both[0] if len(both) == 1 else both[0] + both[1]
+                if delta in VARIED:
+                    gacc[h, VARIED.index(delta)] += both
+                else:
+                    far[h, 0 if delta == 3 else 1] += jnp.sum(both.reshape(H // 8, 8, H), axis=0)
             r = dot_nn(kt[h * 64:(h + 1) * 64, kb * T:(kb + 1) * T], dsb)
             if kb == 0:
                 dqt[h * 64:(h + 1) * 64, :] = r
@@ -690,7 +793,7 @@
     grads[hp, pl.ds(first, L), 0:128] = dqt[...].T.astype(BF)
 
 
-def last_half(sizes, vl, table, qa, qkv, mixed, gm, n1, wq, gain, x, ga, ffn_grads):
+def last_half(sizes, vl, table, bias_t, qa, qkv, mixed, gm, nt, wq, gain, x, ga, ffn_grads):
     HP, S, L, W = qkv.shape
     R, D = x.shape
     B = 512
@@ -702,11 +805,12 @@
     in_specs = [
         pl.BlockSpec(memory_space=pltpu.SMEM),
         whole_block(table.shape),
+        pl.BlockSpec((1, 2, len(VARIED), H, H), lambda t: (pair(t), 0, 0, 0, 0)),
         pl.BlockSpec((1, 1, 2, L, 128), lambda t: (seq(t), pair(t), 0, 0, 0)),
         pl.BlockSpec((1, 1, L, W), lambda t: (pair(t), seq(t), 0, 0)),
         pl.BlockSpec((1, L, 128), lambda t: (seq(t), 0, pair(t))),
         pl.BlockSpec((1, L, 128), lambda t: (seq(t), 0, pair(t))),
-        whole_block((R, D)),
+        whole_block((D, R)),
         whole_block((HP, D, W)),
         whole_block((1, D)),
         late,
@@ -715,17 +819,18 @@
     out_specs = [late, whole_block((8 * HP, 128))]
     out_shape = [jax.ShapeDtypeStruct((R, D), BF), jax.ShapeDtypeStruct((8 * HP, 128), F32)]
     scratch = [
-        pltpu.VMEM((2, 4, T, T), F32), pltpu.VMEM((2, 3, T, T), F32), pltpu.VMEM((8, T), F32), pltpu.VMEM((128, L), F32),
+        pltpu.VMEM((2, len(VARIED), H, H), F32), pltpu.VMEM((2, 2, 8, H), F32), pltpu.VMEM((128, L), F32),
         pltpu.VMEM((HP, R, W), BF),
     ]
-    args = [vl, table, qa, qkv, mixed, gm, n1, wq, gain, x, ga]
+    args = [vl, table, bias_t.reshape(HP, 2, len(VARIED), H, H), qa, qkv, mixed, gm, nt, wq, gain, x, ga]
     plan = None
     if remote:
         count = int(np.prod(sizes))
         terms = [a.reshape(sizes + (a.shape[0] // count, a.shape[1])) for a in ffn_grads]
         args += terms
         in_specs += [whole_block(a.shape) for a in terms]
-        blocks = dict(zip(("out", "up", "down"), [a.shape[4:] for a in terms]))
+        (_, D_), (_, U_), (rows_, _) = [a.shape[4:] for a in terms]
+        blocks = dict(out=(16, D_), up0=(16, U_ // 2), up1=(16, U_ // 2), down0=(rows_ // 2, D_), down1=(rows_ // 2, D_))
         for k in range(HP):
             blocks["q%d" % k] = (16, W)
         plan = {name: Scatter.shapes(sizes, SCATTER_ORDERS[name], blocks[name]) for name in SCATTER_ORDERS}
@@ -737,7 +842,7 @@
         ]
         for name in SCATTER_ORDERS:
             scratch += [pltpu.VMEM(shape, BF) for shape in plan[name][0] + plan[name][1]]
-        scratch += semaphores(len(SCATTER_ORDERS) + 1)
+        scratch += semaphores(sizes, [*SCATTER_ORDERS.values(), SPREAD])
         params = cp(collective_id=2, has_side_effects=True)
     else:
         out_specs += [whole_block((HP, D, W))]
@@ -752,37 +857,33 @@
 def finish_kernel(*refs):
     refs = list(refs)
     take = lambda count: [refs.pop(0) for _ in range(count)]
-    tab_ref, ro_ref, ru_ref, rd_ref = take(4)
+    tab_ref, ru0_ref, rd0_ref, ro_ref, ru1_ref, rd1_ref = take(6)
     pieces = take(4)
-    gains_ref, wq_ref, wu_ref = take(3)
+    first_ref, second_ref, wq_ref, wu_ref = take(4)
     tab_out, wq_out, wo_out, wu_out, wd_out, g1_out, g2_out = refs
     table = jnp.concatenate([tab_ref[8 * pair:8 * pair + 2, :] for pair in range(4)], axis=0)
     tab_out[...] = table[:, :16]
     wo_out[...] = ro_ref[...]
-    wu_out[...] = ru_ref[...]
-    wd_out[...] = rd_ref[...]
+    for half, (ru_ref, rd_ref) in enumerate(((ru0_ref, rd0_ref), (ru1_ref, rd1_ref))):
+        wu_out[:, half * ru_ref.shape[1]:(half + 1) * ru_ref.shape[1]] = ru_ref[...]
+        wd_out[half * rd_ref.shape[0]:(half + 1) * rd_ref.shape[0], :] = rd_ref[...]
     for pair in range(4):
         for part in range(3):
             wq_out[:, (part * 4 + pair) * 128:(part * 4 + pair + 1) * 128] = pieces[pair][:, part * 128:(part + 1) * 128]
-    lane = lax.broadcasted_iota(jnp.int32, (16, 128), 1)
-    row = lax.broadcasted_iota(jnp.int32, (16, 128), 0)
-    own = lane == row + 16 * lax.rem(lax.axis_index("dp"), 8)
     square = lax.broadcasted_iota(jnp.int32, (16, 16), 0) == lax.broadcasted_iota(jnp.int32, (16, 16), 1)
-    gains = gains_ref[...].astype(F32)
-    for k, (w, grad, out) in enumerate(((wq_ref, wq_out, g1_out), (wu_ref, wu_out, g2_out))):
-        gain = jnp.sum(jnp.where(own, gains[k:k + 1, :], 0.0), axis=1, keepdims=True)
+    for first, w, grad, out in ((first_ref, wq_ref, wq_out, g1_out), (second_ref, wu_ref, wu_out, g2_out)):
+        gain = first[...].reshape(1, 16).astype(F32)
         dots = jnp.sum(w[...].astype(F32) * grad[...], axis=1, keepdims=True)
-        out[...] = jnp.sum(jnp.where(square, dots / gain, 0.0), axis=0, keepdims=True)
-
-
-def finish(tab, results, gains, wq, wu):
-    ro, ru, rd = results[:3]
+        out[...] = jnp.sum(jnp.where(square, dots, 0.0), axis=0, keepdims=True) / gain
+
+
+def finish(tab, results, first, second, wq, wu):
     out_shape = [
-        jax.ShapeDtypeStruct((8, 16), F32), jax.ShapeDtypeStruct(wq.shape, F32), jax.ShapeDtypeStruct(ro.shape, F32),
-        jax.ShapeDtypeStruct(ru.shape, F32), jax.ShapeDtypeStruct(rd.shape, F32), jax.ShapeDtypeStruct((1, 16), F32),
+        jax.ShapeDtypeStruct((8, 16), F32), jax.ShapeDtypeStruct(wq.shape, F32), jax.ShapeDtypeStruct((wu.shape[0], wq.shape[1] // 3), F32),
+        jax.ShapeDtypeStruct(wu.shape, F32), jax.ShapeDtypeStruct((2 * results[1].shape[0], wq.shape[1] // 3), F32), jax.ShapeDtypeStruct((1, 16), F32),
         jax.ShapeDtypeStruct((1, 16), F32),
     ]
-    return pl.pallas_call(finish_kernel, out_shape=out_shape, compiler_params=cp())(tab, *results, gains, wq, wu)
+    return pl.pallas_call(finish_kernel, out_shape=out_shape, compiler_params=cp())(tab, *results, first, second, wq, wu)
 
 
 def on_device(devices, inputs, valid_len, norm_first, w_qkv, w_out, relative_bucket_table, norm_second, w_up, w_down, output_gradient):
@@ -797,12 +898,8 @@
     by_pair = lambda w: w.reshape(D, 3, HP, 128).transpose(2, 0, 1, 3).reshape(HP, D, 384)
     if fast:
         sizes = device_grid(devices)
-        mine = jnp.arange(128) // 16 == lax.rem(lax.axis_index("dp"), 8)
-        place = lambda g: jnp.where(mine, jnp.tile(g, 8), jnp.zeros((), BF))
-        row = jnp.arange(16)[:, None]
-        gains = jnp.where(row == 0, place(norm_first), jnp.where(row == 1, place(norm_second), jnp.zeros((), BF)))
-        mixed, qa, qkv, n1, g1, g2, wq, wo, wu, wd = first_half(
-            sizes, valid_len, table, x, S, [gains, w_qkv, w_out, w_up, w_down]
+        mixed, qa, qkv, nt, bias_t, g1, g2, wq, wo, wu, wd = first_half(
+            sizes, valid_len, table, x, S, [norm_first, norm_second, w_qkv, w_out, w_up, w_down]
         )
         wq, wo, wu, wd = wq.reshape(HP, D, 384), wo.reshape(D, D), wu.reshape(D, FFW), wd.reshape(FFW, D)
     else:
@@ -812,14 +909,14 @@
         ]
         g1, g2 = g1.reshape(1, D).astype(F32), g2.reshape(1, D).astype(F32)
         wq = by_pair(wq)
-        mixed, qa, qkv, n1 = first_half(None, valid_len, table, x, S, [g1, wq])
+        mixed, qa, qkv, nt, bias_t = first_half(None, valid_len, table, x, S, [g1, wq])
     out, ga, gm, gwo, gwu, gwd = ffn(x, mixed.reshape(R, D), og, g2, wo, wu, wd)
     got = last_half(
-        sizes, valid_len, table, qa, qkv, mixed, gm.reshape(S, L, D), n1, wq, g1, x, ga, [gwo, gwu, gwd]
+        sizes, valid_len, table, bias_t, qa, qkv, mixed, gm.reshape(S, L, D), nt, wq, g1, x, ga, [gwo, gwu, gwd]
     )
     gi, tab = got[:2]
     if fast:
-        rt, rq, ro, ru, rd, r1, r2 = finish(tab, got[2:], gains, w_qkv, w_up)
+        rt, rq, ro, ru, rd, r1, r2 = finish(tab, got[2:], norm_first, norm_second, w_qkv, w_up)
         r1, r2 = r1.reshape(-1), r2.reshape(-1)
     else:
         gwq = got[2].reshape(HP, D, 3, 128).transpose(1, 2, 0, 3).reshape(D, 3 * D)

time: 229 us -> 189 us (0.83)
  Pallas kernels: 223 us -> 185 us
    pallas_call x1, Pallas kernels: 92.1 us -> 66.6 us  [last_half(): pl.pallas_call(functools.partial(last_kernel, sizes, plan), grid=(steps +...]
    pallas_call x1, Pallas kernels: 81.2 us -> 68.8 us  [first_half(): pl.pallas_call(functools.partial(first_kernel, sizes), grid=(HP, S), in_s...]
where the time goes in v3:
time: 189 us
  Pallas kernels  185 us (98%)
  local copies, waits for them, and re-layouts  3.04 us (2%)
    pallas_call x1, Pallas kernels, first_half(): pl.pallas_call(functools.partial(first_kernel, sizes), grid=(HP, S), in_s...  68.8 us
    pallas_call x1, Pallas kernels, last_half(): pl.pallas_call(functools.partial(last_kernel, sizes, plan), grid=(steps +...  66.6 us
    pallas_call x1, Pallas kernels, ffn(): pl.pallas_call(ffn_kernel, grid=(R // B,), in_specs=[row, row, row, full(...  47.6 us

profile of v3, /device:TPU:0, one launch (start us, length us, event | category | flops | bytes accessed | tf_op | source)
XLA Modules:
  0.0 188.5 jit_solution(7911086379785449140)
XLA Ops:
  0.6 68.8 %shard_map.169 = (bf16[2,1024,512]{2,1,0:T(8,128)(2,1)}, bf16[2,4,2,1024,128]{4,3,2,1,0:T(8,128)(2,1)}, bf16[4,2,1024,384]{3,2,1,0:T(8,128)(2,1)}, bf16[512,2048...) custom-call(s32[2]{0:T(128)} %refs_0_.3, ...), custom_call_target="tpu_custom_call" | custom-call | tf_op jit(solution)/shard_map/pallas_call | solution.py:594
  69.4 47.6 %shard_map.170 = (bf16[2048,512]{1,0:T(8,128)(2,1)}, f32[2048,512]{1,0:T(8,128)}, bf16[2048,512]{1,0:T(8,128)(2,1)}, bf16[512,512]{1,0:T(8,128)(2,1)}, bf16[512,...) custom-call(bf16[2048,512]{1,0:T(8,128)(2,1)} %bitcast.17, bf16[2048,512]{1,0:T(8,128)(2,1)} %bitcast.19, ...), custom_call_target="tpu_custom_call" | custom-call | tf_op jit(solution)/shard_map/pallas_call | solution.py:324
  117.0 66.6 %shard_map.171 = (bf16[2048,512]{1,0:T(8,128)(2,1)}, f32[32,128]{1,0:T(8,128)}, f32[16,1024]{1,0:T(8,128)}, f32[32,512]{1,0:T(8,128)}, f32[16,512]{1,0:T(8,128)}...) custom-call(s32[2]{0:T(128)} %refs_0_.3, ...), custom_call_target="tpu_custom_call" | custom-call | tf_op jit(solution)/shard_map/pallas_call | solution.py:851
  183.6 1.9 shard_map.172
  185.5 3.0 %copy.20 = bf16[2,1024,512]{2,1,0:T(8,128)(2,1)} copy(bf16[2,1024,512]{2,1,0:T(8,128)(2,1)} %bitcast.24) | data formatting | bytes 4194304

commit v4 on v3

--- a/solution.py
+++ b/solution.py
@@ -283,57 +283,102 @@
     gv=r*(e-jnp.mean(e,axis=1,keepdims=True)-xhat*jnp.mean(e*xhat,axis=1,keepdims=True))
     return (gv,)
 
-def ffn_kernel(x_ref,m_ref,og_ref,g_ref,wo_ref,wu_ref,wd_ref,out_ref,ga_ref,gm_ref,gwo_ref,gwu_ref,gwd_ref,ao,au,ad):
-    i=pl.program_id(0)
-    m=m_ref[...]; og=og_ref[...]
-    after=x_ref[...].astype(F32)+dot_nn(m,wo_ref[...])
-    xhat,r=ln_parts(after)
-    gain=g_ref[...].astype(F32)
-    n=(xhat*gain).astype(BF)
-    pre=dot_nn(n,wu_ref[...])
-    dh=dot_nt(og,wd_ref[...])
-    c=0.7978845608028654
-    sq=pre*pre
-    t=jnp.tanh(pre*(c+c*0.044715*sq))
-    half=0.5*(1.0+t)
-    hid=(pre*half).astype(BF)
-    dg=half+(0.5*pre)*(1.0-t*t)*(c+3*c*0.044715*sq)
-    gp=(dh*dg).astype(BF)
-    out_ref[...]=(after+dot_nn(hid,wd_ref[...])).astype(BF)
-    pd=dot_tn(hid,og); pu=dot_tn(n,gp)
-    dn=dot_nt(gp,wu_ref[...])
-    (gv,)=ln_back(dn,gain,xhat,r)
-    ga=og.astype(F32)+gv
-    ga_ref[...]=ga
-    gb=ga.astype(BF)
-    po=dot_tn(m,gb)
-    gm_ref[...]=dot_nt(gb,wo_ref[...]).astype(BF)
-    @pl.when(i==0)
+def ffn_kernel(x_ref, m_ref, og_ref, g_ref, wo_ref, wu_ref, wd_ref, out_ref, ga_ref, gm_ref, gwo_ref, gwu_ref, gwd_ref,
+               hid_s, gp_s, gb_s, nt_s, ogt_s, mt_s):
+    i = pl.program_id(0)
+    B = x_ref.shape[0]
+    R = hid_s.shape[0]
+    blocks = R // B
+    C = hid_s.shape[1] // FFN_PARTS
+
+    @pl.when(i < blocks)
     def _():
-        ad[...]=pd; au[...]=pu; ao[...]=po
-    @pl.when(i>0)
+        at = pl.ds(pl.multiple_of(i * B, B), B)
+        m = m_ref[...]
+        og = og_ref[...]
+        after = x_ref[...].astype(F32) + dot_nn(m, wo_ref[...])
+        xhat, r = ln_parts(after)
+        gain = g_ref[...]
+        n = (xhat * gain).astype(BF)
+        c = 0.7978845608028654
+        for j in range(FFN_PARTS):
+            cols = slice(j * C, (j + 1) * C)
+            pre = dot_nn(n, wu_ref[:, cols])
+            dh = dot_nt(og, wd_ref[cols, :])
+            a = c + (c * 0.044715) * (pre * pre)
+            half = 0.5 + 0.5 * jnp.tanh(pre * a)
+            h = pre * half
+            gp_s[at, cols] = (dh * (half + (h - h * half) * (6.0 * a - 4.0 * c))).astype(BF)
+            hid_s[at, cols] = h.astype(BF)
+        out_ref[...] = (after + dot_nn(hid_s[at, :], wd_ref[...])).astype(BF)
+        dn = dot_nt(gp_s[at, :], wu_ref[...])
+        (gv,) = ln_back(dn, gain, xhat, r)
+        ga = og.astype(F32) + gv
+        ga_ref[...] = ga
+        gb = ga.astype(BF)
+        gb_s[at, :] = gb
+        gm_ref[...] = dot_nt(gb, wo_ref[...]).astype(BF)
+        nt_s[:, at] = n.T
+        ogt_s[:, at] = og.T
+        mt_s[:, at] = m.T
+
+    @pl.when(i >= blocks)
     def _():
-        ad[...]+=pd; au[...]+=pu; ao[...]+=po
-    @pl.when(i==pl.num_programs(0)-1)
-    def _():
-        gwo_ref[...]=ao[...].astype(BF); gwu_ref[...]=au[...].astype(BF); gwd_ref[...]=ad[...].astype(BF)
-def ffn(x,m,og,gain,wo,wu,wd,B=512):
-    R,D=x.shape; FF=wu.shape[1]
-    row=pl.BlockSpec((B,D),lambda i:(i,0))
-    full=lambda a,b:pl.BlockSpec((a,b),lambda i:(0,0))
-    return pl.pallas_call(ffn_kernel,grid=(R//B,),
-      in_specs=[row,row,row,full(1,D),full(D,D),full(D,FF),full(FF,D)],
-      out_specs=[row,row,row,full(D,D),full(D,FF),full(FF,D)],
-      out_shape=[jax.ShapeDtypeStruct((R,D),BF),jax.ShapeDtypeStruct((R,D),F32),jax.ShapeDtypeStruct((R,D),BF),
-        jax.ShapeDtypeStruct((D,D),BF),jax.ShapeDtypeStruct((D,FF),BF),jax.ShapeDtypeStruct((FF,D),BF)],
-      scratch_shapes=[pltpu.VMEM((D,D),F32),pltpu.VMEM((D,FF),F32),pltpu.VMEM((FF,D),F32)],
-      compiler_params=cp())(x,m,og,gain,wo,wu,wd)
+        j = i - blocks
+        cols = pl.ds(pl.multiple_of(j * C, C), C)
+        gwd_ref[...] = dot_nn(ogt_s[...], hid_s[:, cols]).astype(BF).T
+        gwu_ref[...] = dot_nn(nt_s[...], gp_s[:, cols]).astype(BF)
+        share = mt_s.shape[0] // FFN_PARTS
+        gwo_ref[...] = dot_nn(mt_s[pl.ds(pl.multiple_of(j * share, share), share), :], gb_s[...]).astype(BF)
+
+
+FFN_PARTS = 4
+
+
+def ffn(x, m, og, gain, wo, wu, wd, B=512):
+    R, D = x.shape
+    FF = wu.shape[1]
+    n = R // B
+    C = FF // FFN_PARTS
+    row = pl.BlockSpec((B, D), lambda i: (jnp.minimum(i, n - 1), 0))
+    late = lambda i: jnp.maximum(i - n, 0)
+    return pl.pallas_call(
+        ffn_kernel,
+        grid=(n + FFN_PARTS,),
+        in_specs=[row, row, row, whole_block((1, D)), whole_block((D, D)), whole_block((D, FF)), whole_block((FF, D))],
+        out_specs=[
+            row, row, row,
+            pl.BlockSpec((D // FFN_PARTS, D), lambda i: (late(i), 0)),
+            pl.BlockSpec((D, C), lambda i: (0, late(i))),
+            pl.BlockSpec((C, D), lambda i: (late(i), 0)),
+        ],
+        out_shape=[
+            jax.ShapeDtypeStruct((R, D), BF), jax.ShapeDtypeStruct((R, D), F32), jax.ShapeDtypeStruct((R, D), BF),
+            jax.ShapeDtypeStruct((D, D), BF), jax.ShapeDtypeStruct((D, FF), BF), jax.ShapeDtypeStruct((FF, D), BF),
+        ],
+        scratch_shapes=[
+            pltpu.VMEM((R, FF), BF), pltpu.VMEM((R, FF), BF), pltpu.VMEM((R, D), BF), pltpu.VMEM((D, R), BF),
+            pltpu.VMEM((D, R), BF), pltpu.VMEM((D, R), BF),
+        ],
+        compiler_params=cp(),
+    )(x, m, og, gain, wo, wu, wd)
 
 
 SPREAD = ((0, 1, 2), (3,))
-ZXY, YZX, XZY, XYZ = (((a,), (b,), (c,), (3,)) for a, b, c in ((0, 2, 1), (1, 0, 2), (2, 0, 1), (2, 1, 0)))
+ZYX, ZXY, YZX, XZY, XYZ, YXZ = (
+    ((a,), (b,), (c,), (3,)) for a, b, c in ((0, 1, 2), (0, 2, 1), (1, 0, 2), (2, 0, 1), (2, 1, 0), (1, 2, 0))
+)
 GATHER_ORDERS = {
-    "q0": SPREAD, "gains": SPREAD, "q2": XZY, "q1": ZXY, "down1": XZY, "q3": ZXY, "down0": ZXY, "up0": YZX, "out": XYZ, "up1": YZX,
+    "q0": SPREAD,
+    "gains": SPREAD,
+    "q3": ZYX,
+    "q1": XZY,
+    "out": ZYX,
+    "down0": XYZ,
+    "up1": ZXY,
+    "q2": ZXY,
+    "up0": ZYX,
+    "down1": ZXY,
 }
 
 
@@ -350,10 +395,17 @@
 
 GATHER_SCHEDULE = timetable(
     {
-        "q2": (-1, 0, 2, 4, 5), "q1": (0, 2, 3, 3, 3), "down1": (-1, 0, 3, 6, 8), "q3": (0, 3, 4, 6, 7),
-        "down0": (0, 3, 5, 7, 8), "up0": (-1, 0, 4, 7, 8), "out": (-1, 0, 2, 7, 9), "up1": (-1, 0, 6, 8, 9),
+        "q3": (0, 2, 6, 8, 10),
+        "q1": (-1, 0, 3, 7, 7),
+        "out": (1, 5, 8, 14, 17),
+        "down0": (-1, 0, 2, 20, 23),
+        "up1": (1, 7, 11, 18, 20),
+        "q2": (0, 4, 7, 10, 13),
+        "up0": (1, 8, 13, 20, 25),
+        "down1": (1, 11, 15, 22, 25),
     }
 )
+LAST_TICK = 25
 
 
 def own_lanes():
@@ -409,6 +461,11 @@
         }
         out_copy = lambda pair: pltpu.make_async_copy(wq.at[pair], wq_out.at[pair], out_sem.at[pair])
 
+    def gather_tick(place):
+        if remote:
+            now = {t // 3: GATHER_SCHEDULE[t + 1] for t in range(place, LAST_TICK - 1, 3) if t + 1 in GATHER_SCHEDULE}
+            run_schedule(step, now, parts)
+
     @pl.when(step == 0)
     def _():
         if remote:
@@ -479,8 +536,7 @@
         if remote:
             parts["q0"].finish(1)
 
-    if remote:
-        run_schedule(step + 1, {tick: GATHER_SCHEDULE[tick] for tick in GATHER_SCHEDULE if 0 < tick < 9}, parts)
+    gather_tick(0)
 
     @pl.when(s == 0)
     def _():
@@ -492,19 +548,19 @@
                 row = seq * L + half * B
                 qkv_ref[0, seq, half * B:(half + 1) * B, :] = dot_nn(n_s[row:row + B, :], weights).astype(BF)
 
-    attend(vl_ref[s], qkv_ref.at[0, s], mixed_ref.at[0], qa_ref.at[0, 0], bias, table_ref, hp)
+    attend(vl_ref[s], qkv_ref.at[0, s], mixed_ref.at[0], qa_ref.at[0, 0], bias, table_ref, hp, gather_tick)
 
     @pl.when(step == pairs * S - 1)
     def _():
         for copy in keep:
             copy.wait()
         if remote:
-            run_actions(GATHER_SCHEDULE[9], parts)
+            run_actions(GATHER_SCHEDULE.get(LAST_TICK, []), parts)
             for pair in range(4):
                 out_copy(pair).wait()
 
 
-def attend(valid, qkv_ref, mixed_ref, qa_ref, bias, table_ref, hp):
+def attend(valid, qkv_ref, mixed_ref, qa_ref, bias, table_ref, hp, between):
     L = qkv_ref.shape[0]
     nb = L // T
     key = lax.broadcasted_iota(jnp.int32, (L, 1), 0)
@@ -514,6 +570,8 @@
     v = qkv_ref[:, 256:384]
     rows = [table_row(table_ref, 2 * hp + h) for h in range(2)]
     for qb in range(nb):
+        if qb >= nb - 2:
+            between(qb - nb + 3)
         kk = (qb + 1) * T
         qt = qkv_ref[qb * T:(qb + 1) * T, 0:128] * jnp.asarray(0.125, BF)
         outs = []

time: 189 us -> 181 us (0.958)
  Pallas kernels: 185 us -> 176 us
    pallas_call x1, Pallas kernels: 47.6 us -> 42.3 us  [ffn(): pl.pallas_call(ffn_kernel, grid=(n + FFN_PARTS,), in_specs=[row, row, row...]
    pallas_call x1, Pallas kernels: 68.8 us -> 66.8 us  [first_half(): pl.pallas_call(functools.partial(first_kernel, sizes), grid=(HP, S), in_s...]
where the time goes in v4:
time: 181 us; the launch traced here: 180 us
  Pallas kernels  176 us (97%)
  local copies, waits for them, and re-layouts  3.04 us (2%)
    pallas_call x1, Pallas kernels, first_half(): pl.pallas_call(functools.partial(first_kernel, sizes), grid=(HP, S), in_s...  66.8 us
    pallas_call x1, Pallas kernels, last_half(): pl.pallas_call(functools.partial(last_kernel, sizes, plan), grid=(steps +...  65.2 us
    pallas_call x1, Pallas kernels, ffn(): pl.pallas_call(ffn_kernel, grid=(n + FFN_PARTS,), in_specs=[row, row, row...  42.3 us

profile of v4, /device:TPU:0, one launch (start us, length us, event | category | flops | bytes accessed | tf_op | source)
XLA Modules:
  0.0 179.9 jit_solution(11096615507050197029)
XLA Ops:
  0.6 66.8 %shard_map.169 = (bf16[2,1024,512]{2,1,0:T(8,128)(2,1)}, bf16[2,4,2,1024,128]{4,3,2,1,0:T(8,128)(2,1)}, bf16[4,2,1024,384]{3,2,1,0:T(8,128)(2,1)}, bf16[512,2048...) custom-call(s32[2]{0:T(128)} %refs_0_.3, ...), custom_call_target="tpu_custom_call" | custom-call | tf_op jit(solution)/shard_map/pallas_call | solution.py:652
  67.4 42.3 %shard_map.170 = (bf16[2048,512]{1,0:T(8,128)(2,1)}, f32[2048,512]{1,0:T(8,128)}, bf16[2048,512]{1,0:T(8,128)(2,1)}, bf16[512,512]{1,0:T(8,128)(2,1)}, bf16[512,...) custom-call(bf16[2048,512]{1,0:T(8,128)(2,1)} %bitcast.17, bf16[2048,512]{1,0:T(8,128)(2,1)} %bitcast.19, ...), custom_call_target="tpu_custom_call" | custom-call | tf_op jit(solution)/shard_map/pallas_call | solution.py:345
  109.8 65.2 %shard_map.171 = (bf16[2048,512]{1,0:T(8,128)(2,1)}, f32[32,128]{1,0:T(8,128)}, f32[16,1024]{1,0:T(8,128)}, f32[32,512]{1,0:T(8,128)}, f32[16,512]{1,0:T(8,128)}...) custom-call(s32[2]{0:T(128)} %refs_0_.3, ...), custom_call_target="tpu_custom_call" | custom-call | tf_op jit(solution)/shard_map/pallas_call | solution.py:909
  175.0 1.9 %shard_map.172 = (f32[8,16]{1,0:T(8,128)}, f32[16,1536]{1,0:T(8,128)}, f32[16,512]{1,0:T(8,128)}, f32[16,2048]{1,0:T(8,128)}, f32[64,512]{1,0:T(8,128)}, /*index=5*/f32[1,16]{1,0:T(1,128)}, f32[1,16]{1,0:T(1,128)}) custom-call(f32[32,128]{1,0:T(8,128)} %get-tuple-element.62.refs_0_, f32[16,1024]{1,0:T(8,128)} %get-tuple-element.63.refs_1_, ...), custom_call_target="tpu_custom_call" | custom-call | tf_op jit(solution)/shard_map/pallas_call | solution.py:944
  176.9 3.0 %copy.20 = bf16[2,1024,512]{2,1,0:T(8,128)(2,1)} copy(bf16[2,1024,512]{2,1,0:T(8,128)(2,1)} %bitcast.24) | data formatting | bytes 4194304

commit v5 on v4

--- a/solution.py
+++ b/solution.py
@@ -567,7 +567,7 @@
     mask = jnp.where(key < valid, 0.0, NEG)
     lane = lax.broadcasted_iota(jnp.int32, (T, 128), 1)
     ks = [halves(h, qkv_ref[:, 128:256], [1.0, 1.0, 1.0, mask], L) for h in range(2)]
-    v = qkv_ref[:, 256:384]
+    vs = [halves(h, qkv_ref[:, 256:384], [1.0], L) for h in range(2)]
     rows = [table_row(table_ref, 2 * hp + h) for h in range(2)]
     for qb in range(nb):
         if qb >= nb - 2:
@@ -593,8 +593,8 @@
             )
             mx = jnp.max(sc, axis=1, keepdims=True)
             p = jnp.exp(sc - mx)
-            l = jnp.sum(p, axis=1, keepdims=True)
-            o = dot_nn(p.astype(BF), v[:kk])
+            o = dot_nn(p.astype(BF), vs[h][:kk])
+            l = o[:, 64 - 64 * h:65 - 64 * h]
             outs.append(o * (1.0 / l))
             hi, mid, lo = split3(-(mx + jnp.log(l)))
             qa_ref[h, qb * T:(qb + 1) * T, :] = halves(h, qt, [hi, mid, lo, 1.0], T)
@@ -672,15 +672,20 @@
     remote = sizes is not None
     refs = list(refs)
     take = lambda count: [refs.pop(0) for _ in range(count)]
-    vl_ref, table_ref, bias, qa_ref, qkv_ref, o_ref, g_ref, nt_ref, w_ref, gain_ref, x_ref, ga_ref = take(12)
+    vl_ref, table_ref, bias, qa_ref, qkv_ref, o_ref, g_ref, nt_any, w_any, gain_ref, x_ref, ga_ref = take(12)
     if remote:
-        wo_terms, wu_terms, wd_terms = take(3)
+        terms_any = take(3)
     gi_ref, tab_ref = take(2)
     if remote:
         results = dict(zip(SCATTER_ORDERS, take(9)))
     else:
         (gw_ref,) = take(1)
-    gacc, far, dqt, grads = take(4)
+    gacc, far, dqt, grads, nt_ref, w_ref, load_sem = take(7)
+    loads = [(nt_any, nt_ref), (w_any, w_ref)]
+    if remote:
+        wo_terms, wu_terms, wd_terms = terms_vm = take(3)
+        loads += list(zip(terms_any, terms_vm))
+    loads = [pltpu.make_async_copy(a, b, load_sem.at[k]) for k, (a, b) in enumerate(loads)]
     t = pl.program_id(0)
     pairs = grads.shape[0]
     S = grads.shape[1] // qkv_ref.shape[2]
@@ -690,6 +695,17 @@
     L = qkv_ref.shape[2]
     R = S * L
     D = x_ref.shape[1]
+
+    @pl.when(t == 0)
+    def _():
+        for load in loads:
+            load.start()
+
+    @pl.when(t == 1)
+    def _():
+        for load in loads:
+            load.wait()
+
     if remote:
         wq_terms, tab_own, tab_all, local = take(4)
         terms = dict(out=wo_terms)
@@ -868,8 +884,8 @@
         pl.BlockSpec((1, 1, L, W), lambda t: (pair(t), seq(t), 0, 0)),
         pl.BlockSpec((1, L, 128), lambda t: (seq(t), 0, pair(t))),
         pl.BlockSpec((1, L, 128), lambda t: (seq(t), 0, pair(t))),
-        whole_block((D, R)),
-        whole_block((HP, D, W)),
+        pl.BlockSpec(memory_space=pl.ANY),
+        pl.BlockSpec(memory_space=pl.ANY),
         whole_block((1, D)),
         late,
         late,
@@ -878,7 +894,8 @@
     out_shape = [jax.ShapeDtypeStruct((R, D), BF), jax.ShapeDtypeStruct((8 * HP, 128), F32)]
     scratch = [
         pltpu.VMEM((2, len(VARIED), H, H), F32), pltpu.VMEM((2, 2, 8, H), F32), pltpu.VMEM((128, L), F32),
-        pltpu.VMEM((HP, R, W), BF),
+        pltpu.VMEM((HP, R, W), BF), pltpu.VMEM((D, R), BF), pltpu.VMEM((HP, D, W), BF),
+        pltpu.SemaphoreType.DMA((5 if remote else 2,)),
     ]
     args = [vl, table, bias_t.reshape(HP, 2, len(VARIED), H, H), qa, qkv, mixed, gm, nt, wq, gain, x, ga]
     plan = None
@@ -886,7 +903,8 @@
         count = int(np.prod(sizes))
         terms = [a.reshape(sizes + (a.shape[0] // count, a.shape[1])) for a in ffn_grads]
         args += terms
-        in_specs += [whole_block(a.shape) for a in terms]
+        in_specs += [pl.BlockSpec(memory_space=pl.ANY) for a in terms]
+        scratch += [pltpu.VMEM(a.shape, BF) for a in terms]
         (_, D_), (_, U_), (rows_, _) = [a.shape[4:] for a in terms]
         blocks = dict(out=(16, D_), up0=(16, U_ // 2), up1=(16, U_ // 2), down0=(rows_ // 2, D_), down1=(rows_ // 2, D_))
         for k in range(HP):

time: 181 us -> 179 us (0.989)
  Pallas kernels: 176 us -> 174 us
    pallas_call x1, Pallas kernels: 65.2 us -> 62.5 us  [last_half(): pl.pallas_call(functools.partial(last_kernel, sizes, plan), grid=(steps +...]
where the time goes in v5:
time: 179 us; the launch traced here: 178 us
  Pallas kernels  174 us (97%)
  local copies, waits for them, and re-layouts  3.04 us (2%)
    pallas_call x1, Pallas kernels, first_half(): pl.pallas_call(functools.partial(first_kernel, sizes), grid=(HP, S), in_s...  67.6 us
    pallas_call x1, Pallas kernels, last_half(): pl.pallas_call(functools.partial(last_kernel, sizes, plan), grid=(steps +...  62.5 us
    pallas_call x1, Pallas kernels, ffn(): pl.pallas_call(ffn_kernel, grid=(n + FFN_PARTS,), in_specs=[row, row, row...  42.3 us

profile of v5, /device:TPU:0, one launch (start us, length us, event | category | flops | bytes accessed | tf_op | source)
XLA Modules:
  0.0 177.9 jit_solution(16726130082443088362)
XLA Ops:
  0.6 67.6 %shard_map.169 = (bf16[2,1024,512]{2,1,0:T(8,128)(2,1)}, bf16[2,4,2,1024,128]{4,3,2,1,0:T(8,128)(2,1)}, bf16[4,2,1024,384]{3,2,1,0:T(8,128)(2,1)}, bf16[512,2048...) custom-call(s32[2]{0:T(128)} %refs_0_.3, ...), custom_call_target="tpu_custom_call" | custom-call | tf_op jit(solution)/shard_map/pallas_call | solution.py:652
  68.2 42.3 %shard_map.170 = (bf16[2048,512]{1,0:T(8,128)(2,1)}, f32[2048,512]{1,0:T(8,128)}, bf16[2048,512]{1,0:T(8,128)(2,1)}, bf16[512,512]{1,0:T(8,128)(2,1)}, bf16[512,...) custom-call(bf16[2048,512]{1,0:T(8,128)(2,1)} %bitcast.17, bf16[2048,512]{1,0:T(8,128)(2,1)} %bitcast.19, ...), custom_call_target="tpu_custom_call" | custom-call | tf_op jit(solution)/shard_map/pallas_call | solution.py:345
  110.6 62.5 %shard_map.171 = (bf16[2048,512]{1,0:T(8,128)(2,1)}, f32[32,128]{1,0:T(8,128)}, f32[16,1024]{1,0:T(8,128)}, f32[32,512]{1,0:T(8,128)}, f32[16,512]{1,0:T(8,128)}...) custom-call(s32[2]{0:T(128)} %refs_0_.3, ...), custom_call_target="tpu_custom_call" | custom-call | tf_op jit(solution)/shard_map/pallas_call | solution.py:927
  173.0 1.9 %shard_map.172 = (f32[8,16]{1,0:T(8,128)}, f32[16,1536]{1,0:T(8,128)}, f32[16,512]{1,0:T(8,128)}, f32[16,2048]{1,0:T(8,128)}, f32[64,512]{1,0:T(8,128)}, /*index=5*/f32[1,16]{1,0:T(1,128)}, f32[1,16]{1,0:T(1,128)}) custom-call(f32[32,128]{1,0:T(8,128)} %get-tuple-element.62.refs_0_, f32[16,1024]{1,0:T(8,128)} %get-tuple-element.63.refs_1_, ...), custom_call_target="tpu_custom_call" | custom-call | tf_op jit(solution)/shard_map/pallas_call | solution.py:962
  174.9 3.0 %copy.20 = bf16[2,1024,512]{2,1,0:T(8,128)(2,1)} copy(bf16[2,1024,512]{2,1,0:T(8,128)(2,1)} %bitcast.24) | data formatting | bytes 4194304

commit v6 on v5

--- a/solution.py
+++ b/solution.py
@@ -70,6 +70,31 @@
         self.own, self.whole = own, whole
         self.local_sem, self.send_sems, self.recv_sems = local_sem, send_sems, recv_sems
 
+    def joined(self, phase):
+        return len(self.order[phase]) == 1
+
+    def sem(self, phase, k):
+        counts = [1 if self.joined(p) else len(moves(self.sizes, self.order[p])) for p in range(phase)]
+        return self.first + sum(counts) + (0 if self.joined(phase) else k)
+
+    def settle(self, phase):
+        count = len(moves(self.sizes, self.order[phase]))
+        if not self.joined(phase) or count == 1:
+            for copy in self.copies(phase):
+                copy.wait()
+        else:
+            every = self.bulk(phase, count)
+            for sems in (self.send_sems, self.recv_sems):
+                pltpu.make_async_copy(every, every, sems.at[self.sem(phase, 0)]).wait()
+
+    def bulk(self, phase, count):
+        place = grid_position(self.sizes)
+        done = [a for group in self.order[:phase] for a in group]
+        (axis,) = self.order[phase]
+        return self.whole.at[
+            tuple(slice(0, count) if a == axis else slice(None) if a in done else place[a] for a in range(4))
+        ]
+
     def copies(self, phase):
         place = grid_position(self.sizes)
         done = [a for group in self.order[:phase] for a in group]
@@ -79,8 +104,8 @@
             pltpu.make_async_remote_copy(
                 src_ref=self.own if phase == 0 else part,
                 dst_ref=part,
-                send_sem=self.send_sems.at[self.first + sum(len(moves(self.sizes, g)) for g in self.order[:phase]) + k],
-                recv_sem=self.recv_sems.at[self.first + sum(len(moves(self.sizes, g)) for g in self.order[:phase]) + k],
+                send_sem=self.send_sems.at[self.sem(phase, k)],
+                recv_sem=self.recv_sems.at[self.sem(phase, k)],
                 device_id=(flat(moved(place, self.sizes, group, move), self.sizes),),
                 device_id_type=MESH,
             )
@@ -99,8 +124,7 @@
     def finish(self, phase):
         if phase == 0:
             self.local().wait()
-        for copy in self.copies(phase):
-            copy.wait()
+        self.settle(phase)
 
 
 class Scatter:
@@ -132,6 +156,26 @@
             return 0
         return flat([place[a] for a in group], [self.sizes[a] for a in group])
 
+    def joined(self, phase):
+        return True
+
+    def sem(self, phase, k):
+        counts = [1 if self.joined(p) else len(moves(self.sizes, self.order[p])) for p in range(phase)]
+        return self.first + sum(counts) + (0 if self.joined(phase) else k)
+
+    def settle(self, phase):
+        count = len(moves(self.sizes, self.order[phase]))
+        if not self.joined(phase) or count == 1:
+            for copy in self.copies(phase):
+                copy.wait()
+        else:
+            every = self.bulk(phase, count)
+            for sems in (self.send_sems, self.recv_sems):
+                pltpu.make_async_copy(every, every, sems.at[self.sem(phase, 0)]).wait()
+
+    def bulk(self, phase, count):
+        return self.landing[phase].at[slice(0, count)]
+
     def copies(self, phase):
         place = grid_position(self.sizes)
         group = self.order[phase]
@@ -143,8 +187,8 @@
                 pltpu.make_async_remote_copy(
                     src_ref=self.held[phase].at[part],
                     dst_ref=self.landing[phase].at[self.slot(phase, place)],
-                    send_sem=self.send_sems.at[self.first + sum(len(moves(self.sizes, g)) for g in self.order[:phase]) + k],
-                    recv_sem=self.recv_sems.at[self.first + sum(len(moves(self.sizes, g)) for g in self.order[:phase]) + k],
+                    send_sem=self.send_sems.at[self.sem(phase, k)],
+                    recv_sem=self.recv_sems.at[self.sem(phase, k)],
                     device_id=(flat(other, self.sizes),),
                     device_id_type=MESH,
                 )
@@ -156,8 +200,7 @@
             copy.start()
 
     def finish(self, phase):
-        for copy in self.copies(phase):
-            copy.wait()
+        self.settle(phase)
         place = grid_position(self.sizes)
         group = self.order[phase]
         held, landed = self.held[phase], self.landing[phase]
@@ -198,13 +241,16 @@
             lax.fori_loop(0, int(np.prod(lead)), body, 0)
 
 
-def firsts(sizes, orders):
-    counts = [sum(len(moves(sizes, group)) for group in order) for order in orders]
+def firsts(sizes, orders, joins_groups):
+    counts = [
+        sum(1 if joins_groups[k] or len(group) == 1 else len(moves(sizes, group)) for group in order)
+        for k, order in enumerate(orders)
+    ]
     return [sum(counts[:k]) for k in range(len(counts))], sum(counts)
 
 
-def semaphores(sizes, orders):
-    return [pltpu.SemaphoreType.DMA((firsts(sizes, orders)[1],))] * 2
+def semaphores(sizes, orders, joins_groups):
+    return [pltpu.SemaphoreType.DMA((firsts(sizes, orders, joins_groups)[1],))] * 2
 
 
 def run_actions(actions, parts):
@@ -454,7 +500,7 @@
             own["down%d" % half], whole["down%d" % half] = wd_own.at[rows], wd_ref.at[:, :, :, :, rows]
         for pair in range(4):
             own["q%d" % pair], whole["q%d" % pair] = q_own.at[pair], wq.at[pair]
-        place = firsts(sizes, GATHER_ORDERS.values())[0]
+        place = firsts(sizes, GATHER_ORDERS.values(), [False] * len(GATHER_ORDERS))[0]
         parts = {
             name: Gather(sizes, GATHER_ORDERS[name], own[name], whole[name], local.at[k], send, recv, place[k])
             for k, name in enumerate(names)
@@ -643,7 +689,7 @@
             pltpu.VMEM((16, 128), BF),
             pltpu.VMEM(sizes + (16, 128), BF),
             pltpu.SemaphoreType.DMA((len(GATHER_ORDERS),)),
-        ] + semaphores(sizes, GATHER_ORDERS.values()) + [pltpu.SemaphoreType.DMA((HP,))]
+        ] + semaphores(sizes, GATHER_ORDERS.values(), [False] * len(GATHER_ORDERS)) + [pltpu.SemaphoreType.DMA((HP,))]
         params = cp(collective_id=1, has_side_effects=True)
     else:
         gain, wq = weights
@@ -717,7 +763,7 @@
         for pair in range(4):
             terms["q%d" % pair] = wq_terms.at[pair]
         send, recv = refs[-2:]
-        place = firsts(sizes, [*SCATTER_ORDERS.values(), SPREAD])[0]
+        place = firsts(sizes, [*SCATTER_ORDERS.values(), SPREAD], [True] * len(SCATTER_ORDERS) + [False])[0]
         parts = {}
         for k, name in enumerate(SCATTER_ORDERS):
             sums, landing = plan[name]
@@ -918,7 +964,7 @@
         ]
         for name in SCATTER_ORDERS:
             scratch += [pltpu.VMEM(shape, BF) for shape in plan[name][0] + plan[name][1]]
-        scratch += semaphores(sizes, [*SCATTER_ORDERS.values(), SPREAD])
+        scratch += semaphores(sizes, [*SCATTER_ORDERS.values(), SPREAD], [True] * len(SCATTER_ORDERS) + [False])
         params = cp(collective_id=2, has_side_effects=True)
     else:
         out_specs += [whole_block((HP, D, W))]
@@ -935,8 +981,17 @@
     take = lambda count: [refs.pop(0) for _ in range(count)]
     tab_ref, ru0_ref, rd0_ref, ro_ref, ru1_ref, rd1_ref = take(6)
     pieces = take(4)
-    first_ref, second_ref, wq_ref, wu_ref = take(4)
-    tab_out, wq_out, wo_out, wu_out, wd_out, g1_out, g2_out = refs
+    first_ref, second_ref, wq_ref, wu_ref, gi_ref = take(5)
+    tab_out, wq_out, wo_out, wu_out, wd_out, g1_out, g2_out, gi_out, held, sems = refs
+    share = gi_ref.shape[0] // 4
+    places = [pl.ds(k * share, share) for k in range(4)]
+    moves_in = [pltpu.make_async_copy(gi_ref.at[at], held.at[at], sems.at[k]) for k, at in enumerate(places)]
+    moves_out = [pltpu.make_async_copy(held.at[at], gi_out.at[at], sems.at[4 + k]) for k, at in enumerate(places)]
+    for move in moves_in:
+        move.start()
+    for move_in, move_out in zip(moves_in, moves_out):
+        move_in.wait()
+        move_out.start()
     table = jnp.concatenate([tab_ref[8 * pair:8 * pair + 2, :] for pair in range(4)], axis=0)
     tab_out[...] = table[:, :16]
     wo_out[...] = ro_ref[...]
@@ -951,15 +1006,26 @@
         gain = first[...].reshape(1, 16).astype(F32)
         dots = jnp.sum(w[...].astype(F32) * grad[...], axis=1, keepdims=True)
         out[...] = jnp.sum(jnp.where(square, dots, 0.0), axis=0, keepdims=True) / gain
-
-
-def finish(tab, results, first, second, wq, wu):
+    for move in moves_out:
+        move.wait()
+
+
+def finish(tab, results, first, second, wq, wu, gi):
     out_shape = [
         jax.ShapeDtypeStruct((8, 16), F32), jax.ShapeDtypeStruct(wq.shape, F32), jax.ShapeDtypeStruct((wu.shape[0], wq.shape[1] // 3), F32),
         jax.ShapeDtypeStruct(wu.shape, F32), jax.ShapeDtypeStruct((2 * results[1].shape[0], wq.shape[1] // 3), F32), jax.ShapeDtypeStruct((1, 16), F32),
         jax.ShapeDtypeStruct((1, 16), F32),
     ]
-    return pl.pallas_call(finish_kernel, out_shape=out_shape, compiler_params=cp())(tab, *results, first, second, wq, wu)
+    args = [tab, *results, first, second, wq, wu, gi]
+    anyspace = pl.BlockSpec(memory_space=pl.ANY)
+    return pl.pallas_call(
+        finish_kernel,
+        in_specs=[whole_block(a.shape) for a in args[:-1]] + [anyspace],
+        out_specs=[whole_block(s.shape) for s in out_shape] + [anyspace],
+        out_shape=out_shape + [jax.ShapeDtypeStruct(gi.shape, gi.dtype)],
+        scratch_shapes=[pltpu.VMEM(gi.shape, gi.dtype), pltpu.SemaphoreType.DMA((8,))],
+        compiler_params=cp(),
+    )(*args)
 
 
 def on_device(devices, inputs, valid_len, norm_first, w_qkv, w_out, relative_bucket_table, norm_second, w_up, w_down, output_gradient):
@@ -992,7 +1058,7 @@
     )
     gi, tab = got[:2]
     if fast:
-        rt, rq, ro, ru, rd, r1, r2 = finish(tab, got[2:], norm_first, norm_second, w_qkv, w_up)
+        rt, rq, ro, ru, rd, r1, r2, gi = finish(tab, got[2:], norm_first, norm_second, w_qkv, w_up, gi)
         r1, r2 = r1.reshape(-1), r2.reshape(-1)
     else:
         gwq = got[2].reshape(HP, D, 3, 128).transpose(1, 2, 0, 3).reshape(D, 3 * D)

time: 179 us -> 177 us (0.989)
  local copies, waits for them, and re-layouts: 3.04 us -> 0 us
    unnamed x1 -> x0, local copies, waits for them, and re-layouts: 3.04 us -> none
    pallas_call x1, Pallas kernels: 1.87 us -> 4.29 us  [finish(): pl.pallas_call(finish_kernel, in_specs=[whole_block(a.shape) for a in arg...]
where the time goes in v6:
time: 177 us; the launch traced here: 176 us
  Pallas kernels  175 us (99%)
    pallas_call x1, Pallas kernels, first_half(): pl.pallas_call(functools.partial(first_kernel, sizes), grid=(HP, S), in_s...  67.2 us
    pallas_call x1, Pallas kernels, last_half(): pl.pallas_call(functools.partial(last_kernel, sizes, plan), grid=(steps +...  61.7 us
    pallas_call x1, Pallas kernels, ffn(): pl.pallas_call(ffn_kernel, grid=(n + FFN_PARTS,), in_specs=[row, row, row...  42.3 us
    pallas_call x1, Pallas kernels, finish(): pl.pallas_call(finish_kernel, in_specs=[whole_block(a.shape) for a in arg...  4.29 us

profile of v6, /device:TPU:0, one launch (start us, length us, event | category | flops | bytes accessed | tf_op | source)
XLA Modules:
  0.0 176.3 jit_solution(6205515481377473850)
XLA Ops:
  0.6 67.2 %shard_map.169 = (bf16[2,1024,512]{2,1,0:T(8,128)(2,1)}, bf16[2,4,2,1024,128]{4,3,2,1,0:T(8,128)(2,1)}, bf16[4,2,1024,384]{3,2,1,0:T(8,128)(2,1)}, bf16[512,2048...) custom-call(s32[2]{0:T(128)} %refs_0_.3, ...), custom_call_target="tpu_custom_call" | custom-call | tf_op jit(solution)/shard_map/pallas_call | solution.py:698
  67.8 42.3 %shard_map.170 = (bf16[2048,512]{1,0:T(8,128)(2,1)}, f32[2048,512]{1,0:T(8,128)}, bf16[2048,512]{1,0:T(8,128)(2,1)}, bf16[512,512]{1,0:T(8,128)(2,1)}, bf16[512,...) custom-call(bf16[2048,512]{1,0:T(8,128)(2,1)} %bitcast.17, bf16[2048,512]{1,0:T(8,128)(2,1)} %bitcast.19, ...), custom_call_target="tpu_custom_call" | custom-call | tf_op jit(solution)/shard_map/pallas_call | solution.py:391
  110.1 61.7 %shard_map.171 = (bf16[2048,512]{1,0:T(8,128)(2,1)}, f32[32,128]{1,0:T(8,128)}, f32[16,1024]{1,0:T(8,128)}, f32[32,512]{1,0:T(8,128)}, f32[16,512]{1,0:T(8,128)}...) custom-call(s32[2]{0:T(128)} %refs_0_.3, ...), custom_call_target="tpu_custom_call" | custom-call | tf_op jit(solution)/shard_map/pallas_call | solution.py:973
  171.8 4.3 %shard_map.172 = (f32[8,16]{1,0:T(8,128)}, f32[16,1536]{1,0:T(8,128)}, f32[16,512]{1,0:T(8,128)}, f32[16,2048]{1,0:T(8,128)}, f32[64,512]{1,0:T(8,128)}, /*index...) custom-call(f32[32,128]{1,0:T(8,128)} %get-tuple-element.62.refs_0_, f32[16,1024]{1,0:T(8,128)} %get-tuple-element.63.refs_1_, ...), custom_call_target="tpu_custom_call" | custom-call | tf_op jit(solution)/shard_map/pallas_call | solution.py:1021

commit v7 on v6

--- a/solution.py
+++ b/solution.py
@@ -539,8 +539,8 @@
         lax.fori_loop(0, R // B, norm, 0)
         if remote:
             await_greetings(sizes, SPREAD)
+            parts["gains"].start(0)
             parts["q0"].start(0)
-            parts["gains"].start(0)
             run_actions(GATHER_SCHEDULE[-1], parts)
 
         def turn(block, unused):
@@ -551,8 +551,8 @@
         lax.fori_loop(0, R // B, turn, 0)
         if remote:
             parts["gains"].finish(0)
+            parts["gains"].start(1)
             parts["q0"].finish(0)
-            parts["gains"].start(1)
             parts["q0"].start(1)
             run_actions(GATHER_SCHEDULE[0], parts)
             parts["gains"].finish(1)

time: 177 us -> 177 us (level)
  no operation moved by 1% of the time
where the time goes in v7:
time: 177 us; the launch traced here: 175 us
  Pallas kernels  174 us (98%)
    pallas_call x1, Pallas kernels, first_half(): pl.pallas_call(functools.partial(first_kernel, sizes), grid=(HP, S), in_s...  67.2 us
    pallas_call x1, Pallas kernels, last_half(): pl.pallas_call(functools.partial(last_kernel, sizes, plan), grid=(steps +...  60.1 us
    pallas_call x1, Pallas kernels, ffn(): pl.pallas_call(ffn_kernel, grid=(n + FFN_PARTS,), in_specs=[row, row, row...  42.3 us
    pallas_call x1, Pallas kernels, finish(): pl.pallas_call(finish_kernel, in_specs=[whole_block(a.shape) for a in arg...  4.29 us

profile of v7, /device:TPU:0, one launch (start us, length us, event | category | flops | bytes accessed | tf_op | source)
XLA Modules:
  0.0 174.8 jit_solution(16939414043928668825)
XLA Ops:
  0.6 67.2 %shard_map.169 = (bf16[2,1024,512]{2,1,0:T(8,128)(2,1)}, bf16[2,4,2,1024,128]{4,3,2,1,0:T(8,128)(2,1)}, bf16[4,2,1024,384]{3,2,1,0:T(8,128)(2,1)}, bf16[512,2048...) custom-call(s32[2]{0:T(128)} %refs_0_.3, ...), custom_call_target="tpu_custom_call" | custom-call | tf_op jit(solution)/shard_map/pallas_call | solution.py:698
  67.9 42.3 %shard_map.170 = (bf16[2048,512]{1,0:T(8,128)(2,1)}, f32[2048,512]{1,0:T(8,128)}, bf16[2048,512]{1,0:T(8,128)(2,1)}, bf16[512,512]{1,0:T(8,128)(2,1)}, bf16[512,...) custom-call(bf16[2048,512]{1,0:T(8,128)(2,1)} %bitcast.17, bf16[2048,512]{1,0:T(8,128)(2,1)} %bitcast.19, ...), custom_call_target="tpu_custom_call" | custom-call | tf_op jit(solution)/shard_map/pallas_call | solution.py:391
  110.2 60.1 %shard_map.171 = (bf16[2048,512]{1,0:T(8,128)(2,1)}, f32[32,128]{1,0:T(8,128)}, f32[16,1024]{1,0:T(8,128)}, f32[32,512]{1,0:T(8,128)}, f32[16,512]{1,0:T(8,128)}...) custom-call(s32[2]{0:T(128)} %refs_0_.3, ...), custom_call_target="tpu_custom_call" | custom-call | tf_op jit(solution)/shard_map/pallas_call | solution.py:973
  170.3 4.3 %shard_map.172 = (f32[8,16]{1,0:T(8,128)}, f32[16,1536]{1,0:T(8,128)}, f32[16,512]{1,0:T(8,128)}, f32[16,2048]{1,0:T(8,128)}, f32[64,512]{1,0:T(8,128)}, /*index...) custom-call(f32[32,128]{1,0:T(8,128)} %get-tuple-element.62.refs_0_, f32[16,1024]{1,0:T(8,128)} %get-tuple-element.63.refs_1_, ...), custom_call_target="tpu_custom_call" | custom-call | tf_op jit(solution)/shard_map/pallas_call | solution.py:1021
